TPU v7x, 32 devices: a whole 2x2x4 slice. The times are simulated.
32 devices in a mesh: blk: 4 (over y, x), exp: 8 (over z, core).
Axes of the slice: x: 2, y: 2, z: 4, core: 2. Of those that a mesh axis runs over, the one named last changes fastest.
Arguments:
- tokens: bfloat16 [16, 1024, 768], P('exp', 'blk'), may hold values from -6 to 6
- output_grad: bfloat16 [16, 1024, 768], P('exp', 'blk'), may hold values from -6 to 6
- expert_index: int32 [4, 16, 256, 1], P('blk', 'exp'), may hold values from 0 to 7; in each aligned block of 512 rows (0 to 511, 512 to 1023, ..., all dimensions but the last counted through in order) at most 80 rows name the same one
- query_weight: bfloat16 [768, 768], replicated, may hold values from -0.21875 to 0.21875
- key_weight: bfloat16 [768, 768], replicated, may hold values from -0.21875 to 0.21875
- value_weight: bfloat16 [768, 768], replicated, may hold values from -0.21875 to 0.21875
- output_weight: bfloat16 [768, 768], replicated, may hold values from -3.5 to 3.5
- router_weight: bfloat16 [768, 8], replicated, may hold values from -0.15625 to 0.15625
- expert_in: bfloat16 [8, 768, 3072], P('exp'), may hold values from -0.21875 to 0.21875
- expert_out: bfloat16 [8, 3072, 768], P('exp'), may hold values from -0.21875 to 0.21875
- norm1_gain: float32 [768], replicated, may hold values from 0.5 to 1.5
- norm1_bias: float32 [768], replicated, may hold values from -3 to 3
- norm2_gain: float32 [768], replicated, may hold values from 0.5 to 1.5
- norm2_bias: float32 [768], replicated, may hold values from -3 to 3
Outputs:
- output: bfloat16 [16, 1024, 768], P('exp', 'blk')
- balance_loss: float32 [], replicated
- grad_tokens: bfloat16 [16, 1024, 768], P('exp', 'blk')
- grad_query: float32 [768, 768], replicated
- grad_key: float32 [768, 768], replicated
- grad_value: float32 [768, 768], replicated
- grad_output: float32 [768, 768], replicated
- grad_router: float32 [768, 8], replicated
- grad_expert_in: float32 [8, 768, 3072], P('exp', None, 'blk')
- grad_expert_out: float32 [8, 3072, 768], P('exp', 'blk')
- grad_norm1_gain: float32 [768], replicated
- grad_norm1_bias: float32 [768], replicated
- grad_norm2_gain: float32 [768], replicated
- grad_norm2_bias: float32 [768], replicated
Inputs may be any that keep to these rules, and one draw needn't show every extreme that they name: `expert_index`: in each aligned block of 512 rows (the tokens of one device, in order of sequence, then position) no expert is named more than 80 times, a bound that some block reaches.
All inputs are finite; a program needn't handle non-finite values.
Results may differ from a plain program's by a relative error of at most 0.023.
Values may be sent and summed in bfloat16 or wider, within the bound.
A program may use at most 256 MiB of HBM per device.

v0:
```python
import jax
import jax.numpy as jnp
from jax import lax
from jax.sharding import PartitionSpec as P

HEADS = 12
HEAD_DIM = 64


EPSILON = 1e-05
FLOOR_SCORE = -1e30


def layer_norm(inputs, gain_row, bias_row):
    centered = inputs - jnp.mean(inputs, axis=-1, keepdims=True)
    variance = jnp.mean(centered * centered, axis=-1, keepdims=True)
    return centered * lax.rsqrt(variance + EPSILON) * gain_row + bias_row


def split_heads(matrix):
    return matrix.reshape(matrix.shape[0], matrix.shape[1], HEADS, HEAD_DIM)


def masked_scores(queries, key_rows, query_places, key_places, score_scale):
    raw_scores = (
        jnp.einsum("sqhd,skhd->shqk", queries, key_rows, preferred_element_type=jnp.float32)
        * score_scale
    )
    visible = key_places[None, :] <= query_places[:, None]
    return (jnp.where(visible, raw_scores, FLOOR_SCORE), visible)


def shards(
    tokens,
    output_grad,
    expert_index,
    query_weight,
    key_weight,
    value_weight,
    output_weight,
    router_weight,
    expert_in,
    expert_out,
    norm1_gain,
    norm1_bias,
    norm2_gain,
    norm2_bias,
):
    seq_count, block_len, model_width = tokens.shape
    row_count = seq_count * block_len
    blk_count = lax.axis_size("blk")
    exp_count = lax.axis_size("exp")
    full_len = block_len * blk_count
    expert_count = router_weight.shape[1]
    local_experts = expert_in.shape[0]
    capacity = max(2, row_count * 5 // (4 * expert_count))
    token_total = row_count * blk_count * exp_count
    score_scale = HEAD_DIM ** (-0.5)
    my_place = lax.axis_index("blk")
    query_places = my_place * block_len + jnp.arange(block_len, dtype=jnp.int32)
    all_places = jnp.arange(full_len, dtype=jnp.int32)
    flat_tokens = tokens.reshape(row_count, model_width).astype(jnp.float32)
    normed_low = layer_norm(flat_tokens, norm1_gain, norm1_bias).astype(jnp.bfloat16)

    def project(matrix):
        made = jnp.dot(normed_low, matrix, preferred_element_type=jnp.float32).astype(jnp.bfloat16)
        return made.reshape(seq_count, block_len, model_width)

    queries = project(query_weight)
    key_rows = project(key_weight)
    value_rows = project(value_weight)
    query_heads = split_heads(queries)
    start_state = (
        jnp.full((seq_count, HEADS, block_len), FLOOR_SCORE, jnp.float32),
        jnp.zeros((seq_count, HEADS, block_len), jnp.float32),
        jnp.zeros((seq_count, HEADS, block_len, HEAD_DIM), jnp.float32),
    )
    piece_keys = lax.all_gather(key_rows, "blk", axis=1, tiled=True)
    piece_values = lax.all_gather(value_rows, "blk", axis=1, tiled=True)
    piece_places = jnp.arange(piece_keys.shape[1], dtype=jnp.int32)

    def update(held):
        old_peak, old_total, old_acc = held
        scores, visible = masked_scores(
            query_heads, split_heads(piece_keys), query_places, piece_places, score_scale
        )
        new_peak = jnp.maximum(old_peak, jnp.max(scores, axis=-1))
        powers = jnp.where(visible, jnp.exp(scores - new_peak[..., None]), 0.0)
        new_total = jnp.sum(powers, axis=-1)
        new_acc = jnp.einsum(
            "shqk,skhd->shqd",
            powers.astype(jnp.bfloat16),
            split_heads(piece_values),
            preferred_element_type=jnp.float32,
        )
        return (new_peak, new_total, new_acc)

    run_peak, run_total, run_acc = lax.cond(
        jnp.int32(0) > query_places[-1], lambda held: held, update, start_state
    )
    log_sums = run_peak + jnp.log(run_total)
    attended = jnp.transpose(run_acc / run_total[..., None], (0, 2, 1, 3))
    mixed_low = attended.reshape(row_count, model_width).astype(jnp.bfloat16)
    hidden_one = flat_tokens + jnp.dot(mixed_low, output_weight, preferred_element_type=jnp.float32)
    normed_two = layer_norm(hidden_one, norm2_gain, norm2_bias).astype(jnp.bfloat16)
    logits = jnp.dot(normed_two, router_weight, preferred_element_type=jnp.float32)
    routing = expert_index.reshape(row_count)
    hot_int = (routing[:, None] == jnp.arange(expert_count, dtype=jnp.int32)[None, :]).astype(
        jnp.int32
    )
    onehot = hot_int.astype(jnp.float32)
    slot_index = jnp.sum((jnp.cumsum(hot_int, axis=0) - hot_int) * hot_int, axis=1)
    counts = lax.psum(jnp.sum(hot_int, axis=0), ("blk", "exp"))
    gate_value = jax.nn.sigmoid(jnp.sum(logits * onehot, axis=1))

    def fill_slots(row_data):
        filled = (
            jnp.zeros((expert_count, capacity, model_width), jnp.bfloat16)
            .at[routing, slot_index]
            .set(row_data)
        )
        return filled.reshape(exp_count, local_experts, capacity, model_width)

    def read_slots(buffer):
        return buffer.reshape(expert_count, capacity, model_width)[routing, slot_index]

    received = lax.all_to_all(
        fill_slots(normed_two), "exp", split_axis=0, concat_axis=0, tiled=True
    )
    before = jnp.einsum("secd,edf->secf", received, expert_in, preferred_element_type=jnp.float32)
    activated = jax.nn.gelu(before).astype(jnp.bfloat16)
    produced = jnp.einsum(
        "secf,efd->secd", activated, expert_out, preferred_element_type=jnp.float32
    ).astype(jnp.bfloat16)
    returned = read_slots(
        lax.all_to_all(produced, "exp", split_axis=0, concat_axis=0, tiled=True)
    ).astype(jnp.float32)
    hidden_two = hidden_one + gate_value[:, None] * returned
    output = hidden_two.astype(jnp.bfloat16).reshape(seq_count, block_len, model_width)
    grad_two = output_grad.reshape(row_count, model_width).astype(jnp.float32)
    mean_load = token_total / expert_count
    load_weight = (counts.astype(jnp.float32) - mean_load) / mean_load
    grad_made = (gate_value[:, None] * grad_two).astype(jnp.bfloat16)
    grad_gate = (
        jnp.sum(grad_two * returned, axis=1)
        + jnp.sum(onehot * load_weight[None, :], axis=1) / token_total
    )
    grad_logits = (onehot * (grad_gate * gate_value * (1.0 - gate_value))[:, None]).astype(
        jnp.bfloat16
    )
    arrived = lax.all_to_all(fill_slots(grad_made), "exp", split_axis=0, concat_axis=0, tiled=True)
    grad_expert_out = jnp.einsum(
        "secf,secd->efd", activated, arrived, preferred_element_type=jnp.float32
    )
    grad_activated = jnp.einsum(
        "secd,efd->secf", arrived, expert_out, preferred_element_type=jnp.float32
    )
    grad_before = jax.vjp(jax.nn.gelu, before)[1](grad_activated)[0].astype(jnp.bfloat16)
    grad_expert_in = jnp.einsum(
        "secd,secf->edf", received, grad_before, preferred_element_type=jnp.float32
    )
    grad_received = jnp.einsum(
        "secf,edf->secd", grad_before, expert_in, preferred_element_type=jnp.float32
    ).astype(jnp.bfloat16)
    grad_normed = read_slots(
        lax.all_to_all(grad_received, "exp", split_axis=0, concat_axis=0, tiled=True)
    ).astype(jnp.float32)
    grad_normed = grad_normed + jnp.dot(
        grad_logits, router_weight.T, preferred_element_type=jnp.float32
    )
    grad_router = jnp.einsum(
        "td,te->de", normed_two, grad_logits, preferred_element_type=jnp.float32
    )
    grad_hidden_part, grad_gain_two, grad_bias_two = jax.vjp(
        layer_norm, hidden_one, norm2_gain, norm2_bias
    )[1](grad_normed)
    grad_one = grad_two + grad_hidden_part
    grad_attn_low = grad_one.astype(jnp.bfloat16)
    grad_output_weight = jnp.einsum(
        "td,te->de", mixed_low, grad_attn_low, preferred_element_type=jnp.float32
    )
    grad_mixed = (
        jnp.dot(grad_attn_low, output_weight.T, preferred_element_type=jnp.float32)
        .astype(jnp.bfloat16)
        .reshape(seq_count, block_len, model_width)
    )
    grad_mixed_heads = split_heads(grad_mixed)
    key_back, value_back = (
        lax.all_gather(key_rows, "blk", axis=1, tiled=True),
        lax.all_gather(value_rows, "blk", axis=1, tiled=True),
    )
    scores, visible = masked_scores(
        query_heads, split_heads(key_back), query_places, all_places, score_scale
    )
    chances = jnp.where(visible, jnp.exp(scores - log_sums[..., None]), 0.0)
    chances_low = chances.astype(jnp.bfloat16)
    grad_chances = jnp.einsum(
        "sqhd,skhd->shqk",
        grad_mixed_heads,
        split_heads(value_back),
        preferred_element_type=jnp.float32,
    )
    row_delta = jnp.sum(chances * grad_chances, axis=-1)
    grad_scores = (chances * (grad_chances - row_delta[..., None])).astype(jnp.bfloat16)
    grad_queries = (
        jnp.einsum(
            "shqk,skhd->sqhd",
            grad_scores,
            split_heads(key_back),
            preferred_element_type=jnp.float32,
        )
        * score_scale
    ).astype(jnp.bfloat16)
    row_total = block_len * lax.axis_size("blk")
    key_term = (
        jnp.einsum("shqk,sqhd->kshd", grad_scores, query_heads, preferred_element_type=jnp.float32)
        * score_scale
    )
    value_term = jnp.einsum(
        "shqk,sqhd->kshd", chances_low, grad_mixed_heads, preferred_element_type=jnp.float32
    )
    summed = lax.psum_scatter(
        jnp.concatenate(
            [
                key_term.reshape(row_total, seq_count, model_width),
                value_term.reshape(row_total, seq_count, model_width),
            ],
            axis=2,
        ).astype(jnp.bfloat16),
        "blk",
        scatter_dimension=0,
        tiled=True,
    ).astype(jnp.float32)
    grad_keys = jnp.transpose(summed[:, :, :model_width], (1, 0, 2)).astype(jnp.bfloat16)
    grad_values = jnp.transpose(summed[:, :, model_width:], (1, 0, 2)).astype(jnp.bfloat16)
    query_flat = grad_queries.reshape(row_count, model_width)
    key_flat = grad_keys.reshape(row_count, model_width)
    value_flat = grad_values.reshape(row_count, model_width)
    grad_query_weight = jnp.einsum(
        "td,te->de", normed_low, query_flat, preferred_element_type=jnp.float32
    )
    grad_key_weight = jnp.einsum(
        "td,te->de", normed_low, key_flat, preferred_element_type=jnp.float32
    )
    grad_value_weight = jnp.einsum(
        "td,te->de", normed_low, value_flat, preferred_element_type=jnp.float32
    )
    grad_normed_one = (
        jnp.dot(query_flat, query_weight.T, preferred_element_type=jnp.float32)
        + jnp.dot(key_flat, key_weight.T, preferred_element_type=jnp.float32)
        + jnp.dot(value_flat, value_weight.T, preferred_element_type=jnp.float32)
    )
    grad_inputs_part, grad_gain_one, grad_bias_one = jax.vjp(
        layer_norm, flat_tokens, norm1_gain, norm1_bias
    )[1](grad_normed_one)
    grad_tokens = (
        (grad_one + grad_inputs_part)
        .astype(jnp.bfloat16)
        .reshape(seq_count, block_len, model_width)
    )
    gate_mass = jnp.sum(onehot * gate_value[:, None], axis=0)
    summed_grads = lax.psum(
        (
            grad_query_weight,
            grad_key_weight,
            grad_value_weight,
            grad_output_weight,
            grad_router,
            grad_gain_one,
            grad_bias_one,
            grad_gain_two,
            grad_bias_two,
            gate_mass,
        ),
        ("blk", "exp"),
    )
    balance = jnp.sum(load_weight * summed_grads[9]) / token_total
    expert_in_grad, expert_out_grad = (
        lax.psum_scatter(
            grad_expert_in.astype(jnp.bfloat16), "blk", scatter_dimension=2, tiled=True
        ).astype(jnp.float32),
        lax.psum_scatter(
            grad_expert_out.astype(jnp.bfloat16), "blk", scatter_dimension=1, tiled=True
        ).astype(jnp.float32),
    )
    return (
        output,
        balance,
        grad_tokens,
        summed_grads[0],
        summed_grads[1],
        summed_grads[2],
        summed_grads[3],
        summed_grads[4],
        expert_in_grad,
        expert_out_grad,
        summed_grads[5],
        summed_grads[6],
        summed_grads[7],
        summed_grads[8],
    )


def solution(mesh):
    return jax.shard_map(
        shards,
        mesh=mesh,
        in_specs=(
            P("exp", "blk", None),
            P("exp", "blk", None),
            P("blk", "exp", None, None),
            P(),
            P(),
            P(),
            P(),
            P(),
            P("exp", None, None),
            P("exp", None, None),
            P(),
            P(),
            P(),
            P(),
        ),
        out_specs=(
            P("exp", "blk", None),
            P(),
            P("exp", "blk", None),
            P(),
            P(),
            P(),
            P(),
            P(),
            P("exp", None, "blk"),
            P("exp", "blk", None),
            P(),
            P(),
            P(),
            P(),
        ),
        check_vma=False,
    )
```

profile of v0, /device:TPU:0, one launch (start us, length us, event | category | flops | bytes accessed | tf_op | source)
XLA Modules:
  0.0 925.5 jit_solution(12557305337200659723)
XLA Ops:
  24.4 37.1 %all-gather.5.cloned.1.call-done = bf16[2,1024,768]{1,2,0:T(8,128)(2,1)} async-done(((bf16[2,256,768]{1,2,0:T(8,128)(2,1)}), bf16[2,1024,768]{1,2,0:T(8,128)(2,1)}) %all-gather.5.cloned.1.call-update) | async-done | bytes 3145744 | tf_op jit(solution)/shard_map/all_gather | solution.py:79
  61.6 46.3 %all-gather.3.cloned.1.call-done = bf16[2,1024,768]{1,2,0:T(8,128)(2,1)} async-done(((bf16[2,256,768]{1,2,0:T(8,128)(2,1)}), bf16[2,1024,768]{1,2,0:T(8,128)(2,1)}) %all-gather.3.cloned.1.call-update) | async-done | bytes 3145744 | tf_op jit(solution)/shard_map/all_gather | solution.py:78
  107.8 38.6 %conditional.1 = (f32[2,12,256]{2,1,0:T(8,128)S(1)}, f32[2,12,256]{2,1,0:T(8,128)S(1)}, f32[2,12,256,64]{2,3,1,0:T(8,128)S(1)}, f32[2,12,256]{2,1,0:T(8,128)S(1)}) conditional(s32[]{:T(128)} %bitcast.3, (s32[1024]{0:T(1024)S(1)}, s32[256]{0:T(256)S(1)}, bf16[2,1024,768]{1,2,0:T(8,128)(2,1)}, bf16[2,256,12,64]{1,0,3,2:T(2,128)(2,1)}, ...), branch_computations={%region_2.5_spmd, %region_5.6_spmd} | conditional | flops 1692657664 | bytes 97981504 | solution.py:98
  108.2 14.8 %fusion = (f32[2,12,256]{2,1,0:T(8,128)S(1)}, f32[2,12,256,1024]{3,2,1,0:T(8,128)}) fusion(pred[256,1024]{1,0:T(8,128)(4,1)S(1)} %broadcast_compare_fusion, bf16[2,1024,12,64]{1,3,2,0:T(8,128)(2,1)} %bitcast.271, bf16[2,256,12,64]{1,0,3,2:T(2,128)(2,1)} %get-tuple-element.51), kind=kOutput, calls=%fused_computation.6 | convolution fusion | flops 824174592 | bytes 29384704 | tf_op jit(solution)/shard_map/cond/branch_0_fun/sqhd,skhd->shqk/dot_general | solution.py:26
  123.1 11.2 %fusion.3 = f32[2,12,256,64]{2,3,1,0:T(8,128)S(1)} fusion(bf16[2,1024,12,64]{1,3,2,0:T(8,128)(2,1)S(1)} %bitcast.305, f32[2,12,256,1024]{3,2,1,0:T(8,128)} %get-tuple-element.79, f32[2,12,256]{2,1,0:T(8,128)S(1)} %broadcast_maximum_fusion, pred[256,1024]{1,0:T(8,128)(4,1)S(1)} %broadcast_compare_fusion), kind=kOutput, calls=%fused_computation.9 | convolution fusion | flops 836763648 | bytes 30171136 | tf_op jit(solution)/shard_map/cond/branch_0_fun/shqk,skhd->shqd/dot_general | solution.py:90
  134.3 12.1 %fusion.2 = f32[2,12,256]{2,1,0:T(8,128)S(1)} fusion(f32[2,12,256,1024]{3,2,1,0:T(8,128)} %get-tuple-element.79, f32[2,12,256]{2,1,0:T(8,128)S(1)} %broadcast_maximum_fusion, pred[256,1024]{1,0:T(8,128)(4,1)S(1)} %broadcast_compare_fusion), kind=kLoop, calls=%fused_computation.8 | loop fusion | flops 31451136 | bytes 25477120 | tf_op jit(solution)/shard_map/cond/branch_0_fun/reduce_sum | solution.py:89
  151.5 69.5 %scatter_fusion = bf16[8,80,768]{2,1,0:T(8,128)(2,1)} fusion(bf16[8,80,768]{2,1,0:T(8,128)(2,1)} %broadcast.264.clone, s32[512]{0:T(512)S(1)} %bitcast.265, bf16[512,768]{1,0:T(8,128)(2,1)S(1)} %add_convert_fusion.2), kind=kCustom, calls=%fused_computation.2 | custom fusion | bytes 2363392 | tf_op jit(solution)/shard_map/scatter | solution.py:120
  221.0 5.5 all-to-all-start
  226.5 44.5 %psum.77 = s32[8]{0:T(128)S(1)} all-reduce(s32[8]{0:T(128)S(1)} %get-tuple-element.62), channel_id=1, replica_groups=mesh['blk'=4,'exp'=8] {'blk','exp'}, use_global_device_ids=true, to_apply=%region_14.15 | all-reduce | flops 8 | bytes 64 | tf_op jit(solution)/shard_map/psum | solution.py:113
  272.6 69.5 %scatter_fusion.1 = bf16[8,80,768]{2,1,0:T(8,128)(2,1)} fusion(bf16[8,80,768]{2,1,0:T(8,128)(2,1)} %broadcast.264.clone.1, s32[512]{0:T(512)S(1)} %bitcast.266, bf16[512,768]{1,0:T(8,128)(2,1)S(1)} %fusion.44), kind=kCustom, calls=%fused_computation.3 | custom fusion | bytes 2363392 | tf_op jit(solution)/shard_map/scatter | solution.py:120
  342.1 4.0 all-to-all-start.2
  346.2 5.3 fusion.30
  351.5 3.0 copy-done.51
  354.6 7.9 fusion.70
  362.5 8.9 all-to-all-done.2
  371.4 4.0 all-to-all-start.1
  375.3 10.5 %fusion.19 = bf16[8,1,80,3072]{3,2,0,1:T(8,128)(2,1)S(1)} fusion(f32[8,80,3072]{2,1,0:T(8,128)} %copy-done.51, bf16[1,3072,768]{2,1,0:T(8,128)(2,1)} %param.25, bf16[8,1,80,768]{3,2,1,0:T(8,128)(2,1)S(1)} %all-to-all-done.2), kind=kOutput, calls=%fused_computation.33 | convolution fusion | flops 3059220480 | bytes 17498112 | tf_op jit(solution)/shard_map/secd,efd->secf/dot_general | solution.py:155
  387.7 6.6 fusion.75
  394.3 6.1 all-to-all-done.1
  400.4 3.6 all-to-all-start.3
  406.2 13.9 %fusion.96 = f32[2,12,256,1024]{3,2,1,0:T(8,128)} fusion(bf16[2,1024,12,64]{1,3,2,0:T(8,128)(2,1)} %bitcast.269, bf16[2,256,12,64]{1,0,3,2:T(2,128)(2,1)} %reshape_reshape.6), kind=kOutput, calls=%fused_computation.120 | convolution fusion | flops 805306368 | bytes 29097984 | tf_op jit(solution)/shard_map/sqhd,skhd->shqk/dot_general | solution.py:26
  420.1 7.4 gather_fusion
  429.2 4.7 gather_fusion.1
  433.9 3.0 multiply_reduce_fusion.1
  444.3 13.0 %fusion.38 = bf16[2,12,64,1024]{3,2,1,0:T(8,128)(2,1)} fusion(f32[2,12,256]{2,1,0:T(8,128)} %add.183, f32[2,12,256,1024]{3,2,1,0:T(8,128)} %fusion.96, pred[256,1024]{1,0:T(8,128)(4,1)} %iota_compare_fusion, bf16[2,256,12,64]{1,0,3,2:T(2,128)(2,1)} %reshape_reshape.7), kind=kOutput, calls=%fused_computation.59 | convolution fusion | flops 838336512 | bytes 29384704 | tf_op jit(solution)/shard_map/shqk,sqhd->kshd/dot_general | solution.py:219
  457.4 4.7 copy.69
  462.1 20.5 %multiply_reduce_fusion = (f32[2,12,256]{2,1,0:T(8,128)S(1)}, f32[2,12,256,1024]{3,2,1,0:T(8,128)}) fusion(f32[2,12,256]{2,1,0:T(8,128)S(1)} %copy-done.26, f32[2,12,256,1024]{3,2,1,0:T(8,128)} %fusion.96, pred[256,1024]{1,0:T(8,128)(4,1)S(1)} %copy-done.24, bf16[2,1024,12,64]{1,3,2,0:T(8,128)(2,1)} %bitcast.304, bf16[2,256,12,64]{1,0,3,2:T(2,128)(2,1)} %reshape_reshape.7), kind=kOutput, calls=%fused_computation.19 | convolution fusion | flops 843048960 | bytes 54575104 | tf_op jit(solution)/shard_map/sqhd,skhd->shqk/dot_general | solution.py:197
  482.7 17.0 %multiply_convert_fusion = bf16[2,12,256,1024]{3,2,1,0:T(8,128)(2,1)S(1)} fusion(f32[2,12,256,1024]{3,2,1,0:T(8,128)} %get-tuple-element.91, f32[2,12,256]{2,1,0:T(8,128)S(1)} %get-tuple-element.90, f32[2,12,256]{2,1,0:T(8,128)S(1)} %copy-done.26, f32[2,12,256,1024]{3,2,1,0:T(8,128)} %fusion.96, pred[256,1024]{1,0:T(8,128)(4,1)S(1)} %copy-done.24), kind=kLoop, calls=%fused_computation.18 | loop fusion | flops 44040192 | bytes 63225856 | tf_op jit(solution)/shard_map/convert_element_type | solution.py:204
  499.7 5.7 multiply_convert_fusion.1
  505.5 4.7 copy.68
  510.2 5.9 pad_maximum_fusion
  516.1 8.6 fusion.32
  524.8 10.9 %fusion.33 = bf16[1,3072,768]{2,1,0:T(8,128)(2,1)} fusion(f32[8,80,3072]{2,1,0:T(8,128)} %copy-done.51, bf16[8,1,80,768]{3,2,1,0:T(8,128)(2,1)} %copy-done.25), kind=kOutput, calls=%fused_computation.52 | convolution fusion | flops 3039952896 | bytes 13565952 | tf_op jit(solution)/shard_map/secf,secd->efd/dot_general | solution.py:152
  538.0 10.1 %fusion.80 = bf16[2,256,12,64]{1,3,2,0:T(8,128)(2,1)S(1)} fusion(bf16[2,1024,12,64]{1,3,2,0:T(8,128)(2,1)} %bitcast.270, bf16[2,12,256,1024]{3,2,1,0:T(8,128)(2,1)} %copy-done.1), kind=kOutput, calls=%fused_computation.104 | convolution fusion | flops 806092800 | bytes 16515072 | tf_op jit(solution)/shard_map/shqk,skhd->sqhd/dot_general | solution.py:206
  549.5 2.2 fusion.141
  551.7 2.2 fusion.140
  553.9 34.0 %reduce-scatter.4.cloned.1.call-done = bf16[256,2,1536]{2,0,1:T(8,128)(2,1)} async-done(((bf16[1024,2,1536]{2,0,1:T(8,128)(2,1)}), bf16[256,2,1536]{2,0,1:T(8,128)(2,1)}) %reduce-scatter.4.cloned.1.call-update) | async-done | bytes 1572880 | tf_op jit(solution)/shard_map/reduce_scatter | solution.py:222
  588.0 3.7 convolution_bitcast_fusion
  591.7 2.2 convolution_bitcast_fusion.1
  596.6 4.1 fusion.138
  600.7 47.2 %reduce-scatter.6.cloned.1.call-done = bf16[1,768,768]{2,1,0:T(8,128)(2,1)} async-done(((bf16[1,768,3072]{2,1,0:T(8,128)(2,1)}), bf16[1,768,768]{2,1,0:T(8,128)(2,1)}) %reduce-scatter.6.cloned.1.call-update) | async-done | bytes 1179664 | tf_op jit(solution)/shard_map/reduce_scatter | solution.py:279
  647.9 2.8 convert_element_type.225
  650.7 57.1 %reduce-scatter.8.cloned.1.call-done = bf16[1,768,768]{2,1,0:T(8,128)(2,1)} async-done(((bf16[1,3072,768]{2,1,0:T(8,128)(2,1)}), bf16[1,768,768]{2,1,0:T(8,128)(2,1)}) %reduce-scatter.8.cloned.1.call-update) | async-done | bytes 1179664 | tf_op jit(solution)/shard_map/reduce_scatter | solution.py:282
  707.8 3.0 convert_element_type.228
  716.5 43.2 %all-reduce = (f32[8]{0:T(128)}, f32[768,8]{0,1:T(8,128)}, f32[768]{0:T(1024)}, f32[768]{0:T(1024)}, f32[768]{0:T(1024)}, /*index=5*/f32[768]{0:T(1024)}) all-reduce(f32[8]{0:T(128)} %get-tuple-element.61, f32[768,8]{0,1:T(8,128)} %fusion.107, f32[768]{0:T(1024)} %get-tuple-element.55, ...), channel_id=1, replica_groups=mesh['blk'=4,'exp'=8] {'blk','exp'}, use_global_device_ids=true, to_apply=%region_16.17 | all-reduce | flops 9224 | bytes 73792 | tf_op jit(solution)/shard_map/psum | solution.py:262
  762.4 3.2 add_convert_fusion
  765.7 141.9 %all-reduce.4.cloned.1.call-done = (f32[768,768]{1,0:T(8,128)}, f32[768,768]{1,0:T(8,128)}, f32[768,768]{1,0:T(8,128)}, f32[768,768]{1,0:T(8,128)}) async-done(((f32[768,768]{1,0:T(8,128)}, f32[768,768]{1,0:T(8,128)}, f32[768,768]{1,0:T(8,128)}, f32[768,768]{1,0:T(8,128)}), (f32[768,768]{1,0:T(8,128)}, f32[768,768]{1,0:T(8,128)}, f32[768,768]{1,0:T(8,128)}, ...) | async-done | bytes 9437200 | tf_op jit(solution)/shard_map/psum | solution.py:262
  907.6 3.4 copy.107
  (188 shorter events, 56.7 us)
Async XLA Ops:
  7.2 5.7 copy-start
  7.2 54.4 %all-gather.5.cloned.1.call-start = ((), (), s32[]{:S(2)}) async-start(), calls=%async_computation.8 | async-start | bytes 3932160 | tf_op jit(solution)/shard_map/all_gather | solution.py:79
  8.7 2.1 copy-start.39
  8.7 2.7 copy-start.29
  11.4 1.5 copy-start.35
  14.9 4.5 copy-start.28
  14.9 93.0 %all-gather.3.cloned.1.call-start = ((), (), s32[]{:S(2)}) async-start(), calls=%async_computation.7 | async-start | bytes 3932160 | tf_op jit(solution)/shard_map/all_gather | solution.py:78
  108.2 14.9 %copy-start.46 = (bf16[2,1024,768]{1,2,0:T(8,128)(2,1)S(1)}, bf16[2,1024,768]{1,2,0:T(8,128)(2,1)}, u32[]{:S(2)}) copy-start(bf16[2,1024,768]{1,2,0:T(8,128)(2,1)} %get-tuple-element.15) | copy-start | bytes 9437188 | tf_op jit(solution)/shard_map/cond
  146.5 1.5 copy-start.47
  147.7 1.5 copy-start.15
  147.7 2.3 copy-start.32
  147.7 2.3 copy-start.45
  150.3 120.7 %copy-start.9 = (bf16[512,768]{1,0:T(8,128)(2,1)}, bf16[512,768]{1,0:T(8,128)(2,1)S(1)}, u32[]{:S(2)}) copy-start(bf16[512,768]{1,0:T(8,128)(2,1)S(1)} %add_convert_fusion.2) | copy-start | bytes 2359300
  151.4 119.6 %copy-start.31 = (bf16[768,8]{0,1:T(8,128)(2,1)S(1)}, bf16[768,8]{0,1:T(8,128)(2,1)}, u32[]{:S(2)}) copy-start(bf16[768,8]{0,1:T(8,128)(2,1)} %param.23) | copy-start | bytes 36868
  221.0 50.4 %copy-start.7 = (bf16[2,256,768]{2,1,0:T(8,128)(2,1)S(1)}, bf16[2,256,768]{2,1,0:T(8,128)(2,1)}, u32[]{:S(2)}) copy-start(bf16[2,256,768]{2,1,0:T(8,128)(2,1)} %param.17) | copy-start | bytes 2359300
  221.0 121.2 %all-to-all-start = ((bf16[8,1,80,768]{3,2,1,0:T(8,128)(2,1)}), bf16[8,1,80,768]{3,2,1,0:T(8,128)(2,1)}, u32[]{:S(2)}, u32[]{:S(2)}) async-start(bf16[8,1,80,768]{3,2,1,0:T(8,128)(2,1)} %bitcast.14), calls=%async_computation | async-start | bytes 1966080 | tf_op jit(solution)/shard_map/all_to_all | solution.py:127
  271.0 133.0 %copy-start.50 = (s32[8]{0:T(128)}, s32[8]{0:T(128)S(1)}, u32[]{:S(2)}) copy-start(s32[8]{0:T(128)S(1)} %psum.77) | copy-start | bytes 100
  271.4 134.2 %copy-start.33 = (f32[512]{0:T(512)}, f32[512]{0:T(512)S(1)}, u32[]{:S(2)}) copy-start(f32[512]{0:T(512)S(1)} %add_divide_fusion) | copy-start | bytes 6148
  342.1 29.2 %all-to-all-start.2 = ((bf16[8,1,80,768]{3,2,1,0:T(8,128)(2,1)}), bf16[8,1,80,768]{3,2,1,0:T(8,128)(2,1)S(1)}, u32[]{:S(2)}, u32[]{:S(2)}) async-start(bf16[8,1,80,768]{3,2,1,0:T(8,128)(2,1)} %bitcast.35), calls=%async_computation.2 | async-start | bytes 1966080 | tf_op jit(solution)/shard_map/all_to_all | solution.py:151
  351.5 3.1 copy-start.51
  371.4 14.5 %copy-start.25 = (bf16[8,1,80,768]{3,2,1,0:T(8,128)(2,1)}, bf16[8,1,80,768]{3,2,1,0:T(8,128)(2,1)S(1)}, u32[]{:S(2)}) copy-start(bf16[8,1,80,768]{3,2,1,0:T(8,128)(2,1)S(1)} %all-to-all-done.2) | copy-start | bytes 2949124
  371.4 29.1 %all-to-all-start.1 = ((bf16[8,1,80,768]{3,2,1,0:T(8,128)(2,1)}), bf16[8,1,80,768]{3,2,1,0:T(8,128)(2,1)S(1)}, u32[]{:S(2)}, u32[]{:S(2)}) async-start(bf16[8,1,80,768]{3,2,1,0:T(8,128)(2,1)} %fusion.70), calls=%async_computation.1 | async-start | bytes 1966080 | tf_op jit(solution)/shard_map/all_to_all | solution.py:136
  385.8 1.9 copy-start.52
  400.4 28.7 %all-to-all-start.3 = ((bf16[8,1,80,768]{3,2,1,0:T(8,128)(2,1)}), bf16[8,1,80,768]{3,2,1,0:T(8,128)(2,1)S(1)}, u32[]{:S(2)}, u32[]{:S(2)}) async-start(bf16[8,1,80,768]{3,2,1,0:T(8,128)(2,1)} %fusion.75), calls=%async_computation.3 | async-start | bytes 1966080 | tf_op jit(solution)/shard_map/all_to_all | solution.py:166
  404.0 184.0 %reduce-scatter.4.cloned.1.call-start = ((), (), s32[]{:S(2)}) async-start(), calls=%async_computation.9 | async-start | bytes 7864320 | tf_op jit(solution)/shard_map/reduce_scatter | solution.py:222
  433.9 3.1 copy-start.5
  433.9 3.1 copy-start.12
  433.9 3.1 copy-start.34
  433.9 3.1 copy-start.37
  437.0 1.8 copy-start.8
  438.8 3.1 copy-start.43
  457.4 4.7 copy-start.24
  457.4 4.7 copy-start.26
  499.7 5.7 copy-start.1
  516.1 131.8 %reduce-scatter.6.cloned.1.call-start = ((), (), s32[]{:S(2)}) async-start(), calls=%async_computation.10 | async-start | bytes 5898240 | tf_op jit(solution)/shard_map/reduce_scatter | solution.py:279
  524.8 183.1 %reduce-scatter.8.cloned.1.call-start = ((), (), s32[]{:S(2)}) async-start(), calls=%async_computation.11 | async-start | bytes 5898240 | tf_op jit(solution)/shard_map/reduce_scatter | solution.py:282
  535.7 371.8 %all-reduce.4.cloned.1.call-start = ((), (), s32[]{:S(2)}) async-start(), calls=%async_computation.12 | async-start | bytes 18874368 | tf_op jit(solution)/shard_map/psum | solution.py:262
  538.0 13.8 %copy-start.10 = (bf16[2,256,768]{2,1,0:T(8,128)(2,1)}, bf16[2,256,768]{2,1,0:T(8,128)(2,1)S(1)}, u32[]{:S(2)}) copy-start(bf16[2,256,768]{2,1,0:T(8,128)(2,1)S(1)} %fusion.58) | copy-start | bytes 2359300
  549.5 2.2 copy-start.17
  588.0 3.7 copy-start.11
  588.0 3.7 copy-start.13
  707.8 3.0 copy-start.14
  707.8 3.1 copy-start.49
  712.2 1.7 copy-start.42
  712.2 2.8 copy-start.36
  907.6 3.4 copy-start.22
  910.9 2.5 copy-start.21
  913.5 2.5 copy-start.20
  (15 other events, 17.4 us)
Sparse Core Ops, SparseCore 0:
  15.0 46.5 all-gather.4
  64.0 43.8 all-gather.2
  516.2 71.7 reduce-scatter.3
  590.8 57.0 reduce-scatter.5
  650.7 57.0 reduce-scatter.7
  714.5 193.0 all-reduce.3
where the time goes:
time: 940 us; the launch traced here: 926 us
  waiting for transfers between devices  379 us (40%)
  local copies, waits for them, and re-layouts  193 us (21%)
  matrix products  169 us (18%)
  blocking collectives  87.7 us (9%)
  other arithmetic  62.1 us (7%)
  starting transfers between devices  17.5 us (2%)
  between operations  17.4 us (2%)
    psum x1, waiting for transfers between devices, shards(): lax.psum((grad_query_weight, grad_key_weight, grad_value_weight, grad_out...  142 us
    scatter x2, local copies, waits for them, and re-layouts, fill_slots(): filled = jnp.zeros((expert_count, capacity, model_width), jnp.bfloat16).a...  139 us
    reduce_scatter x1, waiting for transfers between devices, shards(): lax.psum_scatter(grad_expert_out.astype(jnp.bfloat16), 'blk', scatter_dim...  57.1 us
    reduce_scatter x1, waiting for transfers between devices, shards(): lax.psum_scatter(grad_expert_in.astype(jnp.bfloat16), 'blk', scatter_dime...  47.2 us
    all_gather x1, waiting for transfers between devices, shards(): piece_keys = lax.all_gather(key_rows, 'blk', axis=1, tiled=True)  46.3 us
    psum x1, blocking collectives, shards(): counts = lax.psum(jnp.sum(hot_int, axis=0), ('blk', 'exp'))  44.5 us
    psum x1, blocking collectives, shards(): lax.psum((grad_query_weight, grad_key_weight, grad_value_weight, grad_out...  43.2 us
    all_gather x1, waiting for transfers between devices, shards(): piece_values = lax.all_gather(value_rows, 'blk', axis=1, tiled=True)  37.1 us
  transfers between devices with their start and end apart: 10, of which 8 were waited for; matrix products, arithmetic and copies ran while one was open for 21% of the time, Pallas kernels for 0%

commit v1 on v0

v1 whole, which is shorter than its diff:
```python
import functools

import jax
import jax.numpy as jnp
from jax import lax
from jax.experimental import pallas as pl
from jax.experimental.pallas import tpu as pltpu
from jax.sharding import PartitionSpec as P

HEAD_DIM = 64
PAIR = 2 * HEAD_DIM
EPSILON = 1e-05
SCALE = HEAD_DIM ** (-0.5)
QUERY_ROWS = 256
ROWS = 128
FF_COLS = 256
MESH = pl.DeviceIdType.MESH
BF16, F32 = jnp.bfloat16, jnp.float32
VMEM_BYTES = 62 << 20
NT = (((1,), (1,)), ((), ()))
TN = (((0,), (0,)), ((), ()))


def dot(left, right, dims=(((1,), (0,)), ((), ()))):
    return lax.dot_general(left, right, dims, preferred_element_type=F32)


def iota(shape, dim):
    return lax.broadcasted_iota(jnp.int32, shape, dim)


def normalize(values):
    centered = values - jnp.mean(values, axis=-1, keepdims=True)
    variance = jnp.mean(centered * centered, axis=-1, keepdims=True)
    inverse = lax.rsqrt(variance + EPSILON)
    return centered * inverse, inverse


def norm_back(hat, inverse, gain, grad):
    scaled = grad * gain
    return inverse * (
        scaled
        - jnp.mean(scaled, axis=-1, keepdims=True)
        - hat * jnp.mean(scaled * hat, axis=-1, keepdims=True)
    )


def split_rows(base, size):
    return pl.ds(pl.multiple_of(base, size), size)


class Place:
    def __init__(self, cfg):
        self.__dict__.update(cfg)
        self.b = lax.axis_index("blk")
        self.e = lax.axis_index("exp")
        self.c = lax.rem(self.e, 2)
        self.pair = self.e - self.c
        self.sibling = self.pair + 1 - self.c

    def greet(self):
        bar = pltpu.get_barrier_semaphore()

        def exp_peer(k, _):
            pl.semaphore_signal(
                bar, 1, device_id=(self.b, lax.rem(self.e + k, self.ne)), device_id_type=MESH
            )

        def blk_peer(k, _):
            there = lax.rem(self.b + k, self.nb)
            pl.semaphore_signal(bar, 1, device_id=(there, self.e), device_id_type=MESH)
            pl.semaphore_signal(bar, 1, device_id=(there, self.sibling), device_id_type=MESH)

        lax.fori_loop(1, self.ne, exp_peer, None)
        lax.fori_loop(1, self.nb, blk_peer, None)
        pl.semaphore_wait(bar, self.ne - 1 + 2 * (self.nb - 1))

    def is_me(self, there):
        return there[0] * self.ne + there[1] == self.b * self.ne + self.e


def remote(src, dst, send_sem, recv_sem, there):
    return pltpu.make_async_remote_copy(
        src, dst, send_sem, recv_sem, device_id=there, device_id_type=MESH
    )


def push(me, src, dst, send_sem, recv_sem, there):
    mine = me.is_me(there)

    @pl.when(mine)
    def _():
        pltpu.make_async_copy(src, dst, recv_sem).start()

    @pl.when(jnp.logical_not(mine))
    def _():
        remote(src, dst, send_sem, recv_sem, there).start()


def push_done(me, src, dst, send_sem, recv_sem, there):
    @pl.when(jnp.logical_not(me.is_me(there)))
    def _():
        remote(src, dst, send_sem, recv_sem, there).wait_send()


def landed(dst, recv_sem):
    pltpu.make_async_copy(dst, dst, recv_sem).wait()


def exchange_start(me, src, dst, send_sem, recv_sem, size):
    def one(k, _):
        there = lax.rem(me.e + k, me.ne)
        remote(
            src.at[split_rows(there * size, size)],
            dst.at[split_rows(me.e * size, size)],
            send_sem.at[k],
            recv_sem.at[k],
            (me.b, there),
        ).start()

    own = split_rows(me.e * size, size)
    pltpu.make_async_copy(src.at[own], dst.at[own], recv_sem.at[0]).start()
    lax.fori_loop(1, me.ne, one, None)


def exchange_wait(me, src, dst, send_sem, recv_sem, size):
    own = split_rows(me.e * size, size)
    landed(dst.at[own], recv_sem.at[0])

    def one(k, _):
        source = lax.rem(me.e + me.ne - k, me.ne)
        landed(dst.at[split_rows(source * size, size)], recv_sem.at[k])

    lax.fori_loop(1, me.ne, one, None)


def exchange_sent(me, src, dst, send_sem, recv_sem, size):
    def one(k, _):
        there = lax.rem(me.e + k, me.ne)
        remote(
            src.at[split_rows(there * size, size)],
            dst.at[split_rows(me.e * size, size)],
            send_sem.at[k],
            recv_sem.at[k],
            (me.b, there),
        ).wait_send()

    lax.fori_loop(1, me.ne, one, None)


def token_slots(me, idx):
    rows = idx.shape[0]
    hot = (idx == iota((rows, 128), 1)).astype(F32)
    earlier = (iota((rows, rows), 1) < iota((rows, rows), 0)).astype(F32).astype(BF16)
    ahead = dot(earlier, hot.astype(BF16))
    slot = jnp.sum(ahead * hot, axis=1, keepdims=True)
    return idx.astype(F32) * me.cap + slot, jnp.sum(hot, axis=0, keepdims=True)


def slots_by_token(me, slot):
    rows = slot.shape[0]
    across = jnp.transpose(jnp.broadcast_to(slot, (rows, 128)))[0:1, :]
    slots = me.experts * me.cap
    return (iota((slots, rows), 0) == across.astype(jnp.int32)).astype(F32).astype(BF16)


def tokens_by_slot(me, slot):
    rows = slot.shape[0]
    slots = me.experts * me.cap
    return (iota((rows, slots), 1) == slot.astype(jnp.int32)).astype(F32).astype(BF16)


def head_masks():
    lane = iota((1, PAIR), 1)
    first = (lane < HEAD_DIM).astype(F32).astype(BF16)
    second = (lane >= HEAD_DIM).astype(F32).astype(BF16)
    return first, second


def attend_kernel(
    cfg,
    x, og, idx, gain, bias, wq, wk, wv,
    q, k, v, a, lse, o, dh, cnt,
    w, xin, o_send, lse_cols, dh_send, cnt_exp, cnt_part, cnt_blk,
    wsem, xs, xr, fs, fr, os, orr, ds, dr, cs, cr, bs, br,
):
    me = Place(cfg)
    half = me.span // 2
    columns = pl.ds(pl.multiple_of(me.c * me.half_width, 128), me.half_width)
    loads = [
        pltpu.make_async_copy(m.at[:, columns], w.at[j], wsem.at[j])
        for j, m in enumerate((wq, wk, wv))
    ]
    for load in loads:
        load.start()
    me.greet()

    def row_moves():
        for s in range(me.seqs):
            for h in range(2):
                there = (me.c * me.seqs + s, me.pair + h)
                yield (
                    x.at[pl.ds(s * me.span + h * half, half)],
                    xin.at[me.b],
                    xs.at[2 * s + h],
                    xr.at[me.b],
                    there,
                )

    for move in row_moves():
        push(me, *move)

    slot, counts = token_slots(me, idx[...])
    dh_send[...] = dot(slots_by_token(me, slot), og[...]).astype(BF16)
    exchange_start(me, dh_send, dh, ds, dr, me.cap)
    cnt_part[...] = jnp.broadcast_to(counts, cnt_part.shape)
    own = me.e
    pltpu.make_async_copy(cnt_part, cnt_exp.at[own], cr.at[0]).start()

    def count_move(j):
        return remote(
            cnt_part, cnt_exp.at[me.e], cs.at[j], cr.at[j], (me.b, lax.rem(me.e + j, me.ne))
        )

    lax.fori_loop(1, me.ne, lambda j, _: count_move(j).start(), None)

    def forward_move(j):
        rows = split_rows(j * me.span + me.c * half, half)
        return remote(a.at[rows], a.at[rows], fs.at[j], fr.at[j], (me.b, me.sibling))

    for j in range(me.nb):
        landed(xin.at[j], xr.at[j])
        hat, _ = normalize(xin[j].astype(F32))
        a[split_rows(j * me.span + me.c * half, half), :] = (
            hat * gain[...] + bias[...]
        ).astype(BF16)
        forward_move(j).start()

    landed(cnt_exp.at[me.e], cr.at[0])
    lax.fori_loop(
        1,
        me.ne,
        lambda j, _: landed(cnt_exp.at[lax.rem(me.e + me.ne - j, me.ne)], cr.at[j]),
        None,
    )
    lax.fori_loop(1, me.ne, lambda j, _: count_move(j).wait_send(), None)
    cnt_blk[me.b] = jnp.sum(cnt_exp[...], axis=0)

    def blk_move(j):
        return remote(
            cnt_blk.at[me.b],
            cnt_blk.at[me.b],
            bs.at[j],
            br.at[j],
            (lax.rem(me.b + j, me.nb), me.e),
        )

    for j in range(1, me.nb):
        blk_move(j).start()

    for load in loads:
        load.wait()
    first, second = head_masks()
    blocks = me.length // QUERY_ROWS
    spans = QUERY_ROWS // me.span
    lane = iota((1, PAIR), 1)
    visible = iota((QUERY_ROWS, QUERY_ROWS), 1) <= iota((QUERY_ROWS, QUERY_ROWS), 0)
    source = me.pair + lax.div(me.b, me.seqs)

    def o_move(j):
        return (
            o_send.at[pl.ds(j * me.span, me.span)],
            o.at[split_rows(lax.rem(me.b, me.seqs) * me.span, me.span), columns],
            os.at[j],
            orr.at[2 * lax.rem(me.b, me.seqs) + me.c],
            (j, source),
        )

    for i in range(blocks):
        for j in range(i * spans, (i + 1) * spans):
            theirs = split_rows(j * me.span + (1 - me.c) * half, half)
            landed(a.at[theirs], fr.at[j])
        here = pl.ds(i * QUERY_ROWS, QUERY_ROWS)
        rows = a[here, :]
        q[here, :] = dot(rows, w[0]).astype(BF16) * jnp.asarray(SCALE, BF16)
        k[here, :] = dot(rows, w[1]).astype(BF16)
        v[here, :] = dot(rows, w[2]).astype(BF16)

        def pair_of_heads(p, _, i=i, here=here):
            lanes = split_rows(p * PAIR, PAIR)
            queries = q[here, lanes]
            parts = [pl.ds(i * QUERY_ROWS, QUERY_ROWS)]
            if i:
                parts.append(pl.ds(0, i * QUERY_ROWS))
            done = []
            for h, mask in enumerate((first, second)):
                masked = queries * mask
                scores = [dot(masked, k[part, lanes], NT) for part in parts]
                scores[0] = jnp.where(visible, scores[0], -1e30)
                peak = functools.reduce(
                    jnp.maximum, [jnp.max(s, axis=1, keepdims=True) for s in scores]
                )
                powers = [jnp.exp(s - peak) for s in scores]
                total = sum(jnp.sum(s, axis=1, keepdims=True) for s in powers)
                mixed = sum(dot(s.astype(BF16), v[part, lanes]) for s, part in zip(powers, parts))
                done.append(mixed / total)
                lse_cols[here, :] = jnp.where(
                    lane == 2 * p + h, peak + jnp.log(total), lse_cols[here, :]
                )
            o_send[here, lanes] = jnp.where(lane < HEAD_DIM, done[0], done[1]).astype(BF16)

        lax.fori_loop(0, me.half_width // PAIR, pair_of_heads, None)
        for j in range(i * spans, (i + 1) * spans):
            push(me, *o_move(j))

    lse[...] = jnp.transpose(lse_cols[...])[0:8, :]

    for j in range(1, me.nb):
        blk_move(j).wait_send()
        landed(cnt_blk.at[lax.rem(me.b + me.nb - j, me.nb)], br.at[j])
    cnt[...] = jnp.sum(cnt_blk[...], axis=0)
    for move in row_moves():
        push_done(me, *move)
    for j in range(me.nb):
        forward_move(j).wait_send()
        push_done(me, *o_move(j))
    for s in range(me.seqs):
        for h in range(2):
            landed(
                o.at[pl.ds(s * me.span, me.span), pl.ds(h * me.half_width, me.half_width)],
                orr.at[2 * s + h],
            )
    exchange_wait(me, dh_send, dh, ds, dr, me.cap)
    exchange_sent(me, dh_send, dh, ds, dr, me.cap)


def gelu_parts(u):
    root = 0.7978845608028654
    cubic = 0.044715
    square = u * u
    t = jnp.tanh(root * u * (1.0 + cubic * square))
    value = 0.5 * u * (1.0 + t)
    slope = 0.5 * (1.0 + t) + (0.5 * root) * u * (1.0 - t * t) * (1.0 + 3.0 * cubic * square)
    return value, slope


def expert_kernel(
    cfg,
    x, o, wo, router, gain, bias, idx, dh, cnt, win_hbm, wout_hbm,
    h1, gate, mass, back, y, dwin, dwout, drouter,
    win, wout, n2, disp, took, g, du, made, dn,
    wsem, ns, nr, rs, rr,
):
    me = Place(cfg)
    loads = [
        pltpu.make_async_copy(win_hbm, win, wsem.at[0]),
        pltpu.make_async_copy(wout_hbm, wout, wsem.at[1]),
    ]
    for load in loads:
        load.start()
    me.greet()
    expert_lane = iota((ROWS, me.experts), 1)
    mass[...] = jnp.zeros_like(mass)

    def token_rows(r, _):
        here = split_rows(r * ROWS, ROWS)
        hidden = x[here, :].astype(F32) + dot(o[here, :], wo[...])
        h1[here, :] = hidden
        hat, _ = normalize(hidden)
        normed = (hat * gain[...] + bias[...]).astype(BF16)
        n2[here, :] = normed
        logits = dot(normed, router[...])
        hot = idx[here, :] == expert_lane
        value = jax.nn.sigmoid(jnp.sum(jnp.where(hot, logits, 0.0), axis=1, keepdims=True))
        gate[here, :] = value
        mass[...] += jnp.broadcast_to(
            jnp.sum(jnp.where(hot, value, 0.0), axis=0, keepdims=True), mass.shape
        )

    lax.fori_loop(0, me.rows // ROWS, token_rows, None)
    slot, _ = token_slots(me, idx[...])
    disp[...] = dot(slots_by_token(me, slot), n2[...]).astype(BF16)
    exchange_start(me, disp, took, ns, nr, me.cap)
    for load in loads:
        load.wait()
    exchange_wait(me, disp, took, ns, nr, me.cap)
    exchange_sent(me, disp, took, ns, nr, me.cap)

    slots = me.experts * me.cap
    lanes = iota((slots, me.experts), 1)
    logits = jnp.sum(jnp.where(lanes == me.e, dot(took[...], router[...]), 0.0), axis=1, keepdims=True)
    value = jax.nn.sigmoid(logits)
    disp[...] = (value * dh[...].astype(F32)).astype(BF16)

    def hidden_columns(f, _):
        here = split_rows(f * FF_COLS, FF_COLS)
        act, slope = gelu_parts(dot(took[...], win[:, here]))
        g[:, here] = act.astype(BF16)
        du[:, here] = (dot(disp[...], wout[here, :], NT) * slope).astype(BF16)

    lax.fori_loop(0, me.ff // FF_COLS, hidden_columns, None)

    def model_columns(f, _):
        here = split_rows(f * FF_COLS, FF_COLS)
        y[:, here] = dot(g[...], wout[:, here]).astype(BF16)
        made[:, here] = dot(du[...], win[here, :], NT)

    lax.fori_loop(0, me.width // FF_COLS, model_columns, None)

    load_lane = iota(cnt.shape, 1)
    load = jnp.sum(jnp.where(load_lane == me.e, cnt[...], 0.0), axis=1, keepdims=True)[0:1, :]
    weight = (load - me.mean_load) / me.mean_load
    dgate = (
        jnp.sum(dh[...].astype(F32) * y[...].astype(F32), axis=1, keepdims=True)
        + weight / me.tokens
    )
    dlogits = jnp.where(lanes == me.e, dgate * value * (1.0 - value), 0.0).astype(BF16)
    dn[...] = (made[...] + dot(dlogits, router[...], NT)).astype(BF16)
    exchange_start(me, dn, back, rs, rr, me.cap)
    drouter[...] = dot(dlogits, took[...], TN)

    def weight_columns(f, _):
        here = split_rows(f * FF_COLS, FF_COLS)
        dwin[:, here] = dot(took[...], du[:, here], TN).astype(BF16)
        dwout[here, :] = dot(g[:, here], disp[...], TN).astype(BF16)

    lax.fori_loop(0, me.ff // FF_COLS, weight_columns, None)
    exchange_wait(me, dn, back, rs, rr, me.cap)
    exchange_sent(me, dn, back, rs, rr, me.cap)


def backward_kernel(
    cfg,
    x, og, idx, h1, gate, back, y, o, q, k, v, a, lse, wo, wq, wk, wv,
    gain1, bias1, gain2, bias2,
    out, dx, dwq, dwk, dwv, dwo, norms,
    w, dh1, do_send, do, yback, dk_sum, dv_sum, dq, dk, dv, da, swap_send, swap, da_send, da_in,
    wsem, ys, yr, os, orr, ss, sr, fs, fr,
):
    me = Place(cfg)
    half = me.span // 2
    columns = pl.ds(pl.multiple_of(me.c * me.half_width, 128), me.half_width)
    loads = [
        pltpu.make_async_copy(m.at[:, columns], w.at[j], wsem.at[j])
        for j, m in enumerate((wq, wk, wv))
    ]
    for load in loads:
        load.start()
    me.greet()
    exchange_start(me, y, yback, ys, yr, me.cap)
    slot, _ = token_slots(me, idx[...])
    takes = tokens_by_slot(me, slot)
    norms[...] = jnp.zeros_like(norms)
    da[0 : me.rows, :] = dot(takes, back[...])

    def norm_rows(r, _):
        here = split_rows(r * ROWS, ROWS)
        grad = da[here, :]
        hat, inverse = normalize(h1[here, :])
        norms[2:3, :] += jnp.sum(grad * hat, axis=0, keepdims=True)
        norms[3:4, :] += jnp.sum(grad, axis=0, keepdims=True)
        total = og[here, :].astype(F32) + norm_back(hat, inverse, gain2[...], grad)
        dh1[here, :] = total
        do_send[here, :] = dot(total.astype(BF16), wo[...], NT).astype(BF16)

    lax.fori_loop(0, me.rows // ROWS, norm_rows, None)

    def o_moves():
        for s in range(me.seqs):
            for h in range(2):
                yield (
                    do_send.at[
                        pl.ds(s * me.span, me.span), pl.ds(h * me.half_width, me.half_width)
                    ],
                    do.at[split_rows(me.b * me.span, me.span)],
                    os.at[2 * s + h],
                    orr.at[me.b],
                    (me.c * me.seqs + s, me.pair + h),
                )

    for move in o_moves():
        push(me, *move)
    dwo[...] = dot(o[...], dh1[...].astype(BF16), TN)
    for j in range(me.nb):
        landed(do.at[pl.ds(j * me.span, me.span)], orr.at[j])

    first, second = head_masks()
    blocks = me.length // QUERY_ROWS
    visible = iota((QUERY_ROWS, QUERY_ROWS), 0) <= iota((QUERY_ROWS, QUERY_ROWS), 1)

    def pair_of_heads(p, _):
        lanes = split_rows(p * PAIR, PAIR)
        dk_sum[...] = jnp.zeros_like(dk_sum)
        dv_sum[...] = jnp.zeros_like(dv_sum)
        for i in range(blocks):
            here = pl.ds(i * QUERY_ROWS, QUERY_ROWS)
            queries, grads = q[here, lanes], do[here, lanes]
            parts = [here]
            if i:
                parts.append(pl.ds(0, i * QUERY_ROWS))
            dq_block = jnp.zeros((QUERY_ROWS, PAIR), F32)
            for h, mask in enumerate((first, second)):
                qm, gm = queries * mask, grads * mask
                sums = lse[pl.ds(2 * p + h, 1), here]
                scores = [dot(k[part, lanes], qm, NT) for part in parts]
                powers = [jnp.exp(s - sums) for s in scores]
                powers[0] = jnp.where(visible, powers[0], 0.0)
                weighted = [
                    s * dot(v[part, lanes], gm, NT) for s, part in zip(powers, parts)
                ]
                delta = sum(jnp.sum(t, axis=0, keepdims=True) for t in weighted)
                for s, t, part in zip(powers, weighted, parts):
                    ds = (t - s * delta).astype(BF16)
                    dv_sum[part, :] += dot(s.astype(BF16), gm)
                    dk_sum[part, :] += dot(ds, qm)
                    dq_block += dot(ds, k[part, lanes] * mask, TN)
            dq[here, lanes] = (dq_block * SCALE).astype(BF16)
        dk[:, lanes] = dk_sum[...].astype(BF16)
        dv[:, lanes] = dv_sum[...].astype(BF16)

    lax.fori_loop(0, me.half_width // PAIR, pair_of_heads, None)

    for load in loads:
        load.wait()
    da[...] = dot(dq[...], w[0], NT) + dot(dk[...], w[1], NT) + dot(dv[...], w[2], NT)
    for j in range(me.nb):
        swap_send[j] = da[split_rows(j * me.span + (1 - me.c) * half, half), :].astype(BF16)
    swap_move = remote(swap_send, swap, ss, sr, (me.b, me.sibling))
    swap_move.start()
    dwq[...] = dot(a[...], dq[...], TN)
    swap_move.wait()
    source = me.pair + lax.div(me.b, me.seqs)

    def da_move(j):
        return (
            da_send.at[j],
            da_in.at[split_rows(lax.rem(me.b, me.seqs) * me.span + me.c * half, half)],
            fs.at[j],
            fr.at[2 * lax.rem(me.b, me.seqs) + me.c],
            (j, source),
        )

    for j in range(me.nb):
        mine = da[split_rows(j * me.span + me.c * half, half), :]
        da_send[j] = (mine + swap[j].astype(F32)).astype(BF16)
        push(me, *da_move(j))
    dwk[...] = dot(a[...], dk[...], TN)
    dwv[...] = dot(a[...], dv[...], TN)

    exchange_wait(me, y, yback, ys, yr, me.cap)
    exchange_sent(me, y, yback, ys, yr, me.cap)
    da[0 : me.rows, :] = dot(takes, yback[...])

    def out_rows(r, _):
        here = split_rows(r * ROWS, ROWS)
        out[here, :] = (h1[here, :] + gate[here, :] * da[here, :]).astype(BF16)

    lax.fori_loop(0, me.rows // ROWS, out_rows, None)

    for s in range(me.seqs):
        for h in range(2):
            landed(da_in.at[pl.ds(s * me.span + h * half, half)], fr.at[2 * s + h])

    def token_rows(r, _):
        here = split_rows(r * ROWS, ROWS)
        grad = da_in[here, :].astype(F32)
        hat, inverse = normalize(x[here, :].astype(F32))
        norms[0:1, :] += jnp.sum(grad * hat, axis=0, keepdims=True)
        norms[1:2, :] += jnp.sum(grad, axis=0, keepdims=True)
        dx[here, :] = (dh1[here, :] + norm_back(hat, inverse, gain1[...], grad)).astype(BF16)

    lax.fori_loop(0, me.rows // ROWS, token_rows, None)
    for move in o_moves():
        push_done(me, *move)
    for j in range(me.nb):
        push_done(me, *da_move(j))


def in_vmem(count):
    return [pl.BlockSpec(memory_space=pltpu.VMEM)] * count


def anywhere(count):
    return [pl.BlockSpec(memory_space=pl.ANY)] * count


def call(body, cfg, number, in_specs, outs, scratch, name, cost):
    return pl.pallas_call(
        functools.partial(body, cfg),
        out_shape=[jax.ShapeDtypeStruct(shape, kind) for shape, kind in outs],
        in_specs=in_specs,
        out_specs=in_vmem(len(outs)),
        scratch_shapes=scratch,
        compiler_params=pltpu.CompilerParams(
            collective_id=number, has_side_effects=True, vmem_limit_bytes=VMEM_BYTES
        ),
        cost_estimate=pl.CostEstimate(flops=cost, bytes_accessed=1 << 24, transcendentals=1 << 22),
        name=name,
    )


def shards(
    tokens,
    output_grad,
    expert_index,
    query_weight,
    key_weight,
    value_weight,
    output_weight,
    router_weight,
    expert_in,
    expert_out,
    norm1_gain,
    norm1_bias,
    norm2_gain,
    norm2_bias,
):
    seqs, span, width = tokens.shape
    rows = seqs * span
    nb, ne = lax.axis_size("blk"), lax.axis_size("exp")
    length = span * nb
    experts = router_weight.shape[1]
    ff = expert_in.shape[2]
    cap = -(-max(2, rows * 5 // (4 * experts)) // 16) * 16
    slots = experts * cap
    token_total = rows * nb * ne
    half_width = width // 2
    cfg = dict(
        seqs=seqs, span=span, width=width, rows=rows, nb=nb, ne=ne, length=length,
        experts=experts, ff=ff, cap=cap, half_width=half_width, tokens=token_total,
        mean_load=token_total / experts,
    )
    x = tokens.reshape(rows, width)
    og = output_grad.reshape(rows, width)
    idx = expert_index.reshape(rows, 1)
    gain1, bias1 = norm1_gain.reshape(1, width), norm1_bias.reshape(1, width)
    gain2, bias2 = norm2_gain.reshape(1, width), norm2_bias.reshape(1, width)
    dma = pltpu.SemaphoreType.DMA
    vmem = pltpu.VMEM
    half = span // 2
    q, k, v, a, lse, o, dh, cnt = call(
        attend_kernel, cfg, 1,
        in_vmem(5) + anywhere(3),
        [
            ((length, half_width), BF16),
            ((length, half_width), BF16),
            ((length, half_width), BF16),
            ((length, width), BF16),
            ((8, length), F32),
            ((rows, width), BF16),
            ((slots, width), BF16),
            ((8, 128), F32),
        ],
        [
            vmem((3, width, half_width), BF16),
            vmem((nb, half, width), BF16),
            vmem((length, half_width), BF16),
            vmem((length, 128), F32),
            vmem((slots, width), BF16),
            vmem((ne, 8, 128), F32),
            vmem((8, 128), F32),
            vmem((nb, 8, 128), F32),
            dma((3,)),
            dma((2 * seqs,)), dma((nb,)),
            dma((nb,)), dma((nb,)),
            dma((nb,)), dma((2 * seqs,)),
            dma((ne,)), dma((ne,)),
            dma((ne,)), dma((ne,)),
            dma((nb,)), dma((nb,)),
        ],
        "attend", 8 << 30,
    )(x, og, idx, gain1, bias1, query_weight, key_weight, value_weight)
    h1, gate, mass, back, y, dwin, dwout, drouter = call(
        expert_kernel, cfg, 2,
        in_vmem(9) + anywhere(2),
        [
            ((rows, width), F32),
            ((rows, 1), F32),
            ((8, experts), F32),
            ((slots, width), BF16),
            ((slots, width), BF16),
            ((width, ff), BF16),
            ((ff, width), BF16),
            ((experts, width), F32),
        ],
        [
            vmem((width, ff), BF16),
            vmem((ff, width), BF16),
            vmem((rows, width), BF16),
            vmem((slots, width), BF16),
            vmem((slots, width), BF16),
            vmem((slots, ff), BF16),
            vmem((slots, ff), BF16),
            vmem((slots, width), F32),
            vmem((slots, width), BF16),
            dma((2,)),
            dma((ne,)), dma((ne,)),
            dma((ne,)), dma((ne,)),
        ],
        "experts", 20 << 30,
    )(
        x, o, output_weight, router_weight, gain2, bias2, idx, dh, cnt,
        expert_in.reshape(width, ff), expert_out.reshape(ff, width),
    )
    out, dx, dwq, dwk, dwv, dwo, norms = call(
        backward_kernel, cfg, 3,
        in_vmem(14) + anywhere(3) + in_vmem(4),
        [
            ((rows, width), BF16),
            ((rows, width), BF16),
            ((width, half_width), F32),
            ((width, half_width), F32),
            ((width, half_width), F32),
            ((width, width), F32),
            ((8, width), F32),
        ],
        [
            vmem((3, width, half_width), BF16),
            vmem((rows, width), F32),
            vmem((rows, width), BF16),
            vmem((length, half_width), BF16),
            vmem((slots, width), BF16),
            vmem((length, PAIR), F32),
            vmem((length, PAIR), F32),
            vmem((length, half_width), BF16),
            vmem((length, half_width), BF16),
            vmem((length, half_width), BF16),
            vmem((length, width), F32),
            vmem((nb, half, width), BF16),
            vmem((nb, half, width), BF16),
            vmem((nb, half, width), BF16),
            vmem((rows, width), BF16),
            dma((3,)),
            dma((ne,)), dma((ne,)),
            dma((2 * seqs,)), dma((nb,)),
            dma, dma,
            dma((nb,)), dma((2 * seqs,)),
        ],
        "backward", 20 << 30,
    )(
        x, og, idx, h1, gate, back, y, o, q, k, v, a, lse, output_weight,
        query_weight, key_weight, value_weight, gain1, bias1, gain2, bias2,
    )

    expert_in_grad = lax.psum_scatter(dwin, "blk", scatter_dimension=1, tiled=True).astype(F32)
    expert_out_grad = lax.psum_scatter(dwout, "blk", scatter_dimension=0, tiled=True).astype(F32)
    core = lax.rem(lax.axis_index("exp"), 2)
    halves = jnp.stack([dwq, dwk, dwv]).astype(BF16)
    empty = jnp.zeros_like(halves)
    full = jnp.concatenate(
        [jnp.where(core == 0, halves, empty), jnp.where(core == 0, empty, halves)], axis=2
    )
    wide, small = lax.psum(
        (
            jnp.concatenate([full, dwo.astype(BF16)[None]]),
            jnp.concatenate([norms[:4], drouter, jnp.pad(mass[:1], ((0, 0), (0, width - experts)))]),
        ),
        ("blk", "exp"),
    )
    wide = wide.astype(F32)
    load_weight = (cnt[0, :experts] - cfg["mean_load"]) / cfg["mean_load"]
    balance = jnp.sum(load_weight * small[4 + experts, :experts]) / token_total
    return (
        out.reshape(seqs, span, width),
        balance,
        dx.reshape(seqs, span, width),
        wide[0],
        wide[1],
        wide[2],
        wide[3],
        small[4 : 4 + experts].T,
        expert_in_grad[None],
        expert_out_grad[None],
        small[0],
        small[1],
        small[2],
        small[3],
    )


def solution(mesh):
    return jax.shard_map(
        shards,
        mesh=mesh,
        in_specs=(
            P("exp", "blk", None),
            P("exp", "blk", None),
            P("blk", "exp", None, None),
            P(),
            P(),
            P(),
            P(),
            P(),
            P("exp", None, None),
            P("exp", None, None),
            P(),
            P(),
            P(),
            P(),
        ),
        out_specs=(
            P("exp", "blk", None),
            P(),
            P("exp", "blk", None),
            P(),
            P(),
            P(),
            P(),
            P(),
            P("exp", None, "blk"),
            P("exp", "blk", None),
            P(),
            P(),
            P(),
            P(),
        ),
        check_vma=False,
    )
```

time: 940 us -> 417 us (0.44); the launches traced: 926 us -> 416 us
  waiting for transfers between devices: 379 us -> 131 us
  Pallas kernels: 0 us -> 193 us
  local copies, waits for them, and re-layouts: 193 us -> 15.6 us
  matrix products: 169 us -> 0 us
  other arithmetic: 62.1 us -> 16.5 us
  blocking collectives: 87.7 us -> 42.6 us
  starting transfers between devices: 17.5 us -> 0.12 us
    pallas_call x0 -> x3, Pallas kernels: none -> 193 us  [the longest x1 76.4 us: shards(): call(expert_kernel, cfg, 2, in_vmem(9) + anywhere(2), [((rows, width), F3...]
    dot_general x28 -> x0, matrix products: 169 us -> none  [the longest x2 28.7 us: masked_scores(): jnp.einsum('sqhd,skhd->shqk', queries, key_rows, preferred_element_type=j...]
    scatter x2 -> x0, local copies, waits for them, and re-layouts: 139 us -> none  [fill_slots(): filled = jnp.zeros((expert_count, capacity, model_width), jnp.bfloat16).a...]
    reduce_scatter x3 -> x2, waiting for transfers between devices: 138 us -> 0.01 us  [the longest x1 0.01 us: shards(): lax.psum_scatter(dwout, 'blk', scatter_dimension=0, tiled=True).astype(F32)]
    all_gather x2 -> x0, waiting for transfers between devices: 83.4 us -> none  [the longest x1 46.3 us: shards(): piece_keys = lax.all_gather(key_rows, 'blk', axis=1, tiled=True)]
    psum x2 -> x1, blocking collectives: 87.7 us -> 42.6 us  [shards(): lax.psum((jnp.concatenate([full, dwo.astype(BF16)[None]]), jnp.concatenat...]
    convert_element_type x11 -> x1, other arithmetic: 29.6 us -> 3.15 us  [shards(): wide = wide.astype(F32)]
    reduce_sum x10 -> x1, other arithmetic: 22.2 us -> 1.29 us  [shards(): balance = jnp.sum(load_weight * small[4 + experts, :experts]) / token_total]
  transfers between devices with their start and end apart: 10 -> 3, of which waited for: 8 -> 1; matrix products, arithmetic and copies ran while one was open for 21% -> 3% of each run, Pallas kernels for 0% -> 0%
where the time goes in v1:
time: 417 us; the launch traced here: 416 us
  Pallas kernels  193 us (46%)
  waiting for transfers between devices  131 us (31%)
  blocking collectives  42.6 us (10%)
  between operations  17.4 us (4%)
  other arithmetic  16.5 us (4%)
  local copies, waits for them, and re-layouts  15.6 us (4%)
    psum x1, waiting for transfers between devices, shards(): lax.psum((jnp.concatenate([full, dwo.astype(BF16)[None]]), jnp.concatenat...  130 us
    pallas_call x1, Pallas kernels, shards(): call(expert_kernel, cfg, 2, in_vmem(9) + anywhere(2), [((rows, width), F3...  76.4 us
    pallas_call x1, Pallas kernels, shards(): call(backward_kernel, cfg, 3, in_vmem(14) + anywhere(3) + in_vmem(4), [((...  62.3 us
    pallas_call x1, Pallas kernels, shards(): call(attend_kernel, cfg, 1, in_vmem(5) + anywhere(3), [((length, half_wid...  54.3 us
    psum x1, blocking collectives, shards(): lax.psum((jnp.concatenate([full, dwo.astype(BF16)[None]]), jnp.concatenat...  42.6 us
  transfers between devices with their start and end apart: 3, of which 1 were waited for; matrix products, arithmetic and copies ran while one was open for 3% of the time, Pallas kernels for 0%

profile of v1, /device:TPU:0, one launch (start us, length us, event | category | flops | bytes accessed | tf_op | source)
XLA Modules:
  0.0 415.9 jit_solution(13047407699621441334)
XLA Ops:
  8.0 0.0 all-reduce.3.cloned.1.call-start
  8.1 1.3 reshape.69.gain.gain1
  9.3 1.3 reshape.70.bias.bias1
  10.6 1.3 reshape.71.gain.gain2
  11.9 1.3 reshape.72.bias.bias2
  13.1 1.5 copy.30.router
  14.7 1.5 copy.32.idx
  16.2 54.3 %attend.1 = (bf16[1024,384]{1,0:T(8,128)(2,1)}, bf16[1024,384]{1,0:T(8,128)(2,1)}, bf16[1024,384]{1,0:T(8,128)(2,1)}, bf16[1024,768]{1,0:T(8,128)(2,1)}, f32[8,1...) custom-call(bf16[512,768]{1,0:T(8,128)(2,1)} %bitcast.36, ...), custom_call_target="tpu_custom_call" | custom-call | flops 8589934592 | bytes 16777216 | tf_op jit(solution)/shard_map/attend/pallas_call | solution.py:641
  70.4 76.4 %experts.1 = (f32[512,768]{1,0:T(8,128)}, f32[512,1]{1,0:T(8,128)}, f32[8,8]{1,0:T(8,128)}, bf16[640,768]{1,0:T(8,128)(2,1)}, bf16[640,768]{1,0:T(8,128)(2,1)}, ...) custom-call(bf16[512,768]{1,0:T(8,128)(2,1)} %bitcast.37, ...), custom_call_target="tpu_custom_call" | custom-call | flops 21474836480 | bytes 16777216 | tf_op jit(solution)/shard_map/experts/pallas_call | solution.py:673
  146.8 62.3 %backward.1 = (bf16[512,768]{1,0:T(8,128)(2,1)}, bf16[512,768]{1,0:T(8,128)(2,1)}, f32[768,384]{1,0:T(8,128)}, f32[768,384]{1,0:T(8,128)}, f32[768,384]{1,0:T(8,...) custom-call(bf16[512,768]{1,0:T(8,128)(2,1)} %bitcast.38, bf16[512,768]{1,0:T(8,128)(2,1)} %bitcast.40, s32[512,1]{1,0:T(8,128)} %copy.32.idx, ...), custom_call_target="tpu_custom_call" | custom-call | flops 21474836480 | bytes 16777216 | tf_op jit(solution)/shard_map/backward/pallas_call | solution.py:705
  209.2 0.0 copy-start
  209.2 0.0 copy-start.1
  209.2 1.5 convert_bitcast_fusion.3
  210.7 1.8 convert_bitcast_fusion
  212.4 0.0 copy-done
  212.5 0.0 copy-done.1
  212.5 0.2 convert_bitcast_fusion.1
  212.6 0.5 broadcast_select_fusion.1
  213.1 2.3 pad_maximum_fusion
  215.5 0.0 all-reduce.3.cloned.1.call-update
  215.5 0.0 reduce-scatter.5.cloned.1.call-start
  215.6 0.5 reduce-scatter.5.cloned.1.call-update
  216.1 0.0 reduce-scatter.3.cloned.1.call-start
  216.1 0.0 copy-start.5
  216.1 0.0 copy-start.4
  216.1 0.5 reduce-scatter.3.cloned.1.call-update
  216.7 0.7 slice.41
  217.3 0.0 copy-done.5
  217.3 0.0 copy-done.4
  217.4 42.6 %psum.14 = f32[13,768]{1,0:T(8,128)S(1)} all-reduce(f32[13,768]{1,0:T(8,128)S(1)} %select_maximum_fusion), channel_id=1, replica_groups=mesh['blk'=4,'exp'=8] {'blk','exp'}, use_global_device_ids=true, to_apply=%region_0.0 | all-reduce | flops 9984 | bytes 79872 | tf_op jit(solution)/shard_map/psum | solution.py:753
  259.9 1.3 fusion
  261.9 0.6 slice_reduce_fusion
  262.5 0.6 slice_bitcast_fusion.4
  263.1 129.6 %all-reduce.3.cloned.1.call-done = bf16[4,768,768]{2,1,0:T(8,128)(2,1)} async-done(((bf16[4,768,768]{2,1,0:T(8,128)(2,1)}), bf16[4,768,768]{2,1,0:T(8,128)(2,1)}) %all-reduce.3.cloned.1.call-update) | async-done | bytes 4718608 | tf_op jit(solution)/shard_map/psum | solution.py:753
  392.7 3.2 convert_element_type.12
  395.9 3.8 slice_bitcast_fusion
  399.7 0.0 reduce-scatter.5.cloned.1.call-done
  399.7 2.8 bitcast_convert_fusion
  402.6 0.0 copy-start.3
  402.6 0.0 copy-start.2
  402.6 0.0 reduce-scatter.3.cloned.1.call-done
  402.6 3.0 bitcast_convert_fusion.1
  405.5 0.0 copy-done.3
  405.6 0.9 copy.36
  406.4 0.0 copy-done.2
  406.4 0.9 copy.37
  (2 shorter events, 0.0 us)
Async XLA Ops:
  8.0 384.7 %all-reduce.3.cloned.1.call-start = ((), (), s32[]{:S(2)}) async-start(), calls=%async_computation.2 | async-start | bytes 9437184 | tf_op jit(solution)/shard_map/psum | solution.py:753
  209.2 3.3 copy-start
  209.2 3.3 copy-start.1
  215.5 184.2 %reduce-scatter.5.cloned.1.call-start = ((), (), s32[]{:S(2)}) async-start(), calls=%async_computation.4 | async-start | bytes 5898240 | tf_op jit(solution)/shard_map/reduce_scatter | solution.py:746
  216.1 186.5 %reduce-scatter.3.cloned.1.call-start = ((), (), s32[]{:S(2)}) async-start(), calls=%async_computation.3 | async-start | bytes 5898240 | tf_op jit(solution)/shard_map/reduce_scatter | solution.py:745
  216.1 1.2 copy-start.5
  216.1 1.2 copy-start.4
  402.6 3.0 copy-start.3
  402.6 3.9 copy-start.2
Sparse Core Ops, SparseCore 0:
  215.6 177.0 all-reduce.2
Sparse Core Ops, SparseCore 1:
  219.2 64.2 reduce-scatter.4
  286.7 58.4 reduce-scatter.2

commit v2 on v1

--- a/solution.py
+++ b/solution.py
@@ -16,7 +16,7 @@
 FF_COLS = 256
 MESH = pl.DeviceIdType.MESH
 BF16, F32 = jnp.bfloat16, jnp.float32
-VMEM_BYTES = 62 << 20
+VMEM_BYTES = 63 << 20
 NT = (((1,), (1,)), ((), ()))
 TN = (((0,), (0,)), ((), ()))
 
@@ -344,124 +344,417 @@
     return value, slope
 
 
-def expert_kernel(
-    cfg,
-    x, o, wo, router, gain, bias, idx, dh, cnt, win_hbm, wout_hbm,
-    h1, gate, mass, back, y, dwin, dwout, drouter,
-    win, wout, n2, disp, took, g, du, made, dn,
-    wsem, ns, nr, rs, rr,
-):
+class Refs:
+    def __init__(self, names, refs):
+        self.__dict__.update(zip(names, refs, strict=True))
+
+
+class ExpertSums:
+    def __init__(self, me, r):
+        self.me, self.r = me, r
+        self.hi, self.lo = lax.div(me.b, 2), lax.rem(me.b, 2)
+        self.other = 1 - self.lo
+        self.count = me.nb // 2
+        self.size = me.ff // me.nb
+
+    def turn(self, step):
+        return lax.rem(self.hi + step, self.count)
+
+    def span(self, hi, lo):
+        return pl.ds(pl.multiple_of((2 * hi + lo) * self.size, 128), self.size)
+
+    def in_first(self, hi):
+        r = self.r
+        there = (2 * self.hi + self.other, self.me.e)
+        return remote(
+            r.win.at[:, self.span(hi, self.other)], r.in1.at[hi], r.in1s.at[hi], r.in1r.at[hi], there
+        )
+
+    def in_second(self, step):
+        r, hi = self.r, self.turn(step)
+        return remote(
+            r.win.at[:, self.span(hi, self.lo)],
+            r.in2.at[step - 1],
+            r.in2s.at[step - 1],
+            r.in2r.at[step - 1],
+            (2 * hi + self.lo, self.me.e),
+        )
+
+    def out_first(self, step, lo):
+        r, hi = self.r, self.turn(step)
+        return remote(
+            r.wout.at[self.span(hi, lo)],
+            r.out1.at[step - 1, lo],
+            r.out1s.at[step - 1, lo],
+            r.out1r.at[step - 1, lo],
+            (2 * hi + self.lo, self.me.e),
+        )
+
+    def out_second(self):
+        r = self.r
+        return remote(
+            r.wout.at[self.span(self.hi, self.other)],
+            r.out2,
+            r.out2s,
+            r.out2r,
+            (2 * self.hi + self.other, self.me.e),
+        )
+
+    def after_part(self, n):
+        step = lax.div(n, 2) + 1
+        lo = lax.rem(self.other + n, 2)
+
+        @pl.when(lax.rem(n, 2) == 0)
+        def _():
+            self.in_first(self.turn(step)).start()
+
+        @pl.when(step < self.count)
+        def _():
+            self.out_first(step, lo).start()
+
+    def second(self):
+        r = self.r
+        for step in range(1, self.count):
+            hi = self.turn(step)
+            landed(r.in1.at[hi], r.in1r.at[hi])
+            here = self.span(hi, self.lo)
+
+            def in_rows(n, _, hi=hi, here=here):
+                rows = split_rows(n * ROWS, ROWS)
+                r.win[rows, here] = (
+                    r.win[rows, here].astype(F32) + r.in1[hi, rows, :].astype(F32)
+                ).astype(BF16)
+
+            lax.fori_loop(0, self.me.width // ROWS, in_rows, None)
+            self.in_second(step).start()
+        for step in range(1, self.count):
+            landed(r.out1.at[step - 1, self.other], r.out1r.at[step - 1, self.other])
+        base = (2 * self.hi + self.other) * self.size
+
+        def out_rows(n, _):
+            here, rows = split_rows(base + n * ROWS, ROWS), split_rows(n * ROWS, ROWS)
+            total = r.wout[here, :].astype(F32)
+            for step in range(1, self.count):
+                total += r.out1[step - 1, self.other, rows, :].astype(F32)
+            r.wout[here, :] = total.astype(BF16)
+
+        lax.fori_loop(0, self.size // ROWS, out_rows, None)
+        self.out_second().start()
+
+    def total_in(self, into):
+        r = self.r
+        landed(r.in1.at[self.hi], r.in1r.at[self.hi])
+        for step in range(1, self.count):
+            landed(r.in2.at[step - 1], r.in2r.at[step - 1])
+
+        def in_rows(n, _):
+            rows = split_rows(n * ROWS, ROWS)
+            total = r.win[rows, self.span(self.hi, self.lo)].astype(F32)
+            total += r.in1[self.hi, rows, :].astype(F32)
+            for step in range(1, self.count):
+                total += r.in2[step - 1, rows, :].astype(F32)
+            into[rows, 0 : self.size] = total
+
+        lax.fori_loop(0, self.me.width // ROWS, in_rows, None)
+
+    def total_out(self, into):
+        r = self.r
+        for step in range(1, self.count):
+            landed(r.out1.at[step - 1, self.lo], r.out1r.at[step - 1, self.lo])
+        landed(r.out2, r.out2r)
+        base = (2 * self.hi + self.lo) * self.size
+
+        def out_rows(n, _):
+            rows = split_rows(n * ROWS, ROWS)
+            total = r.wout[split_rows(base + n * ROWS, ROWS), :].astype(F32)
+            for step in range(1, self.count):
+                total += r.out1[step - 1, self.lo, rows, :].astype(F32)
+            into[rows, :] = total + r.out2[rows, :].astype(F32)
+
+        lax.fori_loop(0, self.size // ROWS, out_rows, None)
+
+    def sent(self):
+        for step in range(1, self.count + 1):
+            self.in_first(self.turn(step)).wait_send()
+            if step < self.count:
+                self.in_second(step).wait_send()
+                for lo in range(2):
+                    self.out_first(step, lo).wait_send()
+        self.out_second().wait_send()
+
+
+class SharedSum:
+    def __init__(self, me, r, p, blk_first):
+        self.me, self.r, self.p = me, r, p
+        z = lax.div(me.e, 2)
+        nz = me.ne // 2
+        blk = (me.b, me.nb, lambda t: (t, me.e))
+        along_z = (z, nz, lambda t: (me.b, 2 * t + me.c))
+        self.first, self.second = (blk, along_z) if blk_first else (along_z, blk)
+        self.outer = me.width // self.first[1]
+        self.inner = self.outer // self.second[1]
+
+    def outer_rows(self, t):
+        return split_rows(t * self.outer, self.outer)
+
+    def inner_rows(self, t, s):
+        return split_rows(t * self.outer + s * self.inner, self.inner)
+
+    def view(self, rows, core):
+        me, r, p = self.me, self.r, self.p
+        if p < 3:
+            return r.shared.at[
+                pl.ds(0, 3), rows, pl.ds(pl.multiple_of(core * me.half_width + p * PAIR, PAIR), PAIR)
+            ]
+        return r.shared.at[
+            3, rows, pl.ds(pl.multiple_of(core * me.half_width, PAIR), me.half_width)
+        ]
+
+    def peer(self, axis, k):
+        return lax.rem(axis[0] + k, axis[1])
+
+    def source(self, axis, k):
+        return lax.rem(axis[0] + axis[1] - k, axis[1])
+
+    def move1(self, k):
+        r, p = self.r, self.p
+        t = self.peer(self.first, k)
+        return remote(
+            r.part.at[p, self.outer_rows(t)],
+            r.got1.at[p, k, pl.ds(0, self.outer)],
+            r.s1.at[p, k],
+            r.r1.at[p, k],
+            self.first[2](t),
+        )
+
+    def move2(self, k):
+        r, p = self.r, self.p
+        t = self.peer(self.second, k)
+        return remote(
+            r.got1.at[p, 0, split_rows(t * self.inner, self.inner)],
+            r.got2.at[p, k],
+            r.s2.at[p, k],
+            r.r2.at[p, k],
+            self.second[2](t),
+        )
+
+    def move3(self, k):
+        r, p = self.r, self.p
+        here = self.view(self.inner_rows(self.first[0], self.second[0]), self.me.c)
+        return remote(
+            here, here, r.s3.at[p, k], r.r3.at[p, k], self.second[2](self.peer(self.second, k))
+        )
+
+    def move4(self, k):
+        r, p = self.r, self.p
+        here = self.view(self.outer_rows(self.first[0]), self.me.c)
+        return remote(
+            here, here, r.s4.at[p, k], r.r4.at[p, k], self.first[2](self.peer(self.first, k))
+        )
+
+    def move5(self):
+        r, p = self.r, self.p
+        here = self.view(pl.ds(0, self.me.width), self.me.c)
+        return remote(here, here, r.s5.at[p], r.r5.at[p], (self.me.b, self.me.sibling))
+
+    def stage1(self):
+        for k in range(1, self.first[1]):
+            self.move1(k).start()
+
+    def stage2(self):
+        r, p = self.r, self.p
+        total = r.part[p, self.outer_rows(self.first[0])].astype(F32)
+        for k in range(1, self.first[1]):
+            here = r.got1.at[p, k, pl.ds(0, self.outer)]
+            landed(here, r.r1.at[p, k])
+            total += here[...].astype(F32)
+        r.got1[p, 0, 0 : self.outer, :] = total.astype(BF16)
+        for k in range(1, self.second[1]):
+            self.move2(k).start()
+
+    def stage3(self):
+        r, p = self.r, self.p
+        total = r.got1[p, 0, split_rows(self.second[0] * self.inner, self.inner)].astype(F32)
+        for k in range(1, self.second[1]):
+            landed(r.got2.at[p, k], r.r2.at[p, k])
+            total += r.got2[p, k].astype(F32)
+        total = total.astype(BF16)
+        here = self.view(self.inner_rows(self.first[0], self.second[0]), self.me.c)
+        if p < 3:
+            for j in range(3):
+                here[j] = total[:, j * PAIR : (j + 1) * PAIR]
+        else:
+            here[...] = total
+        for k in range(1, self.second[1]):
+            self.move3(k).start()
+
+    def stage4(self):
+        for k in range(1, self.second[1]):
+            rows = self.inner_rows(self.first[0], self.source(self.second, k))
+            landed(self.view(rows, self.me.c), self.r.r3.at[self.p, k])
+        for k in range(1, self.first[1]):
+            self.move4(k).start()
+
+    def stage5(self):
+        for k in range(1, self.first[1]):
+            rows = self.outer_rows(self.source(self.first, k))
+            landed(self.view(rows, self.me.c), self.r.r4.at[self.p, k])
+        self.move5().start()
+
+    def end(self):
+        landed(self.view(pl.ds(0, self.me.width), 1 - self.me.c), self.r.r5.at[self.p])
+        for k in range(1, self.first[1]):
+            self.move1(k).wait_send()
+            self.move4(k).wait_send()
+        for k in range(1, self.second[1]):
+            self.move2(k).wait_send()
+            self.move3(k).wait_send()
+        self.move5().wait_send()
+
+
+def layer_kernel(cfg, names, *refs):
     me = Place(cfg)
-    loads = [
-        pltpu.make_async_copy(win_hbm, win, wsem.at[0]),
-        pltpu.make_async_copy(wout_hbm, wout, wsem.at[1]),
+    r = Refs(names, refs)
+    r.ysend, r.yback = r.g, r.du
+    r.swap, r.da_in = r.took.at[pl.ds(0, me.rows)], r.back.at[pl.ds(0, me.rows)]
+    half = me.span // 2
+    pairs = me.half_width // PAIR
+    weight_loads = [
+        pltpu.make_async_copy(r.win_hbm, r.win, r.wsem.at[0]),
+        pltpu.make_async_copy(r.wout_hbm, r.wout, r.wsem.at[1]),
     ]
-    for load in loads:
+    late = [
+        pltpu.make_async_copy(src, dst, r.lsem.at[n])
+        for n, (src, dst) in enumerate(
+            (
+                (r.og_hbm, r.og),
+                (r.q_hbm, r.q),
+                (r.k_hbm, r.k),
+                (r.v_hbm, r.v),
+                (r.a_hbm, r.a),
+                (r.lse_hbm, r.lse),
+            )
+        )
+    ]
+    for p in range(pairs):
+        for j, matrix in enumerate((r.wq_hbm, r.wk_hbm, r.wv_hbm)):
+            src = matrix.at[:, pl.ds(pl.multiple_of(me.c * me.half_width + p * PAIR, PAIR), PAIR)]
+            late.append(
+                pltpu.make_async_copy(
+                    src, r.w.at[p, :, pl.ds(j * PAIR, PAIR)], r.lsem.at[6 + 3 * p + j]
+                )
+            )
+    for load in weight_loads + late:
         load.start()
     me.greet()
+
     expert_lane = iota((ROWS, me.experts), 1)
-    mass[...] = jnp.zeros_like(mass)
-
-    def token_rows(r, _):
-        here = split_rows(r * ROWS, ROWS)
-        hidden = x[here, :].astype(F32) + dot(o[here, :], wo[...])
-        h1[here, :] = hidden
+    r.sums[...] = jnp.zeros_like(r.sums)
+    r.mass[...] = jnp.zeros_like(r.mass)
+
+    def token_rows(n, _):
+        here = split_rows(n * ROWS, ROWS)
+        hidden = r.x[here, :].astype(F32) + dot(r.o[here, :], r.wo[...])
+        r.h1[here, :] = hidden
         hat, _ = normalize(hidden)
-        normed = (hat * gain[...] + bias[...]).astype(BF16)
-        n2[here, :] = normed
-        logits = dot(normed, router[...])
-        hot = idx[here, :] == expert_lane
+        normed = (hat * r.gain2[...] + r.bias2[...]).astype(BF16)
+        r.mail[here, :] = normed
+        logits = dot(normed, r.router[...])
+        hot = r.idx[here, :] == expert_lane
         value = jax.nn.sigmoid(jnp.sum(jnp.where(hot, logits, 0.0), axis=1, keepdims=True))
-        gate[here, :] = value
-        mass[...] += jnp.broadcast_to(
-            jnp.sum(jnp.where(hot, value, 0.0), axis=0, keepdims=True), mass.shape
-        )
+        r.gate[here, :] = value
+        r.mass[...] += jnp.sum(jnp.where(hot, value, 0.0), axis=0, keepdims=True)
 
     lax.fori_loop(0, me.rows // ROWS, token_rows, None)
-    slot, _ = token_slots(me, idx[...])
-    disp[...] = dot(slots_by_token(me, slot), n2[...]).astype(BF16)
-    exchange_start(me, disp, took, ns, nr, me.cap)
-    for load in loads:
+    slot, _ = token_slots(me, r.idx[...])
+    r.disp[...] = dot(slots_by_token(me, slot), r.mail[...]).astype(BF16)
+    exchange_start(me, r.disp, r.took, r.ns, r.nr, me.cap)
+    for load in weight_loads:
         load.wait()
-    exchange_wait(me, disp, took, ns, nr, me.cap)
-    exchange_sent(me, disp, took, ns, nr, me.cap)
+    exchange_wait(me, r.disp, r.took, r.ns, r.nr, me.cap)
+    exchange_sent(me, r.disp, r.took, r.ns, r.nr, me.cap)
 
     slots = me.experts * me.cap
     lanes = iota((slots, me.experts), 1)
-    logits = jnp.sum(jnp.where(lanes == me.e, dot(took[...], router[...]), 0.0), axis=1, keepdims=True)
+    logits = jnp.sum(
+        jnp.where(lanes == me.e, dot(r.took[...], r.router[...]), 0.0), axis=1, keepdims=True
+    )
     value = jax.nn.sigmoid(logits)
-    disp[...] = (value * dh[...].astype(F32)).astype(BF16)
-
-    def hidden_columns(f, _):
-        here = split_rows(f * FF_COLS, FF_COLS)
-        act, slope = gelu_parts(dot(took[...], win[:, here]))
-        g[:, here] = act.astype(BF16)
-        du[:, here] = (dot(disp[...], wout[here, :], NT) * slope).astype(BF16)
-
-    lax.fori_loop(0, me.ff // FF_COLS, hidden_columns, None)
-
-    def model_columns(f, _):
-        here = split_rows(f * FF_COLS, FF_COLS)
-        y[:, here] = dot(g[...], wout[:, here]).astype(BF16)
-        made[:, here] = dot(du[...], win[here, :], NT)
-
-    lax.fori_loop(0, me.width // FF_COLS, model_columns, None)
-
-    load_lane = iota(cnt.shape, 1)
-    load = jnp.sum(jnp.where(load_lane == me.e, cnt[...], 0.0), axis=1, keepdims=True)[0:1, :]
+    r.disp[...] = (value * r.dh[...].astype(F32)).astype(BF16)
+    r.yf[0:slots, :] = jnp.zeros((slots, me.width), F32)
+    r.made[...] = jnp.zeros_like(r.made)
+    sums = ExpertSums(me, r)
+    slot_rows = slots // 2
+
+    def expert_part(n, _):
+        hi, lo = sums.turn(lax.div(n, 2) + 1), lax.rem(sums.other + n, 2)
+        base = (2 * hi + lo) * sums.size
+
+        def hidden_columns(f, _):
+            here = pl.ds(pl.multiple_of(base + f * sums.tile, 128), sums.tile)
+            there = pl.ds(pl.multiple_of(f * sums.tile, 128), sums.tile)
+
+            def hidden_rows(n, _):
+                rows = split_rows(n * slot_rows, slot_rows)
+                act, slope = gelu_parts(dot(r.took[rows, :], r.win[:, here]))
+                r.g[rows, there] = act.astype(BF16)
+                r.du[rows, there] = (dot(r.disp[rows, :], r.wout[here, :], NT) * slope).astype(BF16)
+
+            lax.fori_loop(0, slots // slot_rows, hidden_rows, None)
+
+        lax.fori_loop(0, sums.size // sums.tile, hidden_columns, None)
+        part = sums.span(hi, lo)
+
+        def model_columns(f, _):
+            here = split_rows(f * FF_COLS, FF_COLS)
+            r.yf[0:slots, here] += dot(r.g[:, 0 : sums.size], r.wout[part, here])
+            r.made[0:slots, here] += dot(r.du[:, 0 : sums.size], r.win[here, part], NT)
+
+        lax.fori_loop(0, me.width // FF_COLS, model_columns, None)
+
+        def weight_columns(f, _):
+            here = pl.ds(pl.multiple_of(base + f * sums.tile, 128), sums.tile)
+            there = pl.ds(pl.multiple_of(f * sums.tile, 128), sums.tile)
+            r.win[:, here] = dot(r.took[...], r.du[:, there], TN).astype(BF16)
+            r.wout[here, :] = dot(r.g[:, there], r.disp[...], TN).astype(BF16)
+
+        lax.fori_loop(0, sums.size // sums.tile, weight_columns, None)
+        sums.after_part(n)
+
+    sums.tile = min(FF_COLS, sums.size) if sums.size % FF_COLS == 0 else PAIR
+    lax.fori_loop(0, me.nb, expert_part, None)
+
+    load_lane = iota(r.cnt.shape, 1)
+    load = jnp.sum(jnp.where(load_lane == me.e, r.cnt[...], 0.0), axis=1, keepdims=True)[0:1, :]
     weight = (load - me.mean_load) / me.mean_load
+    r.ysend[...] = r.yf[0:slots, :].astype(BF16)
     dgate = (
-        jnp.sum(dh[...].astype(F32) * y[...].astype(F32), axis=1, keepdims=True)
+        jnp.sum(r.dh[...].astype(F32) * r.ysend[...].astype(F32), axis=1, keepdims=True)
         + weight / me.tokens
     )
     dlogits = jnp.where(lanes == me.e, dgate * value * (1.0 - value), 0.0).astype(BF16)
-    dn[...] = (made[...] + dot(dlogits, router[...], NT)).astype(BF16)
-    exchange_start(me, dn, back, rs, rr, me.cap)
-    drouter[...] = dot(dlogits, took[...], TN)
-
-    def weight_columns(f, _):
-        here = split_rows(f * FF_COLS, FF_COLS)
-        dwin[:, here] = dot(took[...], du[:, here], TN).astype(BF16)
-        dwout[here, :] = dot(g[:, here], disp[...], TN).astype(BF16)
-
-    lax.fori_loop(0, me.ff // FF_COLS, weight_columns, None)
-    exchange_wait(me, dn, back, rs, rr, me.cap)
-    exchange_sent(me, dn, back, rs, rr, me.cap)
-
-
-def backward_kernel(
-    cfg,
-    x, og, idx, h1, gate, back, y, o, q, k, v, a, lse, wo, wq, wk, wv,
-    gain1, bias1, gain2, bias2,
-    out, dx, dwq, dwk, dwv, dwo, norms,
-    w, dh1, do_send, do, yback, dk_sum, dv_sum, dq, dk, dv, da, swap_send, swap, da_send, da_in,
-    wsem, ys, yr, os, orr, ss, sr, fs, fr,
-):
-    me = Place(cfg)
-    half = me.span // 2
-    columns = pl.ds(pl.multiple_of(me.c * me.half_width, 128), me.half_width)
-    loads = [
-        pltpu.make_async_copy(m.at[:, columns], w.at[j], wsem.at[j])
-        for j, m in enumerate((wq, wk, wv))
-    ]
-    for load in loads:
-        load.start()
-    me.greet()
-    exchange_start(me, y, yback, ys, yr, me.cap)
-    slot, _ = token_slots(me, idx[...])
+    r.disp[...] = (r.made[0:slots, :] + dot(dlogits, r.router[...], NT)).astype(BF16)
+    exchange_start(me, r.disp, r.back, r.rs, r.rr, me.cap)
+    r.sums[4 : 4 + me.experts, :] = dot(dlogits, r.took[...], TN)
+    r.sums[4 + me.experts : 5 + me.experts, 0 : me.experts] = r.mass[...]
+    sums.second()
+    exchange_wait(me, r.disp, r.back, r.rs, r.rr, me.cap)
+    exchange_start(me, r.ysend, r.yback, r.ys, r.yr, me.cap)
+
+    for load in late:
+        load.wait()
     takes = tokens_by_slot(me, slot)
-    norms[...] = jnp.zeros_like(norms)
-    da[0 : me.rows, :] = dot(takes, back[...])
-
-    def norm_rows(r, _):
-        here = split_rows(r * ROWS, ROWS)
-        grad = da[here, :]
-        hat, inverse = normalize(h1[here, :])
-        norms[2:3, :] += jnp.sum(grad * hat, axis=0, keepdims=True)
-        norms[3:4, :] += jnp.sum(grad, axis=0, keepdims=True)
-        total = og[here, :].astype(F32) + norm_back(hat, inverse, gain2[...], grad)
-        dh1[here, :] = total
-        do_send[here, :] = dot(total.astype(BF16), wo[...], NT).astype(BF16)
+    r.made[0 : me.rows, :] = dot(takes, r.back[...])
+
+    def norm_rows(n, _):
+        here = split_rows(n * ROWS, ROWS)
+        grad = r.made[here, :]
+        hat, inverse = normalize(r.h1[here, :])
+        r.sums[2:3, :] += jnp.sum(grad * hat, axis=0, keepdims=True)
+        r.sums[3:4, :] += jnp.sum(grad, axis=0, keepdims=True)
+        total = r.og[here, :].astype(F32) + norm_back(hat, inverse, r.gain2[...], grad)
+        r.dh1[here, :] = total
+        r.mail[here, :] = dot(total.astype(BF16), r.wo[...], NT).astype(BF16)
 
     lax.fori_loop(0, me.rows // ROWS, norm_rows, None)
 
@@ -469,111 +762,212 @@
         for s in range(me.seqs):
             for h in range(2):
                 yield (
-                    do_send.at[
+                    r.mail.at[
                         pl.ds(s * me.span, me.span), pl.ds(h * me.half_width, me.half_width)
                     ],
-                    do.at[split_rows(me.b * me.span, me.span)],
-                    os.at[2 * s + h],
-                    orr.at[me.b],
+                    r.do.at[split_rows(me.b * me.span, me.span)],
+                    r.os.at[2 * s + h],
+                    r.orr.at[me.b],
                     (me.c * me.seqs + s, me.pair + h),
                 )
 
     for move in o_moves():
         push(me, *move)
-    dwo[...] = dot(o[...], dh1[...].astype(BF16), TN)
+
+    def output_columns(core):
+        cols = pl.ds(pl.multiple_of(core * me.half_width, PAIR), me.half_width)
+        return dot(r.o[...], r.dh1[:, cols].astype(BF16), TN)
+
+    r.part[0] = output_columns(1 - me.c).astype(BF16)
+    o_swap = remote(r.part.at[0], r.ogot, r.oss, r.osr, (me.b, me.sibling))
+    o_swap.start()
+    own_columns = output_columns(me.c)
+    o_swap.wait()
+    r.part[3] = (own_columns + r.ogot[...].astype(F32)).astype(BF16)
+    pieces = [SharedSum(me, r, p, blk_first=p in (1, 2)) for p in range(4)] if me.sum_here else []
+    if pieces:
+        pieces[3].stage1()
+
+    r.made[...] = jnp.zeros_like(r.made)
     for j in range(me.nb):
-        landed(do.at[pl.ds(j * me.span, me.span)], orr.at[j])
-
+        landed(r.do.at[pl.ds(j * me.span, me.span)], r.orr.at[j])
     first, second = head_masks()
     blocks = me.length // QUERY_ROWS
     visible = iota((QUERY_ROWS, QUERY_ROWS), 0) <= iota((QUERY_ROWS, QUERY_ROWS), 1)
 
-    def pair_of_heads(p, _):
-        lanes = split_rows(p * PAIR, PAIR)
-        dk_sum[...] = jnp.zeros_like(dk_sum)
-        dv_sum[...] = jnp.zeros_like(dv_sum)
+    def pair_of_heads(n, _):
+        lanes = split_rows(n * PAIR, PAIR)
+        r.dk_sum[...] = jnp.zeros_like(r.dk_sum)
+        r.dv_sum[...] = jnp.zeros_like(r.dv_sum)
         for i in range(blocks):
             here = pl.ds(i * QUERY_ROWS, QUERY_ROWS)
-            queries, grads = q[here, lanes], do[here, lanes]
+            queries, grads = r.q[here, lanes], r.do[here, lanes]
             parts = [here]
             if i:
                 parts.append(pl.ds(0, i * QUERY_ROWS))
             dq_block = jnp.zeros((QUERY_ROWS, PAIR), F32)
             for h, mask in enumerate((first, second)):
                 qm, gm = queries * mask, grads * mask
-                sums = lse[pl.ds(2 * p + h, 1), here]
-                scores = [dot(k[part, lanes], qm, NT) for part in parts]
-                powers = [jnp.exp(s - sums) for s in scores]
+                log_sums = r.lse[pl.ds(2 * n + h, 1), here]
+                scores = [dot(r.k[part, lanes], qm, NT) for part in parts]
+                powers = [jnp.exp(s - log_sums) for s in scores]
                 powers[0] = jnp.where(visible, powers[0], 0.0)
                 weighted = [
-                    s * dot(v[part, lanes], gm, NT) for s, part in zip(powers, parts)
+                    s * dot(r.v[part, lanes], gm, NT) for s, part in zip(powers, parts)
                 ]
                 delta = sum(jnp.sum(t, axis=0, keepdims=True) for t in weighted)
                 for s, t, part in zip(powers, weighted, parts):
                     ds = (t - s * delta).astype(BF16)
-                    dv_sum[part, :] += dot(s.astype(BF16), gm)
-                    dk_sum[part, :] += dot(ds, qm)
-                    dq_block += dot(ds, k[part, lanes] * mask, TN)
-            dq[here, lanes] = (dq_block * SCALE).astype(BF16)
-        dk[:, lanes] = dk_sum[...].astype(BF16)
-        dv[:, lanes] = dv_sum[...].astype(BF16)
-
-    lax.fori_loop(0, me.half_width // PAIR, pair_of_heads, None)
-
-    for load in loads:
-        load.wait()
-    da[...] = dot(dq[...], w[0], NT) + dot(dk[...], w[1], NT) + dot(dv[...], w[2], NT)
-    for j in range(me.nb):
-        swap_send[j] = da[split_rows(j * me.span + (1 - me.c) * half, half), :].astype(BF16)
-    swap_move = remote(swap_send, swap, ss, sr, (me.b, me.sibling))
-    swap_move.start()
-    dwq[...] = dot(a[...], dq[...], TN)
-    swap_move.wait()
-    source = me.pair + lax.div(me.b, me.seqs)
-
-    def da_move(j):
-        return (
-            da_send.at[j],
-            da_in.at[split_rows(lax.rem(me.b, me.seqs) * me.span + me.c * half, half)],
-            fs.at[j],
-            fr.at[2 * lax.rem(me.b, me.seqs) + me.c],
-            (j, source),
-        )
-
-    for j in range(me.nb):
-        mine = da[split_rows(j * me.span + me.c * half, half), :]
-        da_send[j] = (mine + swap[j].astype(F32)).astype(BF16)
-        push(me, *da_move(j))
-    dwk[...] = dot(a[...], dk[...], TN)
-    dwv[...] = dot(a[...], dv[...], TN)
-
-    exchange_wait(me, y, yback, ys, yr, me.cap)
-    exchange_sent(me, y, yback, ys, yr, me.cap)
-    da[0 : me.rows, :] = dot(takes, yback[...])
-
-    def out_rows(r, _):
-        here = split_rows(r * ROWS, ROWS)
-        out[here, :] = (h1[here, :] + gate[here, :] * da[here, :]).astype(BF16)
-
-    lax.fori_loop(0, me.rows // ROWS, out_rows, None)
-
-    for s in range(me.seqs):
-        for h in range(2):
-            landed(da_in.at[pl.ds(s * me.span + h * half, half)], fr.at[2 * s + h])
-
-    def token_rows(r, _):
-        here = split_rows(r * ROWS, ROWS)
-        grad = da_in[here, :].astype(F32)
-        hat, inverse = normalize(x[here, :].astype(F32))
-        norms[0:1, :] += jnp.sum(grad * hat, axis=0, keepdims=True)
-        norms[1:2, :] += jnp.sum(grad, axis=0, keepdims=True)
-        dx[here, :] = (dh1[here, :] + norm_back(hat, inverse, gain1[...], grad)).astype(BF16)
-
-    lax.fori_loop(0, me.rows // ROWS, token_rows, None)
+                    r.dv_sum[part, :] += dot(s.astype(BF16), gm)
+                    r.dk_sum[part, :] += dot(ds, qm)
+                    dq_block += dot(ds, r.k[part, lanes] * mask, TN)
+            r.dqkv[here, 0:PAIR] = (dq_block * SCALE).astype(BF16)
+        r.dqkv[:, PAIR : 2 * PAIR] = r.dk_sum[...].astype(BF16)
+        r.dqkv[:, 2 * PAIR : 3 * PAIR] = r.dv_sum[...].astype(BF16)
+        r.part[n] = dot(r.a[...], r.dqkv[...], TN).astype(BF16)
+
+        def normed_columns(f, _):
+            cols = split_rows(f * FF_COLS, FF_COLS)
+            r.made[:, cols] += dot(r.dqkv[...], r.w[n, cols, :], NT)
+
+        lax.fori_loop(0, me.width // FF_COLS, normed_columns, None)
+        if pieces:
+
+            @pl.when(n == 0)
+            def _():
+                pieces[0].stage1()
+                pieces[3].stage2()
+
+            @pl.when(n == 1)
+            def _():
+                pieces[1].stage1()
+                pieces[0].stage2()
+                pieces[3].stage3()
+
+            @pl.when(n == 2)
+            def _():
+                pieces[2].stage1()
+                pieces[1].stage2()
+                pieces[0].stage3()
+                pieces[3].stage4()
+
+    lax.fori_loop(0, pairs, pair_of_heads, None)
+
     for move in o_moves():
         push_done(me, *move)
     for j in range(me.nb):
+        theirs = split_rows(j * me.span + (1 - me.c) * half, half)
+        r.mail[pl.ds(j * half, half), :] = r.made[theirs, :].astype(BF16)
+    swap = remote(r.mail, r.swap, r.ss, r.sr, (me.b, me.sibling))
+    swap.start()
+    exchange_wait(me, r.ysend, r.yback, r.ys, r.yr, me.cap)
+    r.yf[0 : me.rows, :] = dot(takes, r.yback[...])
+
+    def out_rows(n, _):
+        here = split_rows(n * ROWS, ROWS)
+        r.out[here, :] = (r.h1[here, :] + r.gate[here, :] * r.yf[here, :]).astype(BF16)
+
+    lax.fori_loop(0, me.rows // ROWS, out_rows, None)
+    swap.wait()
+    home = me.pair + lax.div(me.b, me.seqs)
+
+    def da_move(j):
+        return (
+            r.mail.at[pl.ds(j * half, half)],
+            r.da_in.at[split_rows(lax.rem(me.b, me.seqs) * me.span + me.c * half, half)],
+            r.fs.at[j],
+            r.fr.at[2 * lax.rem(me.b, me.seqs) + me.c],
+            (j, home),
+        )
+
+    for j in range(me.nb):
+        mine = r.made[split_rows(j * me.span + me.c * half, half), :]
+        rows = pl.ds(j * half, half)
+        r.mail[rows, :] = (mine + r.swap[rows, :].astype(F32)).astype(BF16)
+        push(me, *da_move(j))
+    if pieces:
+        pieces[2].stage2()
+        pieces[1].stage3()
+        pieces[0].stage4()
+        pieces[3].stage5()
+    for s in range(me.seqs):
+        for h in range(2):
+            landed(r.da_in.at[pl.ds(s * me.span + h * half, half)], r.fr.at[2 * s + h])
+
+    def first_norm_rows(n, _):
+        here = split_rows(n * ROWS, ROWS)
+        grad = r.da_in[here, :].astype(F32)
+        hat, inverse = normalize(r.x[here, :].astype(F32))
+        r.sums[0:1, :] += jnp.sum(grad * hat, axis=0, keepdims=True)
+        r.sums[1:2, :] += jnp.sum(grad, axis=0, keepdims=True)
+        r.dx[here, :] = (r.dh1[here, :] + norm_back(hat, inverse, r.gain1[...], grad)).astype(
+            BF16
+        )
+
+    lax.fori_loop(0, me.rows // ROWS, first_norm_rows, None)
+
+    def sum_move(k):
+        return remote(
+            r.sums,
+            r.sum_exp.at[me.e],
+            r.es.at[k],
+            r.er.at[k],
+            (me.b, lax.rem(me.e + k, me.ne)),
+        )
+
+    lax.fori_loop(1, me.ne, lambda k, _: sum_move(k).start(), None)
+    r.sum_exp[me.e] = r.sums[...]
+    if pieces:
+        pieces[2].stage3()
+        pieces[1].stage4()
+        pieces[0].stage5()
+    lax.fori_loop(
+        1,
+        me.ne,
+        lambda k, _: landed(r.sum_exp.at[lax.rem(me.e + me.ne - k, me.ne)], r.er.at[k]),
+        None,
+    )
+    r.sum_blk[me.b] = jnp.sum(r.sum_exp[...], axis=0)
+
+    def blk_move(k):
+        return remote(
+            r.sum_blk.at[me.b],
+            r.sum_blk.at[me.b],
+            r.bs.at[k],
+            r.br.at[k],
+            (lax.rem(me.b + k, me.nb), me.e),
+        )
+
+    for k in range(1, me.nb):
+        blk_move(k).start()
+    if pieces:
+        pieces[2].stage4()
+        pieces[1].stage5()
+
+    size = sums.size
+    sums.total_in(r.made)
+    store_in = pltpu.make_async_copy(r.made.at[pl.ds(0, me.width), pl.ds(0, size)], r.dwin, r.wsem.at[0])
+    store_in.start()
+    sums.total_out(r.yf)
+    store_out = pltpu.make_async_copy(r.yf.at[pl.ds(0, size)], r.dwout, r.wsem.at[1])
+    store_out.start()
+    if pieces:
+        pieces[2].stage5()
+    for k in range(1, me.nb):
+        landed(r.sum_blk.at[lax.rem(me.b + me.nb - k, me.nb)], r.br.at[k])
+    r.small[...] = jnp.sum(r.sum_blk[...], axis=0)
+    lax.fori_loop(1, me.ne, lambda k, _: sum_move(k).wait_send(), None)
+    for k in range(1, me.nb):
+        blk_move(k).wait_send()
+    exchange_sent(me, r.disp, r.back, r.rs, r.rr, me.cap)
+    exchange_sent(me, r.ysend, r.yback, r.ys, r.yr, me.cap)
+    for j in range(me.nb):
         push_done(me, *da_move(j))
+    sums.sent()
+    for piece in pieces:
+        piece.end()
+    store_in.wait()
+    store_out.wait()
 
 
 def in_vmem(count):
@@ -670,94 +1064,139 @@
         ],
         "attend", 8 << 30,
     )(x, og, idx, gain1, bias1, query_weight, key_weight, value_weight)
-    h1, gate, mass, back, y, dwin, dwout, drouter = call(
-        expert_kernel, cfg, 2,
-        in_vmem(9) + anywhere(2),
-        [
-            ((rows, width), F32),
-            ((rows, 1), F32),
-            ((8, experts), F32),
-            ((slots, width), BF16),
-            ((slots, width), BF16),
-            ((width, ff), BF16),
-            ((ff, width), BF16),
-            ((experts, width), F32),
-        ],
-        [
-            vmem((width, ff), BF16),
-            vmem((ff, width), BF16),
-            vmem((rows, width), BF16),
-            vmem((slots, width), BF16),
-            vmem((slots, width), BF16),
-            vmem((slots, ff), BF16),
-            vmem((slots, ff), BF16),
-            vmem((slots, width), F32),
-            vmem((slots, width), BF16),
-            dma((2,)),
-            dma((ne,)), dma((ne,)),
-            dma((ne,)), dma((ne,)),
-        ],
-        "experts", 20 << 30,
-    )(
-        x, o, output_weight, router_weight, gain2, bias2, idx, dh, cnt,
-        expert_in.reshape(width, ff), expert_out.reshape(ff, width),
+    hi = nb // 2
+    size = ff // nb
+    sum_rows = -(-(5 + experts) // 8) * 8
+    cfg["sum_here"] = width % (8 * nb * ne) == 0
+    outer = width // min(nb, ne // 2)
+    inner = width // (nb * ne // 2)
+    inputs = (
+        ("x", x, True),
+        ("o", o, True),
+        ("wo", output_weight, True),
+        ("router", router_weight, True),
+        ("gain1", gain1, True),
+        ("gain2", gain2, True),
+        ("bias2", bias2, True),
+        ("idx", idx, True),
+        ("dh", dh, True),
+        ("cnt", cnt, True),
+        ("win_hbm", expert_in.reshape(width, ff), False),
+        ("wout_hbm", expert_out.reshape(ff, width), False),
+        ("og_hbm", og, False),
+        ("q_hbm", q, False),
+        ("k_hbm", k, False),
+        ("v_hbm", v, False),
+        ("a_hbm", a, False),
+        ("lse_hbm", lse, False),
+        ("wq_hbm", query_weight, False),
+        ("wk_hbm", key_weight, False),
+        ("wv_hbm", value_weight, False),
     )
-    out, dx, dwq, dwk, dwv, dwo, norms = call(
-        backward_kernel, cfg, 3,
-        in_vmem(14) + anywhere(3) + in_vmem(4),
-        [
-            ((rows, width), BF16),
-            ((rows, width), BF16),
-            ((width, half_width), F32),
-            ((width, half_width), F32),
-            ((width, half_width), F32),
-            ((width, width), F32),
-            ((8, width), F32),
-        ],
-        [
-            vmem((3, width, half_width), BF16),
-            vmem((rows, width), F32),
-            vmem((rows, width), BF16),
-            vmem((length, half_width), BF16),
-            vmem((slots, width), BF16),
-            vmem((length, PAIR), F32),
-            vmem((length, PAIR), F32),
-            vmem((length, half_width), BF16),
-            vmem((length, half_width), BF16),
-            vmem((length, half_width), BF16),
-            vmem((length, width), F32),
-            vmem((nb, half, width), BF16),
-            vmem((nb, half, width), BF16),
-            vmem((nb, half, width), BF16),
-            vmem((rows, width), BF16),
-            dma((3,)),
-            dma((ne,)), dma((ne,)),
-            dma((2 * seqs,)), dma((nb,)),
-            dma, dma,
-            dma((nb,)), dma((2 * seqs,)),
-        ],
-        "backward", 20 << 30,
-    )(
-        x, og, idx, h1, gate, back, y, o, q, k, v, a, lse, output_weight,
-        query_weight, key_weight, value_weight, gain1, bias1, gain2, bias2,
+    outputs = (
+        ("out", (rows, width), BF16, True),
+        ("dx", (rows, width), BF16, True),
+        (
+            ("shared", (4, width, width), BF16, True)
+            if cfg["sum_here"]
+            else ("part", (4, width, half_width), BF16, True)
+        ),
+        ("small", (sum_rows, width), F32, True),
+        ("dwin", (width, size), F32, False),
+        ("dwout", (size, width), F32, False),
     )
-
-    expert_in_grad = lax.psum_scatter(dwin, "blk", scatter_dimension=1, tiled=True).astype(F32)
-    expert_out_grad = lax.psum_scatter(dwout, "blk", scatter_dimension=0, tiled=True).astype(F32)
-    core = lax.rem(lax.axis_index("exp"), 2)
-    halves = jnp.stack([dwq, dwk, dwv]).astype(BF16)
-    empty = jnp.zeros_like(halves)
-    full = jnp.concatenate(
-        [jnp.where(core == 0, halves, empty), jnp.where(core == 0, empty, halves)], axis=2
+    scratch = dict(
+        win=vmem((width, ff), BF16),
+        wout=vmem((ff, width), BF16),
+        og=vmem((rows, width), BF16),
+        q=vmem((length, half_width), BF16),
+        k=vmem((length, half_width), BF16),
+        v=vmem((length, half_width), BF16),
+        a=vmem((length, width), BF16),
+        lse=vmem((8, length), F32),
+        w=vmem((half_width // PAIR, width, 3 * PAIR), BF16),
+        h1=vmem((rows, width), F32),
+        gate=vmem((rows, 1), F32),
+        mass=vmem((1, experts), F32),
+        mail=vmem((rows, width), BF16),
+        disp=vmem((slots, width), BF16),
+        took=vmem((slots, width), BF16),
+        g=vmem((slots, width), BF16),
+        du=vmem((slots, width), BF16),
+        yf=vmem((max(slots, size), width), F32),
+        made=vmem((length, width), F32),
+        back=vmem((slots, width), BF16),
+        dh1=vmem((rows, width), F32),
+        do=vmem((length, half_width), BF16),
+        ogot=vmem((width, half_width), BF16),
+        dk_sum=vmem((length, PAIR), F32),
+        dv_sum=vmem((length, PAIR), F32),
+        dqkv=vmem((length, 3 * PAIR), BF16),
+        sums=vmem((sum_rows, width), F32),
+        sum_exp=vmem((ne, sum_rows, width), F32),
+        sum_blk=vmem((nb, sum_rows, width), F32),
+        in1=vmem((hi, width, size), BF16),
+        in2=vmem((hi - 1, width, size), BF16),
+        out1=vmem((hi - 1, 2, size, width), BF16),
+        out2=vmem((size, width), BF16),
+        in1s=dma((hi,)), in1r=dma((hi,)),
+        in2s=dma((hi - 1,)), in2r=dma((hi - 1,)),
+        out1s=dma((hi - 1, 2)), out1r=dma((hi - 1, 2)),
+        out2s=dma, out2r=dma,
+        wsem=dma((2,)),
+        lsem=dma((6 + 3 * (half_width // PAIR),)),
+        ns=dma((ne,)), nr=dma((ne,)),
+        rs=dma((ne,)), rr=dma((ne,)),
+        ys=dma((ne,)), yr=dma((ne,)),
+        os=dma((2 * seqs,)), orr=dma((nb,)),
+        oss=dma, osr=dma,
+        ss=dma, sr=dma,
+        fs=dma((nb,)), fr=dma((2 * seqs,)),
+        es=dma((ne,)), er=dma((ne,)),
+        bs=dma((nb,)), br=dma((nb,)),
     )
-    wide, small = lax.psum(
-        (
-            jnp.concatenate([full, dwo.astype(BF16)[None]]),
-            jnp.concatenate([norms[:4], drouter, jnp.pad(mass[:1], ((0, 0), (0, width - experts)))]),
+    if cfg["sum_here"]:
+        scratch.update(
+            part=vmem((4, width, half_width), BF16),
+            got1=vmem((4, max(nb, ne // 2), outer, half_width), BF16),
+            got2=vmem((4, max(nb, ne // 2), inner, half_width), BF16),
+            s5=dma((4,)),
+            r5=dma((4,)),
+        )
+        for n in range(1, 5):
+            scratch[f"s{n}"] = dma((4, max(nb, ne // 2)))
+            scratch[f"r{n}"] = dma((4, max(nb, ne // 2)))
+    names = [n for n, _, _ in inputs] + [n for n, _, _, _ in outputs] + list(scratch)
+    out, dx, shared, small, dwin, dwout = pl.pallas_call(
+        functools.partial(layer_kernel, cfg, names),
+        out_shape=[jax.ShapeDtypeStruct(shape, kind) for _, shape, kind, _ in outputs],
+        in_specs=[(in_vmem if near else anywhere)(1)[0] for _, _, near in inputs],
+        out_specs=[(in_vmem if near else anywhere)(1)[0] for _, _, _, near in outputs],
+        scratch_shapes=list(scratch.values()),
+        compiler_params=pltpu.CompilerParams(
+            collective_id=2, has_side_effects=True, vmem_limit_bytes=VMEM_BYTES
         ),
-        ("blk", "exp"),
-    )
-    wide = wide.astype(F32)
+        cost_estimate=pl.CostEstimate(
+            flops=30 << 30, bytes_accessed=1 << 25, transcendentals=1 << 23
+        ),
+        name="layer",
+    )(*[value for _, value, _ in inputs])
+    if not cfg["sum_here"]:
+        own = shared.reshape(4, width, half_width)
+        own = jnp.concatenate(
+            [
+                own[:3].reshape(3, width, 3, PAIR).transpose(2, 1, 0, 3).reshape(3, width, half_width),
+                own[3:],
+            ]
+        )
+        core, empty = lax.rem(lax.axis_index("exp"), 2), jnp.zeros_like(own)
+        shared = lax.psum(
+            jnp.concatenate(
+                [jnp.where(core == 0, own, empty), jnp.where(core == 0, empty, own)], axis=2
+            ),
+            ("blk", "exp"),
+        )
+    wide = shared.astype(F32)
     load_weight = (cnt[0, :experts] - cfg["mean_load"]) / cfg["mean_load"]
     balance = jnp.sum(load_weight * small[4 + experts, :experts]) / token_total
     return (
@@ -769,8 +1208,8 @@
         wide[2],
         wide[3],
         small[4 : 4 + experts].T,
-        expert_in_grad[None],
-        expert_out_grad[None],
+        dwin[None],
+        dwout[None],
         small[0],
         small[1],
         small[2],

time: 417 us -> 301 us (0.72)
  waiting for transfers between devices: 131 us -> 0 us
  Pallas kernels: 193 us -> 272 us
  blocking collectives: 42.6 us -> 0 us
  between operations: 17.4 us -> 2.48 us
  other arithmetic: 16.5 us -> 4.45 us
  local copies, waits for them, and re-layouts: 15.6 us -> 21 us
    psum x1 -> x0, waiting for transfers between devices: 130 us -> none  [shards(): lax.psum((jnp.concatenate([full, dwo.astype(BF16)[None]]), jnp.concatenat...]
    pallas_call x2 -> x1, Pallas kernels: 139 us -> 218 us  [shards(): pl.pallas_call(functools.partial(layer_kernel, cfg, names), out_shape=[ja...]
    psum x1 -> x0, blocking collectives: 42.6 us -> none  [shards(): lax.psum((jnp.concatenate([full, dwo.astype(BF16)[None]]), jnp.concatenat...]
    broadcast_in_dim x3 -> x0, other arithmetic: 7.59 us -> none  [the longest x1 2.96 us: shards(): expert_in_grad[None]]
    unnamed x15 -> x13, local copies, waits for them, and re-layouts: 3.3 us -> 7.6 us
  transfers between devices with their start and end apart: 3 -> 0, of which waited for: 1 -> 0; matrix products, arithmetic and copies ran while one was open for 3% -> 0% of each run, Pallas kernels for 0% -> 0%
where the time goes in v2:
time: 301 us; the launch traced here: 300 us
  Pallas kernels  272 us (90%)
  local copies, waits for them, and re-layouts  21 us (7%)
  other arithmetic  4.45 us (1%)
    pallas_call x1, Pallas kernels, shards(): pl.pallas_call(functools.partial(layer_kernel, cfg, names), out_shape=[ja...  218 us
    pallas_call x1, Pallas kernels, shards(): call(attend_kernel, cfg, 1, in_vmem(5) + anywhere(3), [((length, half_wid...  54.3 us
    unnamed x13, local copies, waits for them, and re-layouts  7.6 us

profile of v2, /device:TPU:0, one launch (start us, length us, event | category | flops | bytes accessed | tf_op | source)
XLA Modules:
  0.0 300.1 jit_solution(8685141919536686609)
XLA Ops:
  0.6 1.3 reshape.69.gain.refs_4_
  1.9 1.3 reshape.70.bias
  3.2 1.3 reshape.71.refs_5_
  4.4 1.3 reshape.72.refs_6_
  5.7 1.5 copy.30.refs_3_
  7.2 1.5 copy.29.idx.refs_7_
  8.8 54.3 %attend.1 = (bf16[1024,384]{1,0:T(8,128)(2,1)}, bf16[1024,384]{1,0:T(8,128)(2,1)}, bf16[1024,384]{1,0:T(8,128)(2,1)}, bf16[1024,768]{1,0:T(8,128)(2,1)}, f32[8,1...) custom-call(bf16[512,768]{1,0:T(8,128)(2,1)} %bitcast.26, ...), custom_call_target="tpu_custom_call" | custom-call | flops 8589934592 | bytes 16777216 | tf_op jit(solution)/shard_map/attend/pallas_call | solution.py:1035
  63.0 217.9 %layer.1 = (bf16[512,768]{1,0:T(8,128)(2,1)}, bf16[512,768]{1,0:T(8,128)(2,1)}, bf16[4,768,768]{2,1,0:T(8,128)(2,1)}, f32[16,768]{1,0:T(8,128)}, f32[768,768]{1,0:T(8,128)}, /*index=5*/f32[768,768]{1,0:T(8,128)}) custom-call(bf16[512,768]{1,0:T(8,128)(2,1)} %bitcast.27, bf16[512,768]{1,0:T(8,128)(2,1)} %get-tuple-element.28.refs_1_, ...), custom_call_target="tpu_custom_call" | custom-call | flops 32212254720 | bytes 33554432 | tf_op jit(solution)/shard_map/layer/pallas_call | solution.py:1170
  281.0 1.3 multiply_reduce_fusion
  282.9 1.5 slice_reduce_fusion
  284.5 1.4 slice_bitcast_fusion.4
  285.9 3.2 %convert_element_type.3 = f32[4,768,768]{2,1,0:T(8,128)S(1)} convert(bf16[4,768,768]{2,1,0:T(8,128)(2,1)} %get-tuple-element.39) | non-fusion elementwise | flops 2359296 | bytes 14155776 | tf_op jit(solution)/shard_map/convert_element_type | solution.py:1199
  289.0 0.0 copy-start.3
  289.0 0.0 copy-start.2
  289.0 3.8 %slice_bitcast_fusion = (f32[768,768]{1,0:T(8,128)}, f32[768,768]{1,0:T(8,128)}, f32[768,768]{1,0:T(8,128)}, f32[768,768]{1,0:T(8,128)}) fusion(f32[4,768,768]{2,1,0:T(8,128)S(1)} %convert_element_type.3), kind=kLoop, calls=%fused_computation | loop fusion | bytes 18874368 | tf_op jit(solution)/shard_map/squeeze | solution.py:1209
  292.9 0.0 copy-start.1
  292.9 0.0 copy-done.3
  292.9 0.9 copy.36
  293.7 0.0 copy-done.2
  293.8 0.9 copy.37
  294.6 0.4 copy-done.1
  295.0 0.0 copy-start
  295.0 1.4 copy.38
  296.4 1.1 copy-done
  297.5 1.4 copy.39
Async XLA Ops:
  289.0 3.8 %copy-start.3 = (bf16[512,768]{1,0:T(8,128)(2,1)S(1)}, bf16[512,768]{1,0:T(8,128)(2,1)}, u32[]{:S(2)}) copy-start(bf16[512,768]{1,0:T(8,128)(2,1)} %get-tuple-element.36) | copy-start | bytes 2359300
  289.0 4.7 %copy-start.2 = (bf16[512,768]{1,0:T(8,128)(2,1)S(1)}, bf16[512,768]{1,0:T(8,128)(2,1)}, u32[]{:S(2)}) copy-start(bf16[512,768]{1,0:T(8,128)(2,1)} %get-tuple-element.38) | copy-start | bytes 2359300
  292.9 2.2 copy-start.1
  295.0 2.5 copy-start

commit v3 on v2

--- a/solution.py
+++ b/solution.py
@@ -16,7 +16,7 @@
 FF_COLS = 256
 MESH = pl.DeviceIdType.MESH
 BF16, F32 = jnp.bfloat16, jnp.float32
-VMEM_BYTES = 63 << 20
+VMEM_BYTES = 255 << 18
 NT = (((1,), (1,)), ((), ()))
 TN = (((0,), (0,)), ((), ()))
 
@@ -149,25 +149,17 @@
 
 
 def token_slots(me, idx):
-    rows = idx.shape[0]
-    hot = (idx == iota((rows, 128), 1)).astype(F32)
-    earlier = (iota((rows, rows), 1) < iota((rows, rows), 0)).astype(F32).astype(BF16)
-    ahead = dot(earlier, hot.astype(BF16))
-    slot = jnp.sum(ahead * hot, axis=1, keepdims=True)
-    return idx.astype(F32) * me.cap + slot, jnp.sum(hot, axis=0, keepdims=True)
+    rows = idx.shape[1]
+    hot = (iota((128, rows), 0) == idx).astype(F32)
+    earlier = (iota((rows, rows), 0) < iota((rows, rows), 1)).astype(F32).astype(BF16)
+    ahead = dot(hot.astype(BF16), earlier)
+    slot = jnp.sum(ahead * hot, axis=0, keepdims=True).astype(jnp.int32) + idx * me.cap
+    return slot, jnp.sum(hot, axis=1, keepdims=True)[0 : me.experts]
 
 
 def slots_by_token(me, slot):
-    rows = slot.shape[0]
-    across = jnp.transpose(jnp.broadcast_to(slot, (rows, 128)))[0:1, :]
-    slots = me.experts * me.cap
-    return (iota((slots, rows), 0) == across.astype(jnp.int32)).astype(F32).astype(BF16)
-
-
-def tokens_by_slot(me, slot):
-    rows = slot.shape[0]
-    slots = me.experts * me.cap
-    return (iota((rows, slots), 1) == slot.astype(jnp.int32)).astype(F32).astype(BF16)
+    shape = (me.experts * me.cap, slot.shape[1])
+    return (iota(shape, 0) == slot).astype(F32).astype(BF16)
 
 
 def head_masks():
@@ -175,163 +167,6 @@
     first = (lane < HEAD_DIM).astype(F32).astype(BF16)
     second = (lane >= HEAD_DIM).astype(F32).astype(BF16)
     return first, second
-
-
-def attend_kernel(
-    cfg,
-    x, og, idx, gain, bias, wq, wk, wv,
-    q, k, v, a, lse, o, dh, cnt,
-    w, xin, o_send, lse_cols, dh_send, cnt_exp, cnt_part, cnt_blk,
-    wsem, xs, xr, fs, fr, os, orr, ds, dr, cs, cr, bs, br,
-):
-    me = Place(cfg)
-    half = me.span // 2
-    columns = pl.ds(pl.multiple_of(me.c * me.half_width, 128), me.half_width)
-    loads = [
-        pltpu.make_async_copy(m.at[:, columns], w.at[j], wsem.at[j])
-        for j, m in enumerate((wq, wk, wv))
-    ]
-    for load in loads:
-        load.start()
-    me.greet()
-
-    def row_moves():
-        for s in range(me.seqs):
-            for h in range(2):
-                there = (me.c * me.seqs + s, me.pair + h)
-                yield (
-                    x.at[pl.ds(s * me.span + h * half, half)],
-                    xin.at[me.b],
-                    xs.at[2 * s + h],
-                    xr.at[me.b],
-                    there,
-                )
-
-    for move in row_moves():
-        push(me, *move)
-
-    slot, counts = token_slots(me, idx[...])
-    dh_send[...] = dot(slots_by_token(me, slot), og[...]).astype(BF16)
-    exchange_start(me, dh_send, dh, ds, dr, me.cap)
-    cnt_part[...] = jnp.broadcast_to(counts, cnt_part.shape)
-    own = me.e
-    pltpu.make_async_copy(cnt_part, cnt_exp.at[own], cr.at[0]).start()
-
-    def count_move(j):
-        return remote(
-            cnt_part, cnt_exp.at[me.e], cs.at[j], cr.at[j], (me.b, lax.rem(me.e + j, me.ne))
-        )
-
-    lax.fori_loop(1, me.ne, lambda j, _: count_move(j).start(), None)
-
-    def forward_move(j):
-        rows = split_rows(j * me.span + me.c * half, half)
-        return remote(a.at[rows], a.at[rows], fs.at[j], fr.at[j], (me.b, me.sibling))
-
-    for j in range(me.nb):
-        landed(xin.at[j], xr.at[j])
-        hat, _ = normalize(xin[j].astype(F32))
-        a[split_rows(j * me.span + me.c * half, half), :] = (
-            hat * gain[...] + bias[...]
-        ).astype(BF16)
-        forward_move(j).start()
-
-    landed(cnt_exp.at[me.e], cr.at[0])
-    lax.fori_loop(
-        1,
-        me.ne,
-        lambda j, _: landed(cnt_exp.at[lax.rem(me.e + me.ne - j, me.ne)], cr.at[j]),
-        None,
-    )
-    lax.fori_loop(1, me.ne, lambda j, _: count_move(j).wait_send(), None)
-    cnt_blk[me.b] = jnp.sum(cnt_exp[...], axis=0)
-
-    def blk_move(j):
-        return remote(
-            cnt_blk.at[me.b],
-            cnt_blk.at[me.b],
-            bs.at[j],
-            br.at[j],
-            (lax.rem(me.b + j, me.nb), me.e),
-        )
-
-    for j in range(1, me.nb):
-        blk_move(j).start()
-
-    for load in loads:
-        load.wait()
-    first, second = head_masks()
-    blocks = me.length // QUERY_ROWS
-    spans = QUERY_ROWS // me.span
-    lane = iota((1, PAIR), 1)
-    visible = iota((QUERY_ROWS, QUERY_ROWS), 1) <= iota((QUERY_ROWS, QUERY_ROWS), 0)
-    source = me.pair + lax.div(me.b, me.seqs)
-
-    def o_move(j):
-        return (
-            o_send.at[pl.ds(j * me.span, me.span)],
-            o.at[split_rows(lax.rem(me.b, me.seqs) * me.span, me.span), columns],
-            os.at[j],
-            orr.at[2 * lax.rem(me.b, me.seqs) + me.c],
-            (j, source),
-        )
-
-    for i in range(blocks):
-        for j in range(i * spans, (i + 1) * spans):
-            theirs = split_rows(j * me.span + (1 - me.c) * half, half)
-            landed(a.at[theirs], fr.at[j])
-        here = pl.ds(i * QUERY_ROWS, QUERY_ROWS)
-        rows = a[here, :]
-        q[here, :] = dot(rows, w[0]).astype(BF16) * jnp.asarray(SCALE, BF16)
-        k[here, :] = dot(rows, w[1]).astype(BF16)
-        v[here, :] = dot(rows, w[2]).astype(BF16)
-
-        def pair_of_heads(p, _, i=i, here=here):
-            lanes = split_rows(p * PAIR, PAIR)
-            queries = q[here, lanes]
-            parts = [pl.ds(i * QUERY_ROWS, QUERY_ROWS)]
-            if i:
-                parts.append(pl.ds(0, i * QUERY_ROWS))
-            done = []
-            for h, mask in enumerate((first, second)):
-                masked = queries * mask
-                scores = [dot(masked, k[part, lanes], NT) for part in parts]
-                scores[0] = jnp.where(visible, scores[0], -1e30)
-                peak = functools.reduce(
-                    jnp.maximum, [jnp.max(s, axis=1, keepdims=True) for s in scores]
-                )
-                powers = [jnp.exp(s - peak) for s in scores]
-                total = sum(jnp.sum(s, axis=1, keepdims=True) for s in powers)
-                mixed = sum(dot(s.astype(BF16), v[part, lanes]) for s, part in zip(powers, parts))
-                done.append(mixed / total)
-                lse_cols[here, :] = jnp.where(
-                    lane == 2 * p + h, peak + jnp.log(total), lse_cols[here, :]
-                )
-            o_send[here, lanes] = jnp.where(lane < HEAD_DIM, done[0], done[1]).astype(BF16)
-
-        lax.fori_loop(0, me.half_width // PAIR, pair_of_heads, None)
-        for j in range(i * spans, (i + 1) * spans):
-            push(me, *o_move(j))
-
-    lse[...] = jnp.transpose(lse_cols[...])[0:8, :]
-
-    for j in range(1, me.nb):
-        blk_move(j).wait_send()
-        landed(cnt_blk.at[lax.rem(me.b + me.nb - j, me.nb)], br.at[j])
-    cnt[...] = jnp.sum(cnt_blk[...], axis=0)
-    for move in row_moves():
-        push_done(me, *move)
-    for j in range(me.nb):
-        forward_move(j).wait_send()
-        push_done(me, *o_move(j))
-    for s in range(me.seqs):
-        for h in range(2):
-            landed(
-                o.at[pl.ds(s * me.span, me.span), pl.ds(h * me.half_width, me.half_width)],
-                orr.at[2 * s + h],
-            )
-    exchange_wait(me, dh_send, dh, ds, dr, me.cap)
-    exchange_sent(me, dh_send, dh, ds, dr, me.cap)
 
 
 def gelu_parts(u):
@@ -412,7 +247,7 @@
         def _():
             self.out_first(step, lo).start()
 
-    def second(self):
+    def second_add(self):
         r = self.r
         for step in range(1, self.count):
             hi = self.turn(step)
@@ -426,7 +261,6 @@
                 ).astype(BF16)
 
             lax.fori_loop(0, self.me.width // ROWS, in_rows, None)
-            self.in_second(step).start()
         for step in range(1, self.count):
             landed(r.out1.at[step - 1, self.other], r.out1r.at[step - 1, self.other])
         base = (2 * self.hi + self.other) * self.size
@@ -439,6 +273,10 @@
             r.wout[here, :] = total.astype(BF16)
 
         lax.fori_loop(0, self.size // ROWS, out_rows, None)
+
+    def second_send(self):
+        for step in range(1, self.count):
+            self.in_second(step).start()
         self.out_second().start()
 
     def total_in(self, into):
@@ -612,72 +450,224 @@
         self.move5().wait_send()
 
 
+class AllSum:
+    def __init__(self, me, own, by_exp, by_blk, sems):
+        self.me, self.own, self.by_exp, self.by_blk = me, own, by_exp, by_blk
+        self.es, self.er, self.bs, self.br = sems
+
+    def exp_move(self, k):
+        me = self.me
+        there = (me.b, lax.rem(me.e + k, me.ne))
+        return remote(self.own, self.by_exp.at[me.e], self.es.at[k], self.er.at[k], there)
+
+    def blk_move(self, k):
+        me = self.me
+        here = self.by_blk.at[me.b]
+        there = (lax.rem(me.b + k, me.nb), me.e)
+        return remote(here, here, self.bs.at[k], self.br.at[k], there)
+
+    def start(self):
+        lax.fori_loop(1, self.me.ne, lambda k, _: self.exp_move(k).start(), None)
+        self.by_exp[self.me.e] = self.own[...]
+
+    def middle(self):
+        me = self.me
+
+        def arrived(k, _):
+            landed(self.by_exp.at[lax.rem(me.e + me.ne - k, me.ne)], self.er.at[k])
+
+        lax.fori_loop(1, me.ne, arrived, None)
+        self.by_blk[me.b] = jnp.sum(self.by_exp[...], axis=0)
+        for k in range(1, me.nb):
+            self.blk_move(k).start()
+
+    def total(self):
+        me = self.me
+        for k in range(1, me.nb):
+            landed(self.by_blk.at[lax.rem(me.b + me.nb - k, me.nb)], self.br.at[k])
+        return jnp.sum(self.by_blk[...], axis=0)
+
+    def sent(self):
+        lax.fori_loop(1, self.me.ne, lambda k, _: self.exp_move(k).wait_send(), None)
+        for k in range(1, self.me.nb):
+            self.blk_move(k).wait_send()
+
+
 def layer_kernel(cfg, names, *refs):
     me = Place(cfg)
     r = Refs(names, refs)
+    half = me.span // 2
+    pairs = me.half_width // PAIR
+    blocks = me.length // QUERY_ROWS
+    slots = me.experts * me.cap
     r.ysend, r.yback = r.g, r.du
     r.swap, r.da_in = r.took.at[pl.ds(0, me.rows)], r.back.at[pl.ds(0, me.rows)]
-    half = me.span // 2
-    pairs = me.half_width // PAIR
-    weight_loads = [
-        pltpu.make_async_copy(r.win_hbm, r.win, r.wsem.at[0]),
-        pltpu.make_async_copy(r.wout_hbm, r.wout, r.wsem.at[1]),
-    ]
-    late = [
-        pltpu.make_async_copy(src, dst, r.lsem.at[n])
-        for n, (src, dst) in enumerate(
-            (
-                (r.og_hbm, r.og),
-                (r.q_hbm, r.q),
-                (r.k_hbm, r.k),
-                (r.v_hbm, r.v),
-                (r.a_hbm, r.a),
-                (r.lse_hbm, r.lse),
-            )
-        )
-    ]
+    r.xin, r.o_send, r.lse_cols, r.dh_send = r.mail, r.g, r.dk_sum, r.disp
+    gain1, bias1, gain2, bias2 = (
+        v[...].reshape(1, me.width) for v in (r.gain1, r.bias1, r.gain2, r.bias2)
+    )
+    loads = {}
+    for name in ("x", "og", "wo", "win", "wout"):
+        loads[name] = pltpu.make_async_copy(
+            getattr(r, name + "_hbm"), getattr(r, name), r.lsem.at[len(loads)]
+        )
     for p in range(pairs):
         for j, matrix in enumerate((r.wq_hbm, r.wk_hbm, r.wv_hbm)):
             src = matrix.at[:, pl.ds(pl.multiple_of(me.c * me.half_width + p * PAIR, PAIR), PAIR)]
-            late.append(
-                pltpu.make_async_copy(
-                    src, r.w.at[p, :, pl.ds(j * PAIR, PAIR)], r.lsem.at[6 + 3 * p + j]
-                )
+            loads["w", p, j] = pltpu.make_async_copy(
+                src, r.w.at[p, :, pl.ds(j * PAIR, PAIR)], r.lsem.at[len(loads)]
             )
-    for load in weight_loads + late:
+    for load in loads.values():
         load.start()
     me.greet()
+
+    def row_moves():
+        for s in range(me.seqs):
+            for h in range(2):
+                yield (
+                    r.x_hbm.at[pl.ds(s * me.span + h * half, half)],
+                    r.xin.at[split_rows(me.b * half, half)],
+                    r.xs.at[2 * s + h],
+                    r.xr.at[me.b],
+                    (me.c * me.seqs + s, me.pair + h),
+                )
+
+    for move in row_moves():
+        push(me, *move)
+
+    slot, counts = token_slots(me, r.idx[...])
+    r.cnt[...] = jnp.broadcast_to(counts, r.cnt.shape)
+    count_sum = AllSum(me, r.cnt, r.cnt_exp, r.cnt_blk, (r.ces, r.cer, r.cbs, r.cbr))
+    count_sum.start()
+    r.idx_col[...] = jnp.transpose(
+        jnp.broadcast_to(r.idx[...].astype(F32), (128, me.rows))
+    )
+    loads["og"].wait()
+    r.dh_send[...] = dot(slots_by_token(me, slot), r.og[...]).astype(BF16)
+    exchange_start(me, r.dh_send, r.dh, r.ds, r.dr, me.cap)
+
+    def forward_move(j):
+        rows = split_rows(j * me.span + me.c * half, half)
+        return remote(r.a.at[rows], r.a.at[rows], r.fws.at[j], r.fwr.at[j], (me.b, me.sibling))
+
+    for j in range(me.nb):
+        landed(r.xin.at[pl.ds(j * half, half)], r.xr.at[j])
+        hat, _ = normalize(r.xin[pl.ds(j * half, half), :].astype(F32))
+        r.a[split_rows(j * me.span + me.c * half, half), :] = (hat * gain1 + bias1).astype(BF16)
+        forward_move(j).start()
+
+    for p in range(pairs):
+        for j in range(3):
+            loads["w", p, j].wait()
+    first, second = head_masks()
+    spans = QUERY_ROWS // me.span
+    lane = iota((1, PAIR), 1)
+    visible = iota((QUERY_ROWS, QUERY_ROWS), 1) <= iota((QUERY_ROWS, QUERY_ROWS), 0)
+    home = me.pair + lax.div(me.b, me.seqs)
+    columns = pl.ds(pl.multiple_of(me.c * me.half_width, PAIR), me.half_width)
+
+    def o_move(j):
+        return (
+            r.o_send.at[
+                pl.ds(j * me.span % me.rows, me.span),
+                pl.ds(j * me.span // me.rows * me.half_width, me.half_width),
+            ],
+            r.o.at[split_rows(lax.rem(me.b, me.seqs) * me.span, me.span), columns],
+            r.os.at[j],
+            r.osr.at[2 * lax.rem(me.b, me.seqs) + me.c],
+            (j, home),
+        )
+
+    for i in range(blocks):
+        for j in range(i * spans, (i + 1) * spans):
+            theirs = split_rows(j * me.span + (1 - me.c) * half, half)
+            landed(r.a.at[theirs], r.fwr.at[j])
+        here = pl.ds(i * QUERY_ROWS, QUERY_ROWS)
+
+        def pair_of_heads(p, _, i=i, here=here):
+            lanes = split_rows(p * PAIR, PAIR)
+            qkv = dot(r.a[here, :], r.w[p]).astype(BF16)
+            queries = qkv[:, 0:PAIR] * jnp.asarray(SCALE, BF16)
+            r.q[here, lanes] = queries
+            r.k[here, lanes] = qkv[:, PAIR : 2 * PAIR]
+            r.v[here, lanes] = qkv[:, 2 * PAIR : 3 * PAIR]
+            parts = [pl.ds(i * QUERY_ROWS, QUERY_ROWS)]
+            if i:
+                parts.append(pl.ds(0, i * QUERY_ROWS))
+            done = []
+            for h, mask in enumerate((first, second)):
+                masked = queries * mask
+                scores = [dot(masked, r.k[part, lanes], NT) for part in parts]
+                scores[0] = jnp.where(visible, scores[0], -1e30)
+                peak = functools.reduce(
+                    jnp.maximum, [jnp.max(s, axis=1, keepdims=True) for s in scores]
+                )
+                powers = [jnp.exp(s - peak) for s in scores]
+                total = sum(jnp.sum(s, axis=1, keepdims=True) for s in powers)
+                mixed = sum(
+                    dot(s.astype(BF16), r.v[part, lanes]) for s, part in zip(powers, parts)
+                )
+                done.append(mixed / total)
+                r.lse_cols[here, :] = jnp.where(
+                    lane == 2 * p + h, peak + jnp.log(total), r.lse_cols[here, :]
+                )
+            base = i * QUERY_ROWS // me.rows * me.half_width
+            r.o_send[
+                pl.ds(i * QUERY_ROWS % me.rows, QUERY_ROWS),
+                pl.ds(pl.multiple_of(base + p * PAIR, PAIR), PAIR),
+            ] = jnp.where(lane < HEAD_DIM, done[0], done[1]).astype(BF16)
+
+        lax.fori_loop(0, pairs, pair_of_heads, None)
+        for j in range(i * spans, (i + 1) * spans):
+            push(me, *o_move(j))
+        if i == 0:
+            count_sum.middle()
+    r.lse[...] = jnp.transpose(r.lse_cols[...])[0:8, :]
+    for j in range(me.nb):
+        forward_move(j).wait_send()
+        push_done(me, *o_move(j))
+    for move in row_moves():
+        push_done(me, *move)
+    for name in ("x", "wo"):
+        loads[name].wait()
+    exchange_wait(me, r.dh_send, r.dh, r.ds, r.dr, me.cap)
+    exchange_sent(me, r.dh_send, r.dh, r.ds, r.dr, me.cap)
 
     expert_lane = iota((ROWS, me.experts), 1)
     r.sums[...] = jnp.zeros_like(r.sums)
     r.mass[...] = jnp.zeros_like(r.mass)
+    for s in range(me.seqs):
+        for h in range(2):
+            landed(
+                r.o.at[pl.ds(s * me.span, me.span), pl.ds(h * me.half_width, me.half_width)],
+                r.osr.at[2 * s + h],
+            )
 
     def token_rows(n, _):
         here = split_rows(n * ROWS, ROWS)
         hidden = r.x[here, :].astype(F32) + dot(r.o[here, :], r.wo[...])
         r.h1[here, :] = hidden
         hat, _ = normalize(hidden)
-        normed = (hat * r.gain2[...] + r.bias2[...]).astype(BF16)
+        normed = (hat * gain2 + bias2).astype(BF16)
         r.mail[here, :] = normed
-        logits = dot(normed, r.router[...])
-        hot = r.idx[here, :] == expert_lane
+        logits = dot(normed, r.router[...], NT)
+        hot = r.idx_col[here, 0 : me.experts].astype(jnp.int32) == expert_lane
         value = jax.nn.sigmoid(jnp.sum(jnp.where(hot, logits, 0.0), axis=1, keepdims=True))
         r.gate[here, :] = value
         r.mass[...] += jnp.sum(jnp.where(hot, value, 0.0), axis=0, keepdims=True)
 
     lax.fori_loop(0, me.rows // ROWS, token_rows, None)
-    slot, _ = token_slots(me, r.idx[...])
-    r.disp[...] = dot(slots_by_token(me, slot), r.mail[...]).astype(BF16)
+    takes = slots_by_token(me, slot)
+    r.disp[...] = dot(takes, r.mail[...]).astype(BF16)
     exchange_start(me, r.disp, r.took, r.ns, r.nr, me.cap)
-    for load in weight_loads:
-        load.wait()
+    loads["win"].wait()
+    loads["wout"].wait()
     exchange_wait(me, r.disp, r.took, r.ns, r.nr, me.cap)
     exchange_sent(me, r.disp, r.took, r.ns, r.nr, me.cap)
 
-    slots = me.experts * me.cap
     lanes = iota((slots, me.experts), 1)
     logits = jnp.sum(
-        jnp.where(lanes == me.e, dot(r.took[...], r.router[...]), 0.0), axis=1, keepdims=True
+        jnp.where(lanes == me.e, dot(r.took[...], r.router[...], NT), 0.0), axis=1, keepdims=True
     )
     value = jax.nn.sigmoid(logits)
     r.disp[...] = (value * r.dh[...].astype(F32)).astype(BF16)
@@ -724,62 +714,60 @@
     sums.tile = min(FF_COLS, sums.size) if sums.size % FF_COLS == 0 else PAIR
     lax.fori_loop(0, me.nb, expert_part, None)
 
-    load_lane = iota(r.cnt.shape, 1)
-    load = jnp.sum(jnp.where(load_lane == me.e, r.cnt[...], 0.0), axis=1, keepdims=True)[0:1, :]
-    weight = (load - me.mean_load) / me.mean_load
+    weights = (count_sum.total() - me.mean_load) / me.mean_load
+    weight = jnp.sum(jnp.where(iota(weights.shape, 0) == me.e, weights, 0.0), axis=0, keepdims=True)
+    weight = weight[:, 0:1]
     r.ysend[...] = r.yf[0:slots, :].astype(BF16)
     dgate = (
         jnp.sum(r.dh[...].astype(F32) * r.ysend[...].astype(F32), axis=1, keepdims=True)
         + weight / me.tokens
     )
     dlogits = jnp.where(lanes == me.e, dgate * value * (1.0 - value), 0.0).astype(BF16)
-    r.disp[...] = (r.made[0:slots, :] + dot(dlogits, r.router[...], NT)).astype(BF16)
+    r.disp[...] = (r.made[0:slots, :] + dot(dlogits, r.router[...])).astype(BF16)
     exchange_start(me, r.disp, r.back, r.rs, r.rr, me.cap)
-    r.sums[4 : 4 + me.experts, :] = dot(dlogits, r.took[...], TN)
-    r.sums[4 + me.experts : 5 + me.experts, 0 : me.experts] = r.mass[...]
-    sums.second()
+    r.sums[2 : 2 + me.experts, :] = dot(dlogits, r.took[...], TN)
+    r.sums[2 + me.experts : 3 + me.experts, 0 : me.experts] = r.mass[...]
+    sums.second_add()
     exchange_wait(me, r.disp, r.back, r.rs, r.rr, me.cap)
-    exchange_start(me, r.ysend, r.yback, r.ys, r.yr, me.cap)
-
-    for load in late:
-        load.wait()
-    takes = tokens_by_slot(me, slot)
-    r.made[0 : me.rows, :] = dot(takes, r.back[...])
+
+    r.made[0 : me.rows, :] = dot(takes, r.back[...], TN)
 
     def norm_rows(n, _):
         here = split_rows(n * ROWS, ROWS)
         grad = r.made[here, :]
         hat, inverse = normalize(r.h1[here, :])
-        r.sums[2:3, :] += jnp.sum(grad * hat, axis=0, keepdims=True)
-        r.sums[3:4, :] += jnp.sum(grad, axis=0, keepdims=True)
-        total = r.og[here, :].astype(F32) + norm_back(hat, inverse, r.gain2[...], grad)
+        r.sums[0:1, :] += jnp.sum(grad * hat, axis=0, keepdims=True)
+        r.sums[1:2, :] += jnp.sum(grad, axis=0, keepdims=True)
+        total = r.og[here, :].astype(F32) + norm_back(hat, inverse, gain2, grad)
         r.dh1[here, :] = total
         r.mail[here, :] = dot(total.astype(BF16), r.wo[...], NT).astype(BF16)
 
-    lax.fori_loop(0, me.rows // ROWS, norm_rows, None)
-
-    def o_moves():
-        for s in range(me.seqs):
-            for h in range(2):
-                yield (
-                    r.mail.at[
-                        pl.ds(s * me.span, me.span), pl.ds(h * me.half_width, me.half_width)
-                    ],
-                    r.do.at[split_rows(me.b * me.span, me.span)],
-                    r.os.at[2 * s + h],
-                    r.orr.at[me.b],
-                    (me.c * me.seqs + s, me.pair + h),
-                )
-
-    for move in o_moves():
-        push(me, *move)
+    def do_moves(s):
+        for h in range(2):
+            yield (
+                r.mail.at[pl.ds(s * me.span, me.span), pl.ds(h * me.half_width, me.half_width)],
+                r.do.at[split_rows(me.b * me.span, me.span)],
+                r.dos.at[2 * s + h],
+                r.dor.at[me.b],
+                (me.c * me.seqs + s, me.pair + h),
+            )
+
+    steps = me.span // ROWS
+    for s in range(me.seqs):
+        lax.fori_loop(s * steps, (s + 1) * steps, norm_rows, None)
+        for move in do_moves(s):
+            push(me, *move)
+    sums.second_send()
+    early = AllSum(me, r.sums, r.sum_exp, r.sum_blk, (r.es, r.er, r.bs, r.br))
+    early.start()
+    exchange_start(me, r.ysend, r.yback, r.ys, r.yr, me.cap)
 
     def output_columns(core):
         cols = pl.ds(pl.multiple_of(core * me.half_width, PAIR), me.half_width)
         return dot(r.o[...], r.dh1[:, cols].astype(BF16), TN)
 
     r.part[0] = output_columns(1 - me.c).astype(BF16)
-    o_swap = remote(r.part.at[0], r.ogot, r.oss, r.osr, (me.b, me.sibling))
+    o_swap = remote(r.part.at[0], r.ogot, r.ows, r.owr, (me.b, me.sibling))
     o_swap.start()
     own_columns = output_columns(me.c)
     o_swap.wait()
@@ -790,12 +778,10 @@
 
     r.made[...] = jnp.zeros_like(r.made)
     for j in range(me.nb):
-        landed(r.do.at[pl.ds(j * me.span, me.span)], r.orr.at[j])
-    first, second = head_masks()
-    blocks = me.length // QUERY_ROWS
+        landed(r.do.at[pl.ds(j * me.span, me.span)], r.dor.at[j])
     visible = iota((QUERY_ROWS, QUERY_ROWS), 0) <= iota((QUERY_ROWS, QUERY_ROWS), 1)
 
-    def pair_of_heads(n, _):
+    def pair_back(n, _):
         lanes = split_rows(n * PAIR, PAIR)
         r.dk_sum[...] = jnp.zeros_like(r.dk_sum)
         r.dv_sum[...] = jnp.zeros_like(r.dv_sum)
@@ -851,17 +837,19 @@
                 pieces[0].stage3()
                 pieces[3].stage4()
 
-    lax.fori_loop(0, pairs, pair_of_heads, None)
-
-    for move in o_moves():
-        push_done(me, *move)
+    lax.fori_loop(0, pairs, pair_back, None)
+    early.middle()
+
+    for s in range(me.seqs):
+        for move in do_moves(s):
+            push_done(me, *move)
     for j in range(me.nb):
         theirs = split_rows(j * me.span + (1 - me.c) * half, half)
         r.mail[pl.ds(j * half, half), :] = r.made[theirs, :].astype(BF16)
     swap = remote(r.mail, r.swap, r.ss, r.sr, (me.b, me.sibling))
     swap.start()
     exchange_wait(me, r.ysend, r.yback, r.ys, r.yr, me.cap)
-    r.yf[0 : me.rows, :] = dot(takes, r.yback[...])
+    r.yf[0 : me.rows, :] = dot(takes, r.yback[...], TN)
 
     def out_rows(n, _):
         here = split_rows(n * ROWS, ROWS)
@@ -869,8 +857,6 @@
 
     lax.fori_loop(0, me.rows // ROWS, out_rows, None)
     swap.wait()
-    home = me.pair + lax.div(me.b, me.seqs)
-
     def da_move(j):
         return (
             r.mail.at[pl.ds(j * half, half)],
@@ -894,80 +880,76 @@
         for h in range(2):
             landed(r.da_in.at[pl.ds(s * me.span + h * half, half)], r.fr.at[2 * s + h])
 
+    r.late[...] = jnp.zeros_like(r.late)
+    tiles = me.width // FF_COLS
+
     def first_norm_rows(n, _):
         here = split_rows(n * ROWS, ROWS)
         grad = r.da_in[here, :].astype(F32)
         hat, inverse = normalize(r.x[here, :].astype(F32))
-        r.sums[0:1, :] += jnp.sum(grad * hat, axis=0, keepdims=True)
-        r.sums[1:2, :] += jnp.sum(grad, axis=0, keepdims=True)
-        r.dx[here, :] = (r.dh1[here, :] + norm_back(hat, inverse, r.gain1[...], grad)).astype(
-            BF16
-        )
+        gain_part = jnp.sum(grad * hat, axis=0, keepdims=True)
+        bias_part = jnp.sum(grad, axis=0, keepdims=True)
+        for j in range(tiles):
+            cols = slice(j * FF_COLS, (j + 1) * FF_COLS)
+            r.late[j : j + 1, :] += gain_part[:, cols]
+            r.late[tiles + j : tiles + j + 1, :] += bias_part[:, cols]
+        r.dx[here, :] = (r.dh1[here, :] + norm_back(hat, inverse, gain1, grad)).astype(BF16)
 
     lax.fori_loop(0, me.rows // ROWS, first_norm_rows, None)
-
-    def sum_move(k):
-        return remote(
-            r.sums,
-            r.sum_exp.at[me.e],
-            r.es.at[k],
-            r.er.at[k],
-            (me.b, lax.rem(me.e + k, me.ne)),
-        )
-
-    lax.fori_loop(1, me.ne, lambda k, _: sum_move(k).start(), None)
-    r.sum_exp[me.e] = r.sums[...]
+    late = AllSum(me, r.late, r.late_exp, r.late_blk, (r.les, r.ler, r.lbs, r.lbr))
+    late.start()
     if pieces:
         pieces[2].stage3()
         pieces[1].stage4()
         pieces[0].stage5()
-    lax.fori_loop(
-        1,
-        me.ne,
-        lambda k, _: landed(r.sum_exp.at[lax.rem(me.e + me.ne - k, me.ne)], r.er.at[k]),
-        None,
-    )
-    r.sum_blk[me.b] = jnp.sum(r.sum_exp[...], axis=0)
-
-    def blk_move(k):
-        return remote(
-            r.sum_blk.at[me.b],
-            r.sum_blk.at[me.b],
-            r.bs.at[k],
-            r.br.at[k],
-            (lax.rem(me.b + k, me.nb), me.e),
-        )
-
-    for k in range(1, me.nb):
-        blk_move(k).start()
+    late.middle()
     if pieces:
         pieces[2].stage4()
         pieces[1].stage5()
 
     size = sums.size
     sums.total_in(r.made)
-    store_in = pltpu.make_async_copy(r.made.at[pl.ds(0, me.width), pl.ds(0, size)], r.dwin, r.wsem.at[0])
+    store_in = pltpu.make_async_copy(
+        r.made.at[pl.ds(0, me.width), pl.ds(0, size)], r.dwin, r.fsem.at[0]
+    )
     store_in.start()
     sums.total_out(r.yf)
-    store_out = pltpu.make_async_copy(r.yf.at[pl.ds(0, size)], r.dwout, r.wsem.at[1])
+    store_out = pltpu.make_async_copy(r.yf.at[pl.ds(0, size)], r.dwout, r.fsem.at[1])
     store_out.start()
     if pieces:
         pieces[2].stage5()
-    for k in range(1, me.nb):
-        landed(r.sum_blk.at[lax.rem(me.b + me.nb - k, me.nb)], r.br.at[k])
-    r.small[...] = jnp.sum(r.sum_blk[...], axis=0)
-    lax.fori_loop(1, me.ne, lambda k, _: sum_move(k).wait_send(), None)
-    for k in range(1, me.nb):
-        blk_move(k).wait_send()
+    early_total = early.total()
+    late_total = late.total()
+    r.small[0 : r.sums.shape[0], :] = early_total
+    for j in range(tiles):
+        cols = slice(j * FF_COLS, (j + 1) * FF_COLS)
+        r.small[me.experts + 4 : me.experts + 5, cols] = late_total[j : j + 1, :]
+        r.small[me.experts + 5 : me.experts + 6, cols] = late_total[tiles + j : tiles + j + 1, :]
+    own_weight = jnp.transpose(jnp.broadcast_to(weights, (weights.shape[0], 128)))[0:1, :]
+    mass = early_total[2 + me.experts : 3 + me.experts, 0 : me.experts]
+    r.small[me.experts + 3 : me.experts + 4, 0:1] = (
+        jnp.sum(own_weight[:, 0 : me.experts] * mass, axis=1, keepdims=True) / me.tokens
+    )
+    for each in (count_sum, early, late):
+        each.sent()
     exchange_sent(me, r.disp, r.back, r.rs, r.rr, me.cap)
     exchange_sent(me, r.ysend, r.yback, r.ys, r.yr, me.cap)
     for j in range(me.nb):
         push_done(me, *da_move(j))
     sums.sent()
+    stores = [store_in, store_out]
     for piece in pieces:
         piece.end()
-    store_in.wait()
-    store_out.wait()
+    if pieces:
+        targets = [(r.shared.at[j], out) for j, out in enumerate((r.gq, r.gk, r.gv, r.go))]
+    else:
+        targets = [(r.part, r.own_part)]
+    for n, (src, dst) in enumerate(targets):
+        store = pltpu.make_async_copy(src, dst, r.fsem.at[2 + n])
+        store.start()
+        stores.append(store)
+    for store in stores:
+        store.wait()
 
 
 def in_vmem(count):
@@ -976,21 +958,6 @@
 
 def anywhere(count):
     return [pl.BlockSpec(memory_space=pl.ANY)] * count
-
-
-def call(body, cfg, number, in_specs, outs, scratch, name, cost):
-    return pl.pallas_call(
-        functools.partial(body, cfg),
-        out_shape=[jax.ShapeDtypeStruct(shape, kind) for shape, kind in outs],
-        in_specs=in_specs,
-        out_specs=in_vmem(len(outs)),
-        scratch_shapes=scratch,
-        compiler_params=pltpu.CompilerParams(
-            collective_id=number, has_side_effects=True, vmem_limit_bytes=VMEM_BYTES
-        ),
-        cost_estimate=pl.CostEstimate(flops=cost, bytes_accessed=1 << 24, transcendentals=1 << 22),
-        name=name,
-    )
 
 
 def shards(
@@ -1024,91 +991,54 @@
         experts=experts, ff=ff, cap=cap, half_width=half_width, tokens=token_total,
         mean_load=token_total / experts,
     )
-    x = tokens.reshape(rows, width)
-    og = output_grad.reshape(rows, width)
-    idx = expert_index.reshape(rows, 1)
-    gain1, bias1 = norm1_gain.reshape(1, width), norm1_bias.reshape(1, width)
-    gain2, bias2 = norm2_gain.reshape(1, width), norm2_bias.reshape(1, width)
     dma = pltpu.SemaphoreType.DMA
     vmem = pltpu.VMEM
-    half = span // 2
-    q, k, v, a, lse, o, dh, cnt = call(
-        attend_kernel, cfg, 1,
-        in_vmem(5) + anywhere(3),
-        [
-            ((length, half_width), BF16),
-            ((length, half_width), BF16),
-            ((length, half_width), BF16),
-            ((length, width), BF16),
-            ((8, length), F32),
-            ((rows, width), BF16),
-            ((slots, width), BF16),
-            ((8, 128), F32),
-        ],
-        [
-            vmem((3, width, half_width), BF16),
-            vmem((nb, half, width), BF16),
-            vmem((length, half_width), BF16),
-            vmem((length, 128), F32),
-            vmem((slots, width), BF16),
-            vmem((ne, 8, 128), F32),
-            vmem((8, 128), F32),
-            vmem((nb, 8, 128), F32),
-            dma((3,)),
-            dma((2 * seqs,)), dma((nb,)),
-            dma((nb,)), dma((nb,)),
-            dma((nb,)), dma((2 * seqs,)),
-            dma((ne,)), dma((ne,)),
-            dma((ne,)), dma((ne,)),
-            dma((nb,)), dma((nb,)),
-        ],
-        "attend", 8 << 30,
-    )(x, og, idx, gain1, bias1, query_weight, key_weight, value_weight)
     hi = nb // 2
     size = ff // nb
-    sum_rows = -(-(5 + experts) // 8) * 8
+    sum_rows = -(-(3 + experts) // 8) * 8
     cfg["sum_here"] = width % (8 * nb * ne) == 0
     outer = width // min(nb, ne // 2)
     inner = width // (nb * ne // 2)
     inputs = (
-        ("x", x, True),
-        ("o", o, True),
-        ("wo", output_weight, True),
-        ("router", router_weight, True),
-        ("gain1", gain1, True),
-        ("gain2", gain2, True),
-        ("bias2", bias2, True),
-        ("idx", idx, True),
-        ("dh", dh, True),
-        ("cnt", cnt, True),
+        ("idx", expert_index.reshape(1, rows), True),
+        ("router", router_weight.T, True),
+        ("gain1", norm1_gain, True),
+        ("bias1", norm1_bias, True),
+        ("gain2", norm2_gain, True),
+        ("bias2", norm2_bias, True),
+        ("x_hbm", tokens.reshape(rows, width), False),
+        ("og_hbm", output_grad.reshape(rows, width), False),
+        ("wo_hbm", output_weight, False),
         ("win_hbm", expert_in.reshape(width, ff), False),
         ("wout_hbm", expert_out.reshape(ff, width), False),
-        ("og_hbm", og, False),
-        ("q_hbm", q, False),
-        ("k_hbm", k, False),
-        ("v_hbm", v, False),
-        ("a_hbm", a, False),
-        ("lse_hbm", lse, False),
         ("wq_hbm", query_weight, False),
         ("wk_hbm", key_weight, False),
         ("wv_hbm", value_weight, False),
     )
-    outputs = (
+    small_rows = -(-(6 + experts) // 8) * 8
+    outputs = [
         ("out", (rows, width), BF16, True),
         ("dx", (rows, width), BF16, True),
-        (
-            ("shared", (4, width, width), BF16, True)
-            if cfg["sum_here"]
-            else ("part", (4, width, half_width), BF16, True)
-        ),
-        ("small", (sum_rows, width), F32, True),
+        ("small", (small_rows, width), F32, True),
         ("dwin", (width, size), F32, False),
         ("dwout", (size, width), F32, False),
-    )
+    ]
+    if cfg["sum_here"]:
+        outputs += [(n, (width, width), BF16, False) for n in ("gq", "gk", "gv", "go")]
+    else:
+        outputs.append(("own_part", (4, width, half_width), BF16, False))
     scratch = dict(
         win=vmem((width, ff), BF16),
         wout=vmem((ff, width), BF16),
+        x=vmem((rows, width), BF16),
         og=vmem((rows, width), BF16),
+        o=vmem((rows, width), BF16),
+        wo=vmem((width, width), BF16),
+        dh=vmem((slots, width), BF16),
+        idx_col=vmem((rows, 128), F32),
+        cnt=vmem((experts, 128), F32),
+        cnt_exp=vmem((ne, experts, 128), F32),
+        cnt_blk=vmem((nb, experts, 128), F32),
         q=vmem((length, half_width), BF16),
         k=vmem((length, half_width), BF16),
         v=vmem((length, half_width), BF16),
@@ -1135,6 +1065,10 @@
         sums=vmem((sum_rows, width), F32),
         sum_exp=vmem((ne, sum_rows, width), F32),
         sum_blk=vmem((nb, sum_rows, width), F32),
+        late=vmem((8, FF_COLS), F32),
+        late_exp=vmem((ne, 8, FF_COLS), F32),
+        late_blk=vmem((nb, 8, FF_COLS), F32),
+        part=vmem((4, width, half_width), BF16),
         in1=vmem((hi, width, size), BF16),
         in2=vmem((hi - 1, width, size), BF16),
         out1=vmem((hi - 1, 2, size, width), BF16),
@@ -1143,21 +1077,26 @@
         in2s=dma((hi - 1,)), in2r=dma((hi - 1,)),
         out1s=dma((hi - 1, 2)), out1r=dma((hi - 1, 2)),
         out2s=dma, out2r=dma,
-        wsem=dma((2,)),
-        lsem=dma((6 + 3 * (half_width // PAIR),)),
+        lsem=dma((5 + 3 * (half_width // PAIR),)),
+        fsem=dma((6,)),
+        xs=dma((2 * seqs,)), xr=dma((nb,)),
+        fws=dma((nb,)), fwr=dma((nb,)),
+        os=dma((nb,)), osr=dma((2 * seqs,)),
+        ds=dma((ne,)), dr=dma((ne,)),
+        ces=dma((ne,)), cer=dma((ne,)), cbs=dma((nb,)), cbr=dma((nb,)),
         ns=dma((ne,)), nr=dma((ne,)),
         rs=dma((ne,)), rr=dma((ne,)),
         ys=dma((ne,)), yr=dma((ne,)),
-        os=dma((2 * seqs,)), orr=dma((nb,)),
-        oss=dma, osr=dma,
+        dos=dma((2 * seqs,)), dor=dma((nb,)),
+        ows=dma, owr=dma,
         ss=dma, sr=dma,
         fs=dma((nb,)), fr=dma((2 * seqs,)),
-        es=dma((ne,)), er=dma((ne,)),
-        bs=dma((nb,)), br=dma((nb,)),
+        es=dma((ne,)), er=dma((ne,)), bs=dma((nb,)), br=dma((nb,)),
+        les=dma((ne,)), ler=dma((ne,)), lbs=dma((nb,)), lbr=dma((nb,)),
     )
     if cfg["sum_here"]:
         scratch.update(
-            part=vmem((4, width, half_width), BF16),
+            shared=vmem((4, width, width), BF16),
             got1=vmem((4, max(nb, ne // 2), outer, half_width), BF16),
             got2=vmem((4, max(nb, ne // 2), inner, half_width), BF16),
             s5=dma((4,)),
@@ -1167,14 +1106,14 @@
             scratch[f"s{n}"] = dma((4, max(nb, ne // 2)))
             scratch[f"r{n}"] = dma((4, max(nb, ne // 2)))
     names = [n for n, _, _ in inputs] + [n for n, _, _, _ in outputs] + list(scratch)
-    out, dx, shared, small, dwin, dwout = pl.pallas_call(
+    out, dx, small, dwin, dwout, *wide = pl.pallas_call(
         functools.partial(layer_kernel, cfg, names),
         out_shape=[jax.ShapeDtypeStruct(shape, kind) for _, shape, kind, _ in outputs],
         in_specs=[(in_vmem if near else anywhere)(1)[0] for _, _, near in inputs],
         out_specs=[(in_vmem if near else anywhere)(1)[0] for _, _, _, near in outputs],
         scratch_shapes=list(scratch.values()),
         compiler_params=pltpu.CompilerParams(
-            collective_id=2, has_side_effects=True, vmem_limit_bytes=VMEM_BYTES
+            collective_id=1, has_side_effects=True, vmem_limit_bytes=VMEM_BYTES
         ),
         cost_estimate=pl.CostEstimate(
             flops=30 << 30, bytes_accessed=1 << 25, transcendentals=1 << 23
@@ -1182,7 +1121,7 @@
         name="layer",
     )(*[value for _, value, _ in inputs])
     if not cfg["sum_here"]:
-        own = shared.reshape(4, width, half_width)
+        own = wide[0]
         own = jnp.concatenate(
             [
                 own[:3].reshape(3, width, 3, PAIR).transpose(2, 1, 0, 3).reshape(3, width, half_width),
@@ -1190,30 +1129,25 @@
             ]
         )
         core, empty = lax.rem(lax.axis_index("exp"), 2), jnp.zeros_like(own)
-        shared = lax.psum(
+        wide = lax.psum(
             jnp.concatenate(
                 [jnp.where(core == 0, own, empty), jnp.where(core == 0, empty, own)], axis=2
             ),
             ("blk", "exp"),
         )
-    wide = shared.astype(F32)
-    load_weight = (cnt[0, :experts] - cfg["mean_load"]) / cfg["mean_load"]
-    balance = jnp.sum(load_weight * small[4 + experts, :experts]) / token_total
+    wide = [wide[n].astype(F32) for n in range(4)]
     return (
         out.reshape(seqs, span, width),
-        balance,
+        small[experts + 3, 0],
         dx.reshape(seqs, span, width),
-        wide[0],
-        wide[1],
-        wide[2],
-        wide[3],
-        small[4 : 4 + experts].T,
+        *wide,
+        small[2 : 2 + experts].T,
         dwin[None],
         dwout[None],
+        small[experts + 4],
+        small[experts + 5],
         small[0],
         small[1],
-        small[2],
-        small[3],
     )
 
 

time: 301 us -> 264 us (0.88)
  Pallas kernels: 272 us -> 244 us
  local copies, waits for them, and re-layouts: 21 us -> 10.5 us
  other arithmetic: 4.45 us -> 7.57 us
    pallas_call x1 -> x0, Pallas kernels: 54.3 us -> none  [shards(): call(attend_kernel, cfg, 1, in_vmem(5) + anywhere(3), [((length, half_wid...]
    pallas_call x1, Pallas kernels: 218 us -> 244 us  [shards(): pl.pallas_call(functools.partial(layer_kernel, cfg, names), out_shape=[ja...]
    reshape x5 -> x0, local copies, waits for them, and re-layouts: 6.6 us -> none  [the longest x2 2.53 us: shards(): gain1, bias1 = (norm1_gain.reshape(1, width), norm1_bias.reshape(1, width))]
    convert_element_type x1 -> x4, other arithmetic: 3.15 us -> 7.57 us  [shards(): wide = [wide[n].astype(F32) for n in range(4)]]
    squeeze x1 -> x0, local copies, waits for them, and re-layouts: 3.82 us -> none  [shards(): wide[3]]
    unnamed x13 -> x18, local copies, waits for them, and re-layouts: 7.6 us -> 6.37 us
where the time goes in v3:
time: 264 us; the launch traced here: 263 us
  Pallas kernels  244 us (92%)
  local copies, waits for them, and re-layouts  10.5 us (4%)
  other arithmetic  7.57 us (3%)
    pallas_call x1, Pallas kernels, shards(): pl.pallas_call(functools.partial(layer_kernel, cfg, names), out_shape=[ja...  244 us
    convert_element_type x4, other arithmetic, shards(): wide = [wide[n].astype(F32) for n in range(4)]  7.57 us
    unnamed x18, local copies, waits for them, and re-layouts  6.37 us

profile of v3, /device:TPU:0, one launch (start us, length us, event | category | flops | bytes accessed | tf_op | source)
XLA Modules:
  0.0 263.1 jit_solution(15771774520638289137)
XLA Ops:
  0.7 244.4 %layer.1 = (bf16[512,768]{1,0:T(8,128)(2,1)}, bf16[512,768]{1,0:T(8,128)(2,1)}, f32[16,768]{1,0:T(8,128)}, f32[768,768]{1,0:T(8,128)}, f32[768,768]{1,0:T(8,128)...) custom-call(s32[1,512]{1,0:T(1,128)} %bitcast.22, ...), custom_call_target="tpu_custom_call" | custom-call | flops 32212254720 | bytes 33554432 | tf_op jit(solution)/shard_map/layer/pallas_call | solution.py:1109
  245.0 0.0 copy-start.4
  245.0 1.3 slice.18
  246.3 1.5 slice_reduce_fusion
  247.8 1.4 slice_bitcast_fusion
  249.2 2.8 %convert_element_type.12 = f32[768,768]{1,0:T(8,128)} convert(bf16[768,768]{1,0:T(8,128)(2,1)} %get-tuple-element.26) | non-fusion elementwise | flops 589824 | bytes 3538944 | tf_op jit(solution)/shard_map/convert_element_type | solution.py:1138
  252.0 0.0 copy-done.4
  252.0 0.0 copy-start.3
  252.1 1.6 convert_element_type.13
  253.6 0.1 copy-done.3
  253.7 0.0 copy-start.2
  253.7 1.6 convert_element_type.14
  255.3 0.1 copy-done.2
  255.4 0.0 copy-start.6
  255.4 0.0 copy-start.5
  255.4 1.6 convert_element_type.15
  257.0 0.0 copy-done.6
  257.0 0.0 copy-start.1
  257.0 0.9 copy.32
  257.9 0.0 copy-done.5
  257.9 0.9 copy.33
  258.7 0.5 copy-done.1
  259.2 0.0 copy-start
  259.2 1.4 copy.34
  260.6 1.1 copy-done
  261.7 1.4 copy.35
Async XLA Ops:
  245.0 7.0 %copy-start.4 = (bf16[768,768]{1,0:T(8,128)(2,1)S(1)}, bf16[768,768]{1,0:T(8,128)(2,1)}, u32[]{:S(2)}) copy-start(bf16[768,768]{1,0:T(8,128)(2,1)} %get-tuple-element.27) | copy-start | bytes 3538948
  252.0 1.7 copy-start.3
  253.7 1.7 copy-start.2
  255.4 1.6 copy-start.6
  255.4 2.5 copy-start.5
  257.0 2.2 copy-start.1
  259.2 2.5 copy-start

commit v4 on v3

--- a/solution.py
+++ b/solution.py
@@ -16,6 +16,17 @@
 FF_COLS = 256
 MESH = pl.DeviceIdType.MESH
 BF16, F32 = jnp.bfloat16, jnp.float32
+BLK_FIRST = (0, 1, 2)
+PLAN = {
+    "start": ((3, 1),),
+    0: ((0, 1),),
+    1: ((1, 1),),
+    2: ((2, 1), (3, 2), (0, 2)),
+    "rows sent": ((1, 2), (2, 2), (3, 3), (0, 3)),
+    "rows done": ((1, 3), (2, 3), (3, 4), (0, 4)),
+    "late": ((1, 4), (2, 4), (3, 5), (0, 5)),
+    "last": ((1, 5), (2, 5)),
+}
 VMEM_BYTES = 255 << 18
 NT = (((1,), (1,)), ((), ()))
 TN = (((0,), (0,)), ((), ()))
@@ -500,6 +511,8 @@
     pairs = me.half_width // PAIR
     blocks = me.length // QUERY_ROWS
     slots = me.experts * me.cap
+    roomy = slots * me.width <= 1 << 19
+    model_tile = me.width if roomy else FF_COLS
     r.ysend, r.yback = r.g, r.du
     r.swap, r.da_in = r.took.at[pl.ds(0, me.rows)], r.back.at[pl.ds(0, me.rows)]
     r.xin, r.o_send, r.lse_cols, r.dh_send = r.mail, r.g, r.dk_sum, r.disp
@@ -674,7 +687,7 @@
     r.yf[0:slots, :] = jnp.zeros((slots, me.width), F32)
     r.made[...] = jnp.zeros_like(r.made)
     sums = ExpertSums(me, r)
-    slot_rows = slots // 2
+    slot_rows = slots if roomy else slots // 4
 
     def expert_part(n, _):
         hi, lo = sums.turn(lax.div(n, 2) + 1), lax.rem(sums.other + n, 2)
@@ -695,12 +708,13 @@
         lax.fori_loop(0, sums.size // sums.tile, hidden_columns, None)
         part = sums.span(hi, lo)
 
+
         def model_columns(f, _):
-            here = split_rows(f * FF_COLS, FF_COLS)
+            here = split_rows(f * model_tile, model_tile)
             r.yf[0:slots, here] += dot(r.g[:, 0 : sums.size], r.wout[part, here])
             r.made[0:slots, here] += dot(r.du[:, 0 : sums.size], r.win[here, part], NT)
 
-        lax.fori_loop(0, me.width // FF_COLS, model_columns, None)
+        lax.fori_loop(0, me.width // model_tile, model_columns, None)
 
         def weight_columns(f, _):
             here = pl.ds(pl.multiple_of(base + f * sums.tile, 128), sums.tile)
@@ -711,7 +725,7 @@
         lax.fori_loop(0, sums.size // sums.tile, weight_columns, None)
         sums.after_part(n)
 
-    sums.tile = min(FF_COLS, sums.size) if sums.size % FF_COLS == 0 else PAIR
+    sums.tile = sums.size
     lax.fori_loop(0, me.nb, expert_part, None)
 
     weights = (count_sum.total() - me.mean_load) / me.mean_load
@@ -772,9 +786,13 @@
     own_columns = output_columns(me.c)
     o_swap.wait()
     r.part[3] = (own_columns + r.ogot[...].astype(F32)).astype(BF16)
-    pieces = [SharedSum(me, r, p, blk_first=p in (1, 2)) for p in range(4)] if me.sum_here else []
-    if pieces:
-        pieces[3].stage1()
+    pieces = [SharedSum(me, r, p, p in BLK_FIRST) for p in range(4)] if me.sum_here else []
+
+    def advance(point):
+        for p, stage in PLAN.get(point, ()) if pieces else ():
+            getattr(pieces[p], f"stage{stage}")()
+
+    advance("start")
 
     r.made[...] = jnp.zeros_like(r.made)
     for j in range(me.nb):
@@ -813,29 +831,15 @@
         r.part[n] = dot(r.a[...], r.dqkv[...], TN).astype(BF16)
 
         def normed_columns(f, _):
-            cols = split_rows(f * FF_COLS, FF_COLS)
+            cols = split_rows(f * model_tile, model_tile)
             r.made[:, cols] += dot(r.dqkv[...], r.w[n, cols, :], NT)
 
-        lax.fori_loop(0, me.width // FF_COLS, normed_columns, None)
-        if pieces:
-
-            @pl.when(n == 0)
-            def _():
-                pieces[0].stage1()
-                pieces[3].stage2()
-
-            @pl.when(n == 1)
-            def _():
-                pieces[1].stage1()
-                pieces[0].stage2()
-                pieces[3].stage3()
-
-            @pl.when(n == 2)
-            def _():
-                pieces[2].stage1()
-                pieces[1].stage2()
-                pieces[0].stage3()
-                pieces[3].stage4()
+        lax.fori_loop(0, me.width // model_tile, normed_columns, None)
+        for done in range(pairs):
+
+            @pl.when(n == done)
+            def _(done=done):
+                advance(done)
 
     lax.fori_loop(0, pairs, pair_back, None)
     early.middle()
@@ -871,11 +875,7 @@
         rows = pl.ds(j * half, half)
         r.mail[rows, :] = (mine + r.swap[rows, :].astype(F32)).astype(BF16)
         push(me, *da_move(j))
-    if pieces:
-        pieces[2].stage2()
-        pieces[1].stage3()
-        pieces[0].stage4()
-        pieces[3].stage5()
+    advance("rows sent")
     for s in range(me.seqs):
         for h in range(2):
             landed(r.da_in.at[pl.ds(s * me.span + h * half, half)], r.fr.at[2 * s + h])
@@ -898,14 +898,9 @@
     lax.fori_loop(0, me.rows // ROWS, first_norm_rows, None)
     late = AllSum(me, r.late, r.late_exp, r.late_blk, (r.les, r.ler, r.lbs, r.lbr))
     late.start()
-    if pieces:
-        pieces[2].stage3()
-        pieces[1].stage4()
-        pieces[0].stage5()
+    advance("rows done")
     late.middle()
-    if pieces:
-        pieces[2].stage4()
-        pieces[1].stage5()
+    advance("late")
 
     size = sums.size
     sums.total_in(r.made)
@@ -916,8 +911,7 @@
     sums.total_out(r.yf)
     store_out = pltpu.make_async_copy(r.yf.at[pl.ds(0, size)], r.dwout, r.fsem.at[1])
     store_out.start()
-    if pieces:
-        pieces[2].stage5()
+    advance("last")
     early_total = early.total()
     late_total = late.total()
     r.small[0 : r.sums.shape[0], :] = early_total

time: 264 us -> 240 us (0.909)
  Pallas kernels: 244 us -> 220 us
    pallas_call x1, Pallas kernels: 244 us -> 220 us  [shards(): pl.pallas_call(functools.partial(layer_kernel, cfg, names), out_shape=[ja...]
where the time goes in v4:
time: 240 us; the launch traced here: 239 us
  Pallas kernels  220 us (92%)
  local copies, waits for them, and re-layouts  10.5 us (4%)
  other arithmetic  7.57 us (3%)
    pallas_call x1, Pallas kernels, shards(): pl.pallas_call(functools.partial(layer_kernel, cfg, names), out_shape=[ja...  220 us
    convert_element_type x4, other arithmetic, shards(): wide = [wide[n].astype(F32) for n in range(4)]  7.57 us
    unnamed x18, local copies, waits for them, and re-layouts  6.37 us

profile of v4, /device:TPU:0, one launch (start us, length us, event | category | flops | bytes accessed | tf_op | source)
XLA Modules:
  0.0 238.7 jit_solution(2340806356403158834)
XLA Ops:
  0.7 220.0 %layer.1 = (bf16[512,768]{1,0:T(8,128)(2,1)}, bf16[512,768]{1,0:T(8,128)(2,1)}, f32[16,768]{1,0:T(8,128)}, f32[768,768]{1,0:T(8,128)}, f32[768,768]{1,0:T(8,128)...) custom-call(s32[1,512]{1,0:T(1,128)} %bitcast.22, ...), custom_call_target="tpu_custom_call" | custom-call | flops 32212254720 | bytes 33554432 | tf_op jit(solution)/shard_map/layer/pallas_call | solution.py:1103
  220.6 0.0 copy-start.4
  220.6 1.3 slice.18
  221.9 1.5 slice_reduce_fusion
  223.4 1.4 slice_bitcast_fusion
  224.8 2.8 %convert_element_type.12 = f32[768,768]{1,0:T(8,128)} convert(bf16[768,768]{1,0:T(8,128)(2,1)} %get-tuple-element.26) | non-fusion elementwise | flops 589824 | bytes 3538944 | tf_op jit(solution)/shard_map/convert_element_type | solution.py:1132
  227.6 0.0 copy-done.4
  227.6 0.0 copy-start.3
  227.6 1.6 convert_element_type.13
  229.2 0.1 copy-done.3
  229.3 0.0 copy-start.2
  229.3 1.6 convert_element_type.14
  230.9 0.1 copy-done.2
  231.0 0.0 copy-start.6
  231.0 0.0 copy-start.5
  231.0 1.6 convert_element_type.15
  232.6 0.0 copy-done.6
  232.6 0.0 copy-start.1
  232.6 0.9 copy.32
  233.4 0.0 copy-done.5
  233.4 0.9 copy.33
  234.3 0.5 copy-done.1
  234.8 0.0 copy-start
  234.8 1.4 copy.34
  236.2 1.1 copy-done
  237.3 1.4 copy.35
Async XLA Ops:
  220.6 7.0 %copy-start.4 = (bf16[768,768]{1,0:T(8,128)(2,1)S(1)}, bf16[768,768]{1,0:T(8,128)(2,1)}, u32[]{:S(2)}) copy-start(bf16[768,768]{1,0:T(8,128)(2,1)} %get-tuple-element.27) | copy-start | bytes 3538948
  227.6 1.7 copy-start.3
  229.3 1.7 copy-start.2
  231.0 1.6 copy-start.6
  231.0 2.5 %copy-start.5 = (bf16[512,768]{1,0:T(8,128)(2,1)S(1)}, bf16[512,768]{1,0:T(8,128)(2,1)}, u32[]{:S(2)}) copy-start(bf16[512,768]{1,0:T(8,128)(2,1)} %get-tuple-element.25) | copy-start | bytes 2359300
  232.6 2.2 copy-start.1
  234.8 2.5 %copy-start = (f32[768,768]{1,0:T(8,128)S(1)}, f32[768,768]{1,0:T(8,128)}, u32[]{:S(2)}) copy-start(f32[768,768]{1,0:T(8,128)} %get-tuple-element.31) | copy-start | bytes 7077892

commit v5 on v4

--- a/solution.py
+++ b/solution.py
@@ -21,11 +21,11 @@
     "start": ((3, 1),),
     0: ((0, 1),),
     1: ((1, 1),),
-    2: ((2, 1), (3, 2), (0, 2)),
-    "rows sent": ((1, 2), (2, 2), (3, 3), (0, 3)),
-    "rows done": ((1, 3), (2, 3), (3, 4), (0, 4)),
-    "late": ((1, 4), (2, 4), (3, 5), (0, 5)),
-    "last": ((1, 5), (2, 5)),
+    2: ((2, 1), (0, 2)),
+    "rows sent": ((1, 2), (2, 2), (0, 3), (3, 2), (1, 3), (0, 4), (2, 3), (3, 3)),
+    "rows done": ((1, 4), (2, 4), (3, 4)),
+    "late": ((0, 5), (1, 5)),
+    "last": ((2, 5), (3, 5)),
 }
 VMEM_BYTES = 255 << 18
 NT = (((1,), (1,)), ((), ()))
@@ -118,20 +118,42 @@
     pltpu.make_async_copy(dst, dst, recv_sem).wait()
 
 
-def exchange_start(me, src, dst, send_sem, recv_sem, size):
+def exp_peer(me, k, sign):
+    near = me.ne // 2
+    place = lax.rem(me.e, near)
+    base = lax.rem(me.e - place + near * lax.div(k, near), me.ne)
+    return base + lax.rem(place + near + sign * lax.rem(k, near), near)
+
+
+def turned(me, k):
+    return lax.rem(k + me.ne // 2, me.ne)
+
+
+def exchange_move(me, src, dst, send_sem, recv_sem, size, k):
+    there = exp_peer(me, k, 1)
+    return remote(
+        src.at[split_rows(there * size, size)],
+        dst.at[split_rows(me.e * size, size)],
+        send_sem.at[k],
+        recv_sem.at[k],
+        (me.b, there),
+    )
+
+
+def exchange_start(me, src, dst, send_sem, recv_sem, size, ahead=None):
+    own = split_rows(me.e * size, size)
+
     def one(k, _):
-        there = lax.rem(me.e + k, me.ne)
-        remote(
-            src.at[split_rows(there * size, size)],
-            dst.at[split_rows(me.e * size, size)],
-            send_sem.at[k],
-            recv_sem.at[k],
-            (me.b, there),
-        ).start()
-
-    own = split_rows(me.e * size, size)
+        if ahead:
+            k = turned(me, k)
+            ahead(k, split_rows(exp_peer(me, k, 1) * size, size))
+        exchange_move(me, src, dst, send_sem, recv_sem, size, k).start()
+
+    if ahead:
+        lax.fori_loop(0, me.ne // 2, one, None)
+        ahead(0, own)
     pltpu.make_async_copy(src.at[own], dst.at[own], recv_sem.at[0]).start()
-    lax.fori_loop(1, me.ne, one, None)
+    lax.fori_loop(me.ne // 2 + 1 if ahead else 1, me.ne, one, None)
 
 
 def exchange_wait(me, src, dst, send_sem, recv_sem, size):
@@ -139,22 +161,15 @@
     landed(dst.at[own], recv_sem.at[0])
 
     def one(k, _):
-        source = lax.rem(me.e + me.ne - k, me.ne)
-        landed(dst.at[split_rows(source * size, size)], recv_sem.at[k])
+        rows = split_rows(exp_peer(me, k, -1) * size, size)
+        landed(dst.at[rows], recv_sem.at[k])
 
     lax.fori_loop(1, me.ne, one, None)
 
 
 def exchange_sent(me, src, dst, send_sem, recv_sem, size):
     def one(k, _):
-        there = lax.rem(me.e + k, me.ne)
-        remote(
-            src.at[split_rows(there * size, size)],
-            dst.at[split_rows(me.e * size, size)],
-            send_sem.at[k],
-            recv_sem.at[k],
-            (me.b, there),
-        ).wait_send()
+        exchange_move(me, src, dst, send_sem, recv_sem, size, k).wait_send()
 
     lax.fori_loop(1, me.ne, one, None)
 
@@ -330,6 +345,71 @@
                 for lo in range(2):
                     self.out_first(step, lo).wait_send()
         self.out_second().wait_send()
+
+
+class PairSums:
+    def __init__(self, me, r):
+        self.me, self.r = me, r
+        self.hi, self.lo = lax.div(me.b, 2), lax.rem(me.b, 2)
+        self.count = me.nb // 2
+        self.size = me.ff // me.nb
+        self.partner = (2 * self.hi + 1 - self.lo, me.e)
+
+    def turn(self, step):
+        return lax.rem(self.hi + step, self.count)
+
+    def place(self, hi):
+        return split_rows(hi * self.size, self.size)
+
+    def owner(self, step):
+        return (2 * self.turn(step) + self.lo, self.me.e)
+
+    def in_move(self, step):
+        r, k = self.r, step - 1
+        src = r.win.at[:, self.place(self.turn(step))]
+        return remote(src, r.in_got.at[k], r.ins.at[k], r.inr.at[k], self.owner(step))
+
+    def out_move(self, step):
+        r, k = self.r, step - 1
+        src = r.wout.at[self.place(self.turn(step))]
+        return remote(src, r.out_got.at[k], r.outs.at[k], r.outr.at[k], self.owner(step))
+
+    def second_send(self):
+        for step in range(1, self.count):
+            self.out_move(step).start()
+
+    def total_in(self, into):
+        r = self.r
+        for step in range(1, self.count):
+            landed(r.in_got.at[step - 1], r.inr.at[step - 1])
+
+        def in_rows(n, _):
+            rows = split_rows(n * ROWS, ROWS)
+            total = r.win[rows, self.place(self.hi)].astype(F32)
+            for step in range(1, self.count):
+                total += r.in_got[step - 1, rows, :].astype(F32)
+            into[rows, 0 : self.size] = total
+
+        lax.fori_loop(0, self.me.width // ROWS, in_rows, None)
+
+    def total_out(self, into):
+        r = self.r
+        for step in range(1, self.count):
+            landed(r.out_got.at[step - 1], r.outr.at[step - 1])
+
+        def out_rows(n, _):
+            rows = split_rows(n * ROWS, ROWS)
+            total = r.wout[split_rows(self.hi * self.size + n * ROWS, ROWS), :].astype(F32)
+            for step in range(1, self.count):
+                total += r.out_got[step - 1, rows, :].astype(F32)
+            into[rows, :] = total
+
+        lax.fori_loop(0, self.size // ROWS, out_rows, None)
+
+    def sent(self):
+        for step in range(1, self.count):
+            self.in_move(step).wait_send()
+            self.out_move(step).wait_send()
 
 
 class SharedSum:
@@ -513,14 +593,17 @@
     slots = me.experts * me.cap
     roomy = slots * me.width <= 1 << 19
     model_tile = me.width if roomy else FF_COLS
-    r.ysend, r.yback = r.g, r.du
+    early_g = r.g.at[0] if me.paired else r.g
+    r.ysend, r.yback = early_g, r.dh2 if me.paired else r.du
     r.swap, r.da_in = r.took.at[pl.ds(0, me.rows)], r.back.at[pl.ds(0, me.rows)]
-    r.xin, r.o_send, r.lse_cols, r.dh_send = r.mail, r.g, r.dk_sum, r.disp
+    r.xin, r.o_send, r.lse_cols, r.dh_send = r.mail, early_g, r.dk_sum, r.disp
     gain1, bias1, gain2, bias2 = (
         v[...].reshape(1, me.width) for v in (r.gain1, r.bias1, r.gain2, r.bias2)
     )
     loads = {}
-    for name in ("x", "og", "wo", "win", "wout"):
+    sums = PairSums(me, r) if me.paired else ExpertSums(me, r)
+    whole = ("x", "og", "wo") if me.paired else ("x", "og", "wo", "win", "wout")
+    for name in whole:
         loads[name] = pltpu.make_async_copy(
             getattr(r, name + "_hbm"), getattr(r, name), r.lsem.at[len(loads)]
         )
@@ -530,6 +613,15 @@
             loads["w", p, j] = pltpu.make_async_copy(
                 src, r.w.at[p, :, pl.ds(j * PAIR, PAIR)], r.lsem.at[len(loads)]
             )
+    for h in range(sums.count) if me.paired else ():
+        part = pl.ds(pl.multiple_of((2 * h + sums.lo) * sums.size, 128), sums.size)
+        place = pl.ds(h * sums.size, sums.size)
+        loads["win", h] = pltpu.make_async_copy(
+            r.win_hbm.at[:, part], r.win.at[:, place], r.lsem.at[len(loads)]
+        )
+        loads["wout", h] = pltpu.make_async_copy(
+            r.wout_hbm.at[part], r.wout.at[place], r.lsem.at[len(loads)]
+        )
     for load in loads.values():
         load.start()
     me.greet()
@@ -590,6 +682,18 @@
             r.osr.at[2 * lax.rem(me.b, me.seqs) + me.c],
             (j, home),
         )
+
+    def dh_slot(k):
+        return split_rows(exp_peer(me, jnp.int32(k), -1) * me.cap, me.cap)
+
+    def dh_move(k):
+        rows = dh_slot(k)
+        return remote(r.dh.at[rows], r.dh2.at[rows], r.d2s.at[k], r.d2r.at[k], sums.partner)
+
+    def dh_arrived(k):
+        landed(r.dh.at[dh_slot(k)], r.dr.at[k])
+        if me.paired:
+            dh_move(k).start()
 
     for i in range(blocks):
         for j in range(i * spans, (i + 1) * spans):
@@ -635,6 +739,11 @@
             push(me, *o_move(j))
         if i == 0:
             count_sum.middle()
+        for k in range(me.ne):
+            if (i == blocks - 1) if not me.paired else (max(0, k + 1 - me.ne // 2) == i):
+                dh_arrived(k)
+    for k in range(me.ne // 2 + blocks - 1, me.ne) if me.paired else ():
+        dh_arrived(k)
     r.lse[...] = jnp.transpose(r.lse_cols[...])[0:8, :]
     for j in range(me.nb):
         forward_move(j).wait_send()
@@ -643,7 +752,6 @@
         push_done(me, *move)
     for name in ("x", "wo"):
         loads[name].wait()
-    exchange_wait(me, r.dh_send, r.dh, r.ds, r.dr, me.cap)
     exchange_sent(me, r.dh_send, r.dh, r.ds, r.dr, me.cap)
 
     expert_lane = iota((ROWS, me.experts), 1)
@@ -673,20 +781,29 @@
     takes = slots_by_token(me, slot)
     r.disp[...] = dot(takes, r.mail[...]).astype(BF16)
     exchange_start(me, r.disp, r.took, r.ns, r.nr, me.cap)
-    loads["win"].wait()
-    loads["wout"].wait()
-    exchange_wait(me, r.disp, r.took, r.ns, r.nr, me.cap)
-    exchange_sent(me, r.disp, r.took, r.ns, r.nr, me.cap)
+    for key, load in loads.items():
+        if key in ("win", "wout") or key[0] in ("win", "wout"):
+            load.wait()
+
+    def took_move(k, rows):
+        return remote(r.took.at[rows], r.took2.at[rows], r.t2s.at[k], r.t2r.at[k], sums.partner)
+
+    if not me.paired:
+        exchange_wait(me, r.disp, r.took, r.ns, r.nr, me.cap)
+        exchange_sent(me, r.disp, r.took, r.ns, r.nr, me.cap)
 
     lanes = iota((slots, me.experts), 1)
-    logits = jnp.sum(
-        jnp.where(lanes == me.e, dot(r.took[...], r.router[...], NT), 0.0), axis=1, keepdims=True
-    )
-    value = jax.nn.sigmoid(logits)
-    r.disp[...] = (value * r.dh[...].astype(F32)).astype(BF16)
-    r.yf[0:slots, :] = jnp.zeros((slots, me.width), F32)
-    r.made[...] = jnp.zeros_like(r.made)
-    sums = ExpertSums(me, r)
+
+    def gate_of(rows, lanes):
+        logits = dot(rows, r.router[...], NT)
+        picked = jnp.sum(jnp.where(lanes == me.e, logits, 0.0), axis=1, keepdims=True)
+        return jax.nn.sigmoid(picked)
+
+    if not me.paired:
+        value = gate_of(r.took[...], lanes)
+        r.disp[...] = (value * r.dh[...].astype(F32)).astype(BF16)
+        r.yf[0:slots, :] = jnp.zeros((slots, me.width), F32)
+        r.made[...] = jnp.zeros_like(r.made)
     slot_rows = slots if roomy else slots // 4
 
     def expert_part(n, _):
@@ -725,23 +842,130 @@
         lax.fori_loop(0, sums.size // sums.tile, weight_columns, None)
         sums.after_part(n)
 
-    sums.tile = sums.size
-    lax.fori_loop(0, me.nb, expert_part, None)
+    near = me.ne // 2
+    half_slots = near * me.cap
+    half_lanes = iota((half_slots, me.experts), 1)
+
+    def products(took, dh, dy, act, back, rows):
+        gates = gate_of(took[rows, :], half_lanes)
+        dy[rows, :] = (gates * dh[rows, :].astype(F32)).astype(BF16)
+        for h in range(sums.count):
+            place = pl.ds(h * sums.size, sums.size)
+            value, slope = gelu_parts(dot(took[rows, :], r.win[:, place]))
+            act.at[h][rows, :] = value.astype(BF16)
+            back.at[h][rows, :] = (dot(dy[rows, :], r.wout[place, :], NT) * slope).astype(BF16)
+        places = [pl.ds(h * sums.size, sums.size) for h in range(sums.count)]
+        made_y = sum(dot(act.at[h][rows, :], r.wout[place, :]) for h, place in enumerate(places))
+        made_dn = sum(
+            dot(back.at[h][rows, :], r.win[:, place], NT) for h, place in enumerate(places)
+        )
+        return gates, made_y, made_dn
+
+    def dgate_rows(dh, y):
+        return jnp.sum(dh.astype(F32) * y, axis=1, keepdims=True)
+
+    def dn_move(k, rows):
+        return remote(r.dn2.at[rows], r.dn_got.at[rows], r.g2s.at[k], r.g2r.at[k], sums.partner)
+
+    def slot_rows_of(k):
+        return split_rows(exp_peer(me, k, 1) * me.cap, me.cap)
+
+    if me.paired:
+        act2 = r.shared.at[pl.ds(0, sums.count), pl.ds(0, slots)]
+        back2 = r.shared.at[pl.ds(sums.count, sums.count), pl.ds(0, slots)]
+
+        def half_rows(n, _):
+            def pass_on(k, _):
+                rows = split_rows(exp_peer(me, k, -1) * me.cap, me.cap)
+                landed(r.took.at[rows], r.nr.at[k])
+                took_move(k, rows).start()
+
+            def arrived(k, _):
+                rows = split_rows(exp_peer(me, k, -1) * me.cap, me.cap)
+                landed(r.dh2.at[rows], r.d2r.at[k])
+                landed(r.took2.at[rows], r.t2r.at[k])
+
+            lax.fori_loop(n * near, (n + 1) * near, pass_on, None)
+            base = lax.rem(me.e - lax.rem(me.e, near) + n * near, me.ne)
+            rows = pl.ds(pl.multiple_of(base * me.cap, half_slots), half_slots)
+            gates, made_y, made_dn = products(r.took, r.dh, r.dy, r.g, r.du, rows)
+            r.value[rows, :] = gates
+            r.dgate[rows, :] = dgate_rows(r.dh[rows, :], made_y)
+            r.yf[rows, :] = made_y
+            r.made[rows, :] = made_dn
+            lax.fori_loop(n * near, (n + 1) * near, arrived, None)
+            _, made_y, made_dn = products(r.took2, r.dh2, r.dy2, act2, back2, rows)
+            r.dgate2[rows, :] = dgate_rows(r.dh2[rows, :], made_y)
+            r.y2[rows, :] = made_y.astype(BF16)
+            r.dn2[rows, :] = made_dn.astype(BF16)
+
+        lax.fori_loop(0, 2, half_rows, None)
+        exchange_sent(me, r.disp, r.took, r.ns, r.nr, me.cap)
+        r.dg_send[...] = jnp.transpose(jnp.broadcast_to(r.dgate2[...], (slots, 128)))[0:8, :]
+        dg_move = remote(r.dg_send, r.dg_got, r.dgs, r.dgr, sums.partner)
+        dg_move.start()
+
+        def dn_start(n, _):
+            k = turned(me, n)
+            dn_move(k, slot_rows_of(k)).start()
+
+        lax.fori_loop(0, me.ne, dn_start, None)
+
+        def y_move(part):
+            rows = pl.ds(part * half_slots, half_slots)
+            return remote(
+                r.y2.at[rows], r.y_got.at[rows], r.y2s.at[part], r.y2r.at[part], sums.partner
+            )
+
+        y_move(0).start()
+
+        def weight_part(hi):
+            place = sums.place(hi)
+            r.win[:, place] = (
+                dot(r.took[...], r.du[hi], TN) + dot(r.took2[...], back2[hi], TN)
+            ).astype(BF16)
+            r.wout[place, :] = (
+                dot(r.g[hi], r.dy[...], TN) + dot(act2[hi], r.dy2[...], TN)
+            ).astype(BF16)
+
+        for step in range(1, sums.count):
+            weight_part(sums.turn(step))
+            sums.in_move(step).start()
+    else:
+        sums.tile = sums.size
+        lax.fori_loop(0, me.nb, expert_part, None)
 
     weights = (count_sum.total() - me.mean_load) / me.mean_load
     weight = jnp.sum(jnp.where(iota(weights.shape, 0) == me.e, weights, 0.0), axis=0, keepdims=True)
     weight = weight[:, 0:1]
-    r.ysend[...] = r.yf[0:slots, :].astype(BF16)
-    dgate = (
-        jnp.sum(r.dh[...].astype(F32) * r.ysend[...].astype(F32), axis=1, keepdims=True)
-        + weight / me.tokens
-    )
+    if me.paired:
+        landed(r.dg_got, r.dgr)
+        theirs = jnp.transpose(jnp.broadcast_to(r.dg_got[0:1, :], (128, slots)))[:, 0:1]
+        dgate = r.dgate[...] + theirs + weight / me.tokens
+        value = r.value[...]
+    else:
+        r.ysend[...] = r.yf[0:slots, :].astype(BF16)
+        dgate = (
+            jnp.sum(r.dh[...].astype(F32) * r.ysend[...].astype(F32), axis=1, keepdims=True)
+            + weight / me.tokens
+        )
     dlogits = jnp.where(lanes == me.e, dgate * value * (1.0 - value), 0.0).astype(BF16)
-    r.disp[...] = (r.made[0:slots, :] + dot(dlogits, r.router[...])).astype(BF16)
-    exchange_start(me, r.disp, r.back, r.rs, r.rr, me.cap)
+    if me.paired:
+        r.made[0:slots, :] += dot(dlogits, r.router[...])
+
+        def add_theirs(k, rows):
+            landed(r.dn_got.at[rows], r.g2r.at[k])
+            r.disp[rows, :] = (r.made[rows, :] + r.dn_got[rows, :].astype(F32)).astype(BF16)
+
+        exchange_start(me, r.disp, r.back, r.rs, r.rr, me.cap, ahead=add_theirs)
+        weight_part(sums.hi)
+    else:
+        r.disp[...] = (r.made[0:slots, :] + dot(dlogits, r.router[...])).astype(BF16)
+        exchange_start(me, r.disp, r.back, r.rs, r.rr, me.cap)
     r.sums[2 : 2 + me.experts, :] = dot(dlogits, r.took[...], TN)
     r.sums[2 + me.experts : 3 + me.experts, 0 : me.experts] = r.mass[...]
-    sums.second_add()
+    if not me.paired:
+        sums.second_add()
     exchange_wait(me, r.disp, r.back, r.rs, r.rr, me.cap)
 
     r.made[0 : me.rows, :] = dot(takes, r.back[...], TN)
@@ -774,7 +998,14 @@
     sums.second_send()
     early = AllSum(me, r.sums, r.sum_exp, r.sum_blk, (r.es, r.er, r.bs, r.br))
     early.start()
-    exchange_start(me, r.ysend, r.yback, r.ys, r.yr, me.cap)
+    if me.paired:
+        y_move(1).start()
+        lax.fori_loop(
+            0,
+            me.ne,
+            lambda k, _: took_move(k, split_rows(exp_peer(me, k, -1) * me.cap, me.cap)).wait_send(),
+            None,
+        )
 
     def output_columns(core):
         cols = pl.ds(pl.multiple_of(core * me.half_width, PAIR), me.half_width)
@@ -793,6 +1024,11 @@
             getattr(pieces[p], f"stage{stage}")()
 
     advance("start")
+    if me.paired:
+        for part in range(2):
+            landed(r.y_got.at[pl.ds(part * half_slots, half_slots)], r.y2r.at[part])
+        r.ysend[...] = (r.yf[0:slots, :] + r.y_got[...].astype(F32)).astype(BF16)
+    exchange_start(me, r.ysend, r.yback, r.ys, r.yr, me.cap)
 
     r.made[...] = jnp.zeros_like(r.made)
     for j in range(me.nb):
@@ -931,6 +1167,13 @@
     for j in range(me.nb):
         push_done(me, *da_move(j))
     sums.sent()
+    if me.paired:
+        for k in range(me.ne):
+            dh_move(k).wait_send()
+        dg_move.wait_send()
+        for part in range(2):
+            y_move(part).wait_send()
+        lax.fori_loop(0, me.ne, lambda k, _: dn_move(k, slot_rows_of(k)).wait_send(), None)
     stores = [store_in, store_out]
     for piece in pieces:
         piece.end()
@@ -952,6 +1195,45 @@
 
 def anywhere(count):
     return [pl.BlockSpec(memory_space=pl.ANY)] * count
+
+
+def finish_kernel(experts, *refs):
+    small, *narrow = refs[: len(refs) // 2 - 2]
+    balance, router, *rest = refs[len(refs) // 2 - 2 :]
+    norms, wide = rest[:4], rest[4:]
+    for src, dst in zip(narrow, wide, strict=True):
+        dst[...] = src[...].astype(dst.dtype)
+
+    @pl.when(pl.program_id(0) == 0)
+    def _():
+        balance[...] = small[experts + 3 : experts + 4, 0:128]
+        router[...] = small[2 : 2 + experts, :]
+        for dst, row in zip(norms, (experts + 4, experts + 5, 0, 1), strict=True):
+            dst[...] = small[row, :]
+
+
+def finish(experts, small, narrow, kinds):
+    steps = 4
+    width = small.shape[1]
+
+    def rows(array):
+        return pl.BlockSpec((array.shape[0] // steps, array.shape[1]), lambda n: (n, 0))
+
+    def whole(*shape):
+        return pl.BlockSpec(shape, lambda n: (0,) * len(shape))
+
+    small_shapes = [(1, 128), (experts, width)] + 4 * [(width,)]
+    return pl.pallas_call(
+        functools.partial(finish_kernel, experts),
+        grid=(steps,),
+        out_shape=[jax.ShapeDtypeStruct(shape, F32) for shape in small_shapes]
+        + [jax.ShapeDtypeStruct(a.shape, kind) for a, kind in zip(narrow, kinds)],
+        in_specs=[whole(*small.shape)] + [rows(a) for a in narrow],
+        out_specs=[whole(*shape) for shape in small_shapes] + [rows(a) for a in narrow],
+        compiler_params=pltpu.CompilerParams(vmem_limit_bytes=VMEM_BYTES),
+        cost_estimate=pl.CostEstimate(flops=0, bytes_accessed=24 << 20, transcendentals=0),
+        name="finish",
+    )(small, *narrow)
 
 
 def shards(
@@ -991,6 +1273,7 @@
     size = ff // nb
     sum_rows = -(-(3 + experts) // 8) * 8
     cfg["sum_here"] = width % (8 * nb * ne) == 0
+    paired = cfg["paired"] = cfg["sum_here"] and size == width and hi == 2 and slots <= width
     outer = width // min(nb, ne // 2)
     inner = width // (nb * ne // 2)
     inputs = (
@@ -1022,8 +1305,8 @@
     else:
         outputs.append(("own_part", (4, width, half_width), BF16, False))
     scratch = dict(
-        win=vmem((width, ff), BF16),
-        wout=vmem((ff, width), BF16),
+        win=vmem((width, ff // 2 if paired else ff), BF16),
+        wout=vmem((ff // 2 if paired else ff, width), BF16),
         x=vmem((rows, width), BF16),
         og=vmem((rows, width), BF16),
         o=vmem((rows, width), BF16),
@@ -1045,8 +1328,8 @@
         mail=vmem((rows, width), BF16),
         disp=vmem((slots, width), BF16),
         took=vmem((slots, width), BF16),
-        g=vmem((slots, width), BF16),
-        du=vmem((slots, width), BF16),
+        g=vmem((hi, slots, width) if paired else (slots, width), BF16),
+        du=vmem((hi, slots, width) if paired else (slots, width), BF16),
         yf=vmem((max(slots, size), width), F32),
         made=vmem((length, width), F32),
         back=vmem((slots, width), BF16),
@@ -1063,15 +1346,7 @@
         late_exp=vmem((ne, 8, FF_COLS), F32),
         late_blk=vmem((nb, 8, FF_COLS), F32),
         part=vmem((4, width, half_width), BF16),
-        in1=vmem((hi, width, size), BF16),
-        in2=vmem((hi - 1, width, size), BF16),
-        out1=vmem((hi - 1, 2, size, width), BF16),
-        out2=vmem((size, width), BF16),
-        in1s=dma((hi,)), in1r=dma((hi,)),
-        in2s=dma((hi - 1,)), in2r=dma((hi - 1,)),
-        out1s=dma((hi - 1, 2)), out1r=dma((hi - 1, 2)),
-        out2s=dma, out2r=dma,
-        lsem=dma((5 + 3 * (half_width // PAIR),)),
+        lsem=dma((5 + 2 * hi + 3 * (half_width // PAIR),)),
         fsem=dma((6,)),
         xs=dma((2 * seqs,)), xr=dma((nb,)),
         fws=dma((nb,)), fwr=dma((nb,)),
@@ -1099,6 +1374,33 @@
         for n in range(1, 5):
             scratch[f"s{n}"] = dma((4, max(nb, ne // 2)))
             scratch[f"r{n}"] = dma((4, max(nb, ne // 2)))
+    if paired:
+        scratch.update(
+            {n: vmem((slots, width), BF16) for n in ("took2", "dh2", "dy", "dy2", "dn2", "dn_got", "y2", "y_got")},
+            **{n: vmem((slots, 1), F32) for n in ("value", "dgate", "dgate2")},
+            dg_send=vmem((8, slots), F32),
+            dg_got=vmem((8, slots), F32),
+            in_got=vmem((hi - 1, width, size), BF16),
+            out_got=vmem((hi - 1, size, width), BF16),
+            ins=dma((hi - 1,)), inr=dma((hi - 1,)),
+            outs=dma((hi - 1,)), outr=dma((hi - 1,)),
+            t2s=dma((ne,)), t2r=dma((ne,)),
+            g2s=dma((ne,)), g2r=dma((ne,)),
+            d2s=dma((ne,)), d2r=dma((ne,)),
+            **{n: dma for n in ("dgs", "dgr")},
+            y2s=dma((2,)), y2r=dma((2,)),
+        )
+    else:
+        scratch.update(
+            in1=vmem((hi, width, size), BF16),
+            in2=vmem((hi - 1, width, size), BF16),
+            out1=vmem((hi - 1, 2, size, width), BF16),
+            out2=vmem((size, width), BF16),
+            in1s=dma((hi,)), in1r=dma((hi,)),
+            in2s=dma((hi - 1,)), in2r=dma((hi - 1,)),
+            out1s=dma((hi - 1, 2)), out1r=dma((hi - 1, 2)),
+            out2s=dma, out2r=dma,
+        )
     names = [n for n, _, _ in inputs] + [n for n, _, _, _ in outputs] + list(scratch)
     out, dx, small, dwin, dwout, *wide = pl.pallas_call(
         functools.partial(layer_kernel, cfg, names),
@@ -1129,19 +1431,22 @@
             ),
             ("blk", "exp"),
         )
-    wide = [wide[n].astype(F32) for n in range(4)]
+    arrays = [out, dx, dwin, dwout, *[wide[n] for n in range(4)]]
+    balance, router, gain1, bias1, gain2, bias2, out, dx, dwin, dwout, *wide = finish(
+        experts, small, arrays, [BF16, BF16] + [F32] * 6
+    )
     return (
         out.reshape(seqs, span, width),
-        small[experts + 3, 0],
+        balance[0, 0],
         dx.reshape(seqs, span, width),
         *wide,
-        small[2 : 2 + experts].T,
+        router.T,
         dwin[None],
         dwout[None],
-        small[experts + 4],
-        small[experts + 5],
-        small[0],
-        small[1],
+        gain1,
+        bias1,
+        gain2,
+        bias2,
     )
 
 

time: 240 us -> 226 us (0.942)
  local copies, waits for them, and re-layouts: 10.5 us -> 0 us
  other arithmetic: 7.57 us -> 0 us
  Pallas kernels: 220 us -> 225 us
    pallas_call x0 -> x1, Pallas kernels: none -> 10.6 us  [finish(): pl.pallas_call(functools.partial(finish_kernel, experts), grid=(steps,),...]
    convert_element_type x4 -> x0, other arithmetic: 7.57 us -> none  [shards(): wide = [wide[n].astype(F32) for n in range(4)]]
    unnamed x18 -> x0, local copies, waits for them, and re-layouts: 6.37 us -> none
    pallas_call x1, Pallas kernels: 220 us -> 215 us  [shards(): pl.pallas_call(functools.partial(layer_kernel, cfg, names), out_shape=[ja...]
    slice x2 -> x0, local copies, waits for them, and re-layouts: 2.74 us -> none  [the longest x1 1.45 us: shards(): small[1]]
where the time goes in v5:
time: 226 us
  Pallas kernels  225 us (100%)
    pallas_call x1, Pallas kernels, shards(): pl.pallas_call(functools.partial(layer_kernel, cfg, names), out_shape=[ja...  215 us
    pallas_call x1, Pallas kernels, finish(): pl.pallas_call(functools.partial(finish_kernel, experts), grid=(steps,),...  10.6 us

profile of v5, /device:TPU:0, one launch (start us, length us, event | category | flops | bytes accessed | tf_op | source)
XLA Modules:
  0.0 226.1 jit_solution(14746862766424002836)
XLA Ops:
  0.7 214.6 %layer.1 = (bf16[512,768]{1,0:T(8,128)(2,1)}, bf16[512,768]{1,0:T(8,128)(2,1)}, f32[16,768]{1,0:T(8,128)}, f32[768,768]{1,0:T(8,128)}, f32[768,768]{1,0:T(8,128)...) custom-call(s32[1,512]{1,0:T(1,128)} %bitcast.23, ...), custom_call_target="tpu_custom_call" | custom-call | flops 32212254720 | bytes 33554432 | tf_op jit(solution)/shard_map/layer/pallas_call | solution.py:1405
  215.3 10.6 %finish.1 = (f32[1,128]{1,0:T(1,128)}, f32[8,768]{1,0:T(8,128)}, f32[768]{0:T(1024)}, f32[768]{0:T(1024)}, f32[768]{0:T(1024)}, /*index=5*/f32[768]{0:T(1024)}, ...) custom-call(f32[16,768]{1,0:T(8,128)} %get-tuple-element.37.refs_0_,, ...), custom_call_target="tpu_custom_call" | custom-call | bytes 25165824 | tf_op jit(solution)/shard_map/finish/pallas_call | solution.py:1226

commit v6 on v5

--- a/solution.py
+++ b/solution.py
@@ -305,7 +305,7 @@
             self.in_second(step).start()
         self.out_second().start()
 
-    def total_in(self, into):
+    def total_in(self):
         r = self.r
         landed(r.in1.at[self.hi], r.in1r.at[self.hi])
         for step in range(1, self.count):
@@ -317,11 +317,12 @@
             total += r.in1[self.hi, rows, :].astype(F32)
             for step in range(1, self.count):
                 total += r.in2[step - 1, rows, :].astype(F32)
-            into[rows, 0 : self.size] = total
+            r.win[rows, self.span(self.hi, self.lo)] = total.astype(BF16)
 
         lax.fori_loop(0, self.me.width // ROWS, in_rows, None)
-
-    def total_out(self, into):
+        return r.win.at[:, self.span(self.hi, self.lo)]
+
+    def total_out(self):
         r = self.r
         for step in range(1, self.count):
             landed(r.out1.at[step - 1, self.lo], r.out1r.at[step - 1, self.lo])
@@ -330,12 +331,14 @@
 
         def out_rows(n, _):
             rows = split_rows(n * ROWS, ROWS)
-            total = r.wout[split_rows(base + n * ROWS, ROWS), :].astype(F32)
+            own = split_rows(base + n * ROWS, ROWS)
+            total = r.wout[own, :].astype(F32)
             for step in range(1, self.count):
                 total += r.out1[step - 1, self.lo, rows, :].astype(F32)
-            into[rows, :] = total + r.out2[rows, :].astype(F32)
+            r.wout[own, :] = (total + r.out2[rows, :].astype(F32)).astype(BF16)
 
         lax.fori_loop(0, self.size // ROWS, out_rows, None)
+        return r.wout.at[self.span(self.hi, self.lo)]
 
     def sent(self):
         for step in range(1, self.count + 1):
@@ -378,7 +381,7 @@
         for step in range(1, self.count):
             self.out_move(step).start()
 
-    def total_in(self, into):
+    def total_in(self):
         r = self.r
         for step in range(1, self.count):
             landed(r.in_got.at[step - 1], r.inr.at[step - 1])
@@ -388,23 +391,26 @@
             total = r.win[rows, self.place(self.hi)].astype(F32)
             for step in range(1, self.count):
                 total += r.in_got[step - 1, rows, :].astype(F32)
-            into[rows, 0 : self.size] = total
+            r.win[rows, self.place(self.hi)] = total.astype(BF16)
 
         lax.fori_loop(0, self.me.width // ROWS, in_rows, None)
-
-    def total_out(self, into):
+        return r.win.at[:, self.place(self.hi)]
+
+    def total_out(self):
         r = self.r
         for step in range(1, self.count):
             landed(r.out_got.at[step - 1], r.outr.at[step - 1])
 
         def out_rows(n, _):
             rows = split_rows(n * ROWS, ROWS)
-            total = r.wout[split_rows(self.hi * self.size + n * ROWS, ROWS), :].astype(F32)
+            own = split_rows(self.hi * self.size + n * ROWS, ROWS)
+            total = r.wout[own, :].astype(F32)
             for step in range(1, self.count):
                 total += r.out_got[step - 1, rows, :].astype(F32)
-            into[rows, :] = total
+            r.wout[own, :] = total.astype(BF16)
 
         lax.fori_loop(0, self.size // ROWS, out_rows, None)
+        return r.wout.at[self.place(self.hi)]
 
     def sent(self):
         for step in range(1, self.count):
@@ -911,8 +917,12 @@
 
         lax.fori_loop(0, me.ne, dn_start, None)
 
+        def half_of(part):
+            base = me.e - lax.rem(me.e, near) + (1 - part) * near
+            return pl.ds(pl.multiple_of(lax.rem(base, me.ne) * me.cap, half_slots), half_slots)
+
         def y_move(part):
-            rows = pl.ds(part * half_slots, half_slots)
+            rows = half_of(part)
             return remote(
                 r.y2.at[rows], r.y_got.at[rows], r.y2s.at[part], r.y2r.at[part], sums.partner
             )
@@ -997,9 +1007,24 @@
             push(me, *move)
     sums.second_send()
     early = AllSum(me, r.sums, r.sum_exp, r.sum_blk, (r.es, r.er, r.bs, r.br))
-    early.start()
+    def y_home(part):
+        rows = half_of(part)
+        landed(r.y_got.at[rows], r.y2r.at[part])
+        r.ysend[rows, :] = (r.yf[rows, :] + r.y_got[rows, :].astype(F32)).astype(BF16)
+
+        def one(k, _):
+            exchange_move(me, r.ysend, r.yback, r.ys, r.yr, me.cap, k).start()
+
+        if part:
+            own = split_rows(me.e * me.cap, me.cap)
+            pltpu.make_async_copy(r.ysend.at[own], r.yback.at[own], r.yr.at[0]).start()
+            lax.fori_loop(1, near, one, None)
+        else:
+            lax.fori_loop(near, me.ne, one, None)
+
     if me.paired:
         y_move(1).start()
+        y_home(0)
         lax.fori_loop(
             0,
             me.ne,
@@ -1024,13 +1049,14 @@
             getattr(pieces[p], f"stage{stage}")()
 
     advance("start")
+    early.start()
+    if not me.paired:
+        exchange_start(me, r.ysend, r.yback, r.ys, r.yr, me.cap)
+
+    r.made[...] = jnp.zeros_like(r.made)
     if me.paired:
-        for part in range(2):
-            landed(r.y_got.at[pl.ds(part * half_slots, half_slots)], r.y2r.at[part])
-        r.ysend[...] = (r.yf[0:slots, :] + r.y_got[...].astype(F32)).astype(BF16)
-    exchange_start(me, r.ysend, r.yback, r.ys, r.yr, me.cap)
-
-    r.made[...] = jnp.zeros_like(r.made)
+        store_in = pltpu.make_async_copy(sums.total_in(), r.dwin, r.fsem.at[0])
+        store_in.start()
     for j in range(me.nb):
         landed(r.do.at[pl.ds(j * me.span, me.span)], r.dor.at[j])
     visible = iota((QUERY_ROWS, QUERY_ROWS), 0) <= iota((QUERY_ROWS, QUERY_ROWS), 1)
@@ -1075,6 +1101,8 @@
 
             @pl.when(n == done)
             def _(done=done):
+                if me.paired and done == 1:
+                    y_home(1)
                 advance(done)
 
     lax.fori_loop(0, pairs, pair_back, None)
@@ -1138,14 +1166,10 @@
     late.middle()
     advance("late")
 
-    size = sums.size
-    sums.total_in(r.made)
-    store_in = pltpu.make_async_copy(
-        r.made.at[pl.ds(0, me.width), pl.ds(0, size)], r.dwin, r.fsem.at[0]
-    )
-    store_in.start()
-    sums.total_out(r.yf)
-    store_out = pltpu.make_async_copy(r.yf.at[pl.ds(0, size)], r.dwout, r.fsem.at[1])
+    if not me.paired:
+        store_in = pltpu.make_async_copy(sums.total_in(), r.dwin, r.fsem.at[0])
+        store_in.start()
+    store_out = pltpu.make_async_copy(sums.total_out(), r.dwout, r.fsem.at[1])
     store_out.start()
     advance("last")
     early_total = early.total()
@@ -1297,8 +1321,8 @@
         ("out", (rows, width), BF16, True),
         ("dx", (rows, width), BF16, True),
         ("small", (small_rows, width), F32, True),
-        ("dwin", (width, size), F32, False),
-        ("dwout", (size, width), F32, False),
+        ("dwin", (width, size), BF16, False),
+        ("dwout", (size, width), BF16, False),
     ]
     if cfg["sum_here"]:
         outputs += [(n, (width, width), BF16, False) for n in ("gq", "gk", "gv", "go")]

time: 226 us -> 226 us (level)
  no operation moved by 1% of the time
where the time goes in v6:
time: 226 us
  Pallas kernels  225 us (100%)
    pallas_call x1, Pallas kernels, shards(): pl.pallas_call(functools.partial(layer_kernel, cfg, names), out_shape=[ja...  215 us
    pallas_call x1, Pallas kernels, finish(): pl.pallas_call(functools.partial(finish_kernel, experts), grid=(steps,),...  9.72 us

profile of v6, /device:TPU:0, one launch (start us, length us, event | category | flops | bytes accessed | tf_op | source)
XLA Modules:
  0.0 225.7 jit_solution(12807951550239387037)
XLA Ops:
  0.7 215.2 %layer.1 = (bf16[512,768]{1,0:T(8,128)(2,1)}, bf16[512,768]{1,0:T(8,128)(2,1)}, f32[16,768]{1,0:T(8,128)}, bf16[768,768]{1,0:T(8,128)(2,1)}, bf16[768,768]{1,0:T...) custom-call(s32[1,512]{1,0:T(1,128)} %bitcast.23, ...), custom_call_target="tpu_custom_call" | custom-call | flops 32212254720 | bytes 33554432 | tf_op jit(solution)/shard_map/layer/pallas_call | solution.py:1429
  215.8 9.7 %finish.1 = (f32[1,128]{1,0:T(1,128)}, f32[8,768]{1,0:T(8,128)}, f32[768]{0:T(1024)}, f32[768]{0:T(1024)}, f32[768]{0:T(1024)}, /*index=5*/f32[768]{0:T(1024)}, ...) custom-call(f32[16,768]{1,0:T(8,128)} %get-tuple-element.37.refs_0_,, ...), custom_call_target="tpu_custom_call" | custom-call | bytes 25165824 | tf_op jit(solution)/shard_map/finish/pallas_call | solution.py:1250
